TPU v7x, 128 devices: a whole 4x4x4 slice. The times are simulated.
128 devices in a mesh: dp: 16 (over x, y), rel: 8 (over z, core).
Axes of the slice: x: 4, y: 4, z: 4, core: 2. Of those that a mesh axis runs over, the one named last changes fastest.
Arguments:
- grad_out: bfloat16 [16384, 512], P('dp', 'rel'), may hold values from -6 to 6
- src_feat: bfloat16 [32768, 768], P(('dp', 'rel')), may hold values from -6 to 6
- weight: bfloat16 [768, 2560], replicated, may hold values from -0.21875 to 0.21875
- nbr_slot: int32 [16384, 64, 16], P('dp', 'rel'), may hold values from 0 to 511
- src_ids: int32 [16, 64, 512], P('dp', 'rel'), may hold values from 0 to 2047
- valid_rows: int32 [16, 64], P('dp', 'rel'), may hold values from 1 to 1024, 32768 in all within a row
- block_rel: int32 [64], P('rel'), may hold values from 0 to 4, as said below
Outputs:
- source_grad: bfloat16 [32768, 768], P(('dp', 'rel'))
- weight_grad: float32 [768, 2560], P(('dp', 'rel'))
Inputs may be any that keep to these rules, and one draw needn't show every extreme that they name: `block_rel`: every one of the 5 relations owns one block or more. `valid_rows`: in each group the counts sum to 32768.
All inputs are finite; a program needn't handle non-finite values.
Results may differ from a plain program's by a relative error of at most 0.02.
Values may be sent and summed in bfloat16 or wider, within the bound.
No kernel may reach another device: no remote copies, remote signals or barrier semaphores. Data moves between devices by JAX's collectives and lax.ppermute only.
A program may use at most 128 MiB of HBM per device.

v0:
```python
import jax
import jax.numpy as jnp
from jax import lax
from jax.sharding import PartitionSpec as P

D_IN = 768
HID = 512
RELS = 5
FANOUT = 16


def on_device(grad_out, src_feat, weight, nbr_slot, src_ids, valid_rows, block_rel):
    grads = lax.all_gather(grad_out, "rel", axis=1, tiled=True)
    pool = lax.all_gather(src_feat, "rel", axis=0, tiled=True)
    targets = grads.shape[0]
    blocks = block_rel.shape[0]
    slot_count = src_ids.shape[2]
    weight3 = weight.reshape(D_IN, RELS, HID)
    back = jnp.einsum("th,drh->rtd", grads, weight3, preferred_element_type=jnp.float32).astype(
        jnp.bfloat16
    )
    positions = jnp.arange(targets, dtype=jnp.int32)
    slot_iota = jnp.arange(slot_count, dtype=jnp.int32)

    def adjacency(rows, block, limit):
        block_slots = lax.dynamic_slice(nbr_slot, (0, block, 0), (rows, 1, FANOUT))[:, 0, :]
        counts = jnp.zeros((rows, slot_count), jnp.float32)
        for k in range(FANOUT):
            counts = counts + (block_slots[:, k : k + 1] == slot_iota[None, :]).astype(jnp.float32)
        live = (positions < limit).astype(jnp.float32)
        return (counts * live[:, None] * (1.0 / FANOUT)).astype(jnp.bfloat16)

    def slot_grads(adj, back_rows):
        return lax.dot_general(
            adj, back_rows, (((0,), (0,)), ((), ())), preferred_element_type=jnp.float32
        )

    def one_block(carry, block):
        sums, term = carry
        ids = src_ids[0, block]
        relation = block_rel[block]
        limit = valid_rows[0, block]
        rows_x = jnp.take(pool, ids, axis=0)
        back_r = lax.dynamic_index_in_dim(back, relation, 0, keepdims=False)
        adj = adjacency(targets, block, limit)
        message = jnp.dot(adj, rows_x, preferred_element_type=jnp.float32)
        grad_slots = slot_grads(adj, back_r)
        sums = sums.at[relation].add(message)
        term = term.at[ids].add(grad_slots)
        return ((sums, term), None)

    start_state = (
        jnp.zeros((RELS, targets, D_IN), jnp.float32),
        jnp.zeros((pool.shape[0], D_IN), jnp.float32),
    )
    (sums, term), _ = lax.scan(one_block, start_state, jnp.arange(blocks, dtype=jnp.int32))
    aggregated = sums.astype(jnp.bfloat16)
    source_grad = lax.psum_scatter(
        term.astype(jnp.bfloat16), "rel", scatter_dimension=0, tiled=True
    )
    scale = float(targets * lax.axis_size("dp")) ** (-0.5)
    product = jnp.einsum("rtd,th->drh", aggregated, grads, preferred_element_type=jnp.float32)
    summed = lax.psum_scatter(
        product.reshape(
            D_IN // (lax.axis_size("dp") * lax.axis_size("rel")) * lax.axis_size(("dp", "rel")),
            RELS * HID,
        ),
        ("dp", "rel"),
        scatter_dimension=0,
        tiled=True,
    )
    return (source_grad, summed * scale)


def solution(mesh):
    return jax.shard_map(
        on_device,
        mesh=mesh,
        in_specs=(
            P("dp", "rel"),
            P(("dp", "rel"), None),
            P(),
            P("dp", "rel", None),
            P("dp", "rel", None),
            P("dp", "rel"),
            P("rel"),
        ),
        out_specs=(P(("dp", "rel"), None), P(("dp", "rel"), None)),
        check_vma=False,
    )
```

profile of v0, /device:TPU:0, one launch (start us, length us, event | category | flops | bytes accessed | tf_op | source)
XLA Modules:
  0.0 892.6 jit_solution(6006242704519920782)
XLA Ops:
  15.0 20.8 %all-gather.5.cloned.1.call-done = bf16[1024,512]{0,1:T(8,128)(2,1)} async-done(((bf16[1024,64]{0,1:T(8,128)(2,1)}), bf16[1024,512]{0,1:T(8,128)(2,1)}) %all-gather.5.cloned.1.call-update) | async-done | bytes 1048592 | tf_op jit(solution)/shard_map/all_gather | solution.py:13
  35.8 9.8 %convert_bitcast_fusion = bf16[5,1024,768]{1,2,0:T(8,128)(2,1)} fusion(bf16[768,5,512]{0,2,1:T(8,128)(2,1)} %bitcast.97, bf16[1024,512]{0,1:T(8,128)(2,1)} %all-gather.5.cloned.1.call-done), kind=kOutput, calls=%fused_computation.43 | convolution fusion | flops 4030464000 | bytes 12845056 | tf_op jit(solution)/shard_map/th,drh->rtd/dot_general | solution.py:19
  45.6 19.8 %all-gather.3.cloned.1.call-done = bf16[2048,768]{1,0:T(8,128)(2,1)} async-done(((bf16[256,768]{1,0:T(8,128)(2,1)}), bf16[2048,768]{1,0:T(8,128)(2,1)}) %all-gather.3.cloned.1.call-update) | async-done | bytes 3145744 | tf_op jit(solution)/shard_map/all_gather | solution.py:14
  75.3 305.0 %while.15 = (s32[]{:T(128)}, f32[5,1024,768]{2,1,0:T(8,128)}, f32[2048,768]{1,0:T(8,128)}, s32[8]{0:T(128)S(1)}, s32[8]{0:T(128)S(1)}, /*index=5*/s32[1024,8,16]...) while((s32[]{:T(128)}, f32[5,1024,768]{2,1,0:T(8,128)}, ...), condition=%wide.region_3.4_spmd.clone.clone, body=%wide.region_0.3_spmd.clone.clone.sunk | while | flops 1665408512 | bytes 16941852 | solution.py:56
  87.0 8.8 fusion.31
  95.8 7.6 fusion.32
  103.4 10.2 %scatter_fusion = f32[2048,768]{1,0:T(8,128)} fusion(f32[2048,768]{1,0:T(8,128)} %get-tuple-element.372, s32[512]{0:T(512)S(1)} %bitcast.99, f32[512,768]{1,0:T(8,128)} %fusion.32), kind=kCustom, calls=%fused_computation.1.clone.clone.1 | custom fusion | flops 393216 | bytes 4720640 | tf_op jit(solution)/shard_map/while/body/eval_jaxpr/scatter-add | solution.py:49
  125.1 8.8 fusion.31
  133.9 7.6 fusion.32
  141.5 10.2 %scatter_fusion = f32[2048,768]{1,0:T(8,128)} fusion(f32[2048,768]{1,0:T(8,128)} %get-tuple-element.372, s32[512]{0:T(512)S(1)} %bitcast.99, f32[512,768]{1,0:T(8,128)} %fusion.32), kind=kCustom, calls=%fused_computation.1.clone.clone.1 | custom fusion | flops 393216 | bytes 4720640 | tf_op jit(solution)/shard_map/while/body/eval_jaxpr/scatter-add | solution.py:49
  163.2 8.8 fusion.31
  179.7 10.2 %scatter_fusion = f32[2048,768]{1,0:T(8,128)} fusion(f32[2048,768]{1,0:T(8,128)} %get-tuple-element.372, s32[512]{0:T(512)S(1)} %bitcast.99, f32[512,768]{1,0:T(8,128)} %fusion.32), kind=kCustom, calls=%fused_computation.1.clone.clone.1 | custom fusion | flops 393216 | bytes 4720640 | tf_op jit(solution)/shard_map/while/body/eval_jaxpr/scatter-add | solution.py:49
  201.3 8.8 fusion.31
  210.1 7.6 fusion.32
  217.7 10.2 %scatter_fusion = f32[2048,768]{1,0:T(8,128)} fusion(f32[2048,768]{1,0:T(8,128)} %get-tuple-element.372, s32[512]{0:T(512)S(1)} %bitcast.99, f32[512,768]{1,0:T(8,128)} %fusion.32), kind=kCustom, calls=%fused_computation.1.clone.clone.1 | custom fusion | flops 393216 | bytes 4720640 | tf_op jit(solution)/shard_map/while/body/eval_jaxpr/scatter-add | solution.py:49
  239.4 8.8 fusion.31
  248.2 7.6 fusion.32
  255.8 10.2 %scatter_fusion = f32[2048,768]{1,0:T(8,128)} fusion(f32[2048,768]{1,0:T(8,128)} %get-tuple-element.372, s32[512]{0:T(512)S(1)} %bitcast.99, f32[512,768]{1,0:T(8,128)} %fusion.32), kind=kCustom, calls=%fused_computation.1.clone.clone.1 | custom fusion | flops 393216 | bytes 4720640 | tf_op jit(solution)/shard_map/while/body/eval_jaxpr/scatter-add | solution.py:49
  277.5 8.9 fusion.31
  286.4 7.6 fusion.32
  294.0 10.2 %scatter_fusion = f32[2048,768]{1,0:T(8,128)} fusion(f32[2048,768]{1,0:T(8,128)} %get-tuple-element.372, s32[512]{0:T(512)S(1)} %bitcast.99, f32[512,768]{1,0:T(8,128)} %fusion.32), kind=kCustom, calls=%fused_computation.1.clone.clone.1 | custom fusion | flops 393216 | bytes 4720640 | tf_op jit(solution)/shard_map/while/body/eval_jaxpr/scatter-add | solution.py:49
  315.6 8.8 fusion.31
  324.4 7.6 fusion.32
  332.1 10.2 %scatter_fusion = f32[2048,768]{1,0:T(8,128)} fusion(f32[2048,768]{1,0:T(8,128)} %get-tuple-element.372, s32[512]{0:T(512)S(1)} %bitcast.99, f32[512,768]{1,0:T(8,128)} %fusion.32), kind=kCustom, calls=%fused_computation.1.clone.clone.1 | custom fusion | flops 393216 | bytes 4720640 | tf_op jit(solution)/shard_map/while/body/eval_jaxpr/scatter-add | solution.py:49
  353.7 8.8 fusion.31
  362.5 7.6 fusion.32
  370.1 10.2 %scatter_fusion = f32[2048,768]{1,0:T(8,128)} fusion(f32[2048,768]{1,0:T(8,128)} %get-tuple-element.372, s32[512]{0:T(512)S(1)} %bitcast.99, f32[512,768]{1,0:T(8,128)} %fusion.32), kind=kCustom, calls=%fused_computation.1.clone.clone.1 | custom fusion | flops 393216 | bytes 4720640 | tf_op jit(solution)/shard_map/while/body/eval_jaxpr/scatter-add | solution.py:49
  386.2 11.8 %fusion.15 = f32[5,768,512]{1,2,0:T(8,128)} fusion(f32[5,1024,768]{2,1,0:T(8,128)} %get-tuple-element.123, bf16[1024,512]{0,1:T(8,128)(2,1)S(1)} %copy-done.24), kind=kOutput, calls=%fused_computation.41 | convolution fusion | flops 4030464000 | bytes 24641536 | tf_op jit(solution)/shard_map/rtd,th->drh/dot_general | solution.py:62
  398.1 9.2 %copy.19 = f32[768,2560]{1,0:T(8,128)} copy(f32[768,2560]{0,1:T(8,128)} %bitcast.96) | data formatting | bytes 15728640 | tf_op jit(solution)/shard_map/reshape | solution.py:64
  407.3 365.2 %fusion.4 = f32[8,2560]{1,0:T(8,128)S(1)} fusion(f32[768,2560]{1,0:T(8,128)} %copy.19), kind=kCustom, calls=%all-reduce-scatter | all-reduce-scatter fusion | flops 2621441 | bytes 7946240
  791.8 12.7 %collective-permute-start.17 = (f32[8,2560]{1,0:T(8,128)S(1)}, f32[8,2560]{1,0:T(8,128)S(1)}, u32[]{:S(2)}, u32[]{:S(2)}) collective-permute-start(f32[8,2560]{1,0:T(8,128)S(1)} %fusion.4), channel_id=1, source_target_pairs={{0,18},{1,19},{2,20},{3,21},{4,22},{5,23},{6,24},{7,25},{8,26},{9,... | collective-permute-start | bytes 245768
  860.5 24.9 %concatenate.6 = f32[262,2560]{1,0:T(8,128)S(1)} concatenate(f32[6,2560]{1,0:T(8,128)S(1)} %collective-permute-done.31, f32[8,2560]{1,0:T(8,128)} %copy-done.17, f32[8,2560]{1,0:T(8,128)} %copy-done.15, f32[8,2560]{1,0:T(8,128)} %copy-done.14, f32[8,2560]{1,0:T(8,128)} %copy-done.13, f32[8,2560]{1,0:T(8,128)} %copy-done.12, f32[8,2560]{1,0:T(8,128)} %copy-done.11, ...), dimensions={0} | concatenate | bytes 5365760
  (220 shorter events, 167.3 us)
Async XLA Ops:
  7.2 28.6 %all-gather.5.cloned.1.call-start = ((), (), s32[]{:S(2)}) async-start(), calls=%async_computation.2 | async-start | bytes 1179648 | tf_op jit(solution)/shard_map/all_gather | solution.py:13
  7.9 57.5 %all-gather.3.cloned.1.call-start = ((), (), s32[]{:S(2)}) async-start(), calls=%async_computation.1 | async-start | bytes 3538944 | tf_op jit(solution)/shard_map/all_gather | solution.py:14
  8.6 877.4 %reduce-scatter.4.cloned.1.call-start = ((), (), s32[]{:S(2)}) async-start(), calls=%async_computation.3 | async-start | bytes 3538944 | tf_op jit(solution)/shard_map/reduce_scatter | solution.py:58
  772.4 7.8 collective-permute-start
  775.1 6.5 collective-permute-start.1
  776.4 6.5 collective-permute-start.10
  777.7 6.6 collective-permute-start.11
  779.0 12.8 %collective-permute-start.12 = (f32[8,2560]{1,0:T(8,128)S(1)}, f32[8,2560]{1,0:T(8,128)S(1)}, u32[]{:S(2)}, u32[]{:S(2)}) collective-permute-start(f32[8,2560]{1,0:T(8,128)S(1)} %fusion.4), channel_id=1, source_target_pairs={{0,13},{1,14},{2,15},{3,16},{4,17},{5,18},{6,19},{7,20},{8,21},{9,... | collective-permute-start | bytes 245768
  780.3 24.3 %collective-permute-start.13 = (f32[8,2560]{1,0:T(8,128)S(1)}, f32[8,2560]{1,0:T(8,128)S(1)}, u32[]{:S(2)}, u32[]{:S(2)}) collective-permute-start(f32[8,2560]{1,0:T(8,128)S(1)} %fusion.4), channel_id=1, source_target_pairs={{0,14},{1,15},{2,16},{3,17},{4,18},{5,19},{6,20},{7,21},{8,22},{9,... | collective-permute-start | bytes 245768
  781.6 27.8 %collective-permute-start.14 = (f32[8,2560]{1,0:T(8,128)S(1)}, f32[8,2560]{1,0:T(8,128)S(1)}, u32[]{:S(2)}, u32[]{:S(2)}) collective-permute-start(f32[8,2560]{1,0:T(8,128)S(1)} %fusion.4), channel_id=1, source_target_pairs={{0,15},{1,16},{2,17},{3,18},{4,19},{5,20},{6,21},{7,22},{8,23},{9,... | collective-permute-start | bytes 245768
  782.9 32.4 %collective-permute-start.15 = (f32[8,2560]{1,0:T(8,128)S(1)}, f32[8,2560]{1,0:T(8,128)S(1)}, u32[]{:S(2)}, u32[]{:S(2)}) collective-permute-start(f32[8,2560]{1,0:T(8,128)S(1)} %fusion.4), channel_id=1, source_target_pairs={{0,16},{1,17},{2,18},{3,19},{4,20},{5,21},{6,22},{7,23},{8,24},{9,... | collective-permute-start | bytes 245768
  784.2 32.4 %collective-permute-start.16 = (f32[8,2560]{1,0:T(8,128)S(1)}, f32[8,2560]{1,0:T(8,128)S(1)}, u32[]{:S(2)}, u32[]{:S(2)}) collective-permute-start(f32[8,2560]{1,0:T(8,128)S(1)} %fusion.4), channel_id=1, source_target_pairs={{0,17},{1,18},{2,19},{3,20},{4,21},{5,22},{6,23},{7,24},{8,25},{9,... | collective-permute-start | bytes 245768
  791.8 28.2 %collective-permute-start.17 = (f32[8,2560]{1,0:T(8,128)S(1)}, f32[8,2560]{1,0:T(8,128)S(1)}, u32[]{:S(2)}, u32[]{:S(2)}) collective-permute-start(f32[8,2560]{1,0:T(8,128)S(1)} %fusion.4), channel_id=1, source_target_pairs={{0,18},{1,19},{2,20},{3,21},{4,22},{5,23},{6,24},{7,25},{8,26},{9,... | collective-permute-start | bytes 245768
  804.6 16.9 %collective-permute-start.18 = (f32[8,2560]{1,0:T(8,128)S(1)}, f32[8,2560]{1,0:T(8,128)S(1)}, u32[]{:S(2)}, u32[]{:S(2)}) collective-permute-start(f32[8,2560]{1,0:T(8,128)S(1)} %fusion.4), channel_id=1, source_target_pairs={{0,19},{1,20},{2,21},{3,22},{4,23},{5,24},{6,25},{7,26},{8,27},{9,... | collective-permute-start | bytes 245768
  809.4 13.9 %collective-permute-start.19 = (f32[8,2560]{1,0:T(8,128)S(1)}, f32[8,2560]{1,0:T(8,128)S(1)}, u32[]{:S(2)}, u32[]{:S(2)}) collective-permute-start(f32[8,2560]{1,0:T(8,128)S(1)} %fusion.4), channel_id=1, source_target_pairs={{0,20},{1,21},{2,22},{3,23},{4,24},{5,25},{6,26},{7,27},{8,28},{9,... | collective-permute-start | bytes 245768
  815.3 9.7 %collective-permute-start.2 = (f32[8,2560]{1,0:T(8,128)S(1)}, f32[8,2560]{1,0:T(8,128)S(1)}, u32[]{:S(2)}, u32[]{:S(2)}) collective-permute-start(f32[8,2560]{1,0:T(8,128)S(1)} %fusion.4), channel_id=1, source_target_pairs={{0,3},{1,4},{2,5},{3,6},{4,7},{5,8},{6,9},{7,10},{8,11},{9,12},{10... | collective-permute-start | bytes 245768
  816.7 10.1 %collective-permute-start.20 = (f32[8,2560]{1,0:T(8,128)S(1)}, f32[8,2560]{1,0:T(8,128)S(1)}, u32[]{:S(2)}, u32[]{:S(2)}) collective-permute-start(f32[8,2560]{1,0:T(8,128)S(1)} %fusion.4), channel_id=1, source_target_pairs={{0,21},{1,22},{2,23},{3,24},{4,25},{5,26},{6,27},{7,28},{8,29},{9,... | collective-permute-start | bytes 245768
  820.1 9.2 %collective-permute-start.21 = (f32[8,2560]{1,0:T(8,128)S(1)}, f32[8,2560]{1,0:T(8,128)S(1)}, u32[]{:S(2)}, u32[]{:S(2)}) collective-permute-start(f32[8,2560]{1,0:T(8,128)S(1)} %fusion.4), channel_id=1, source_target_pairs={{0,22},{1,23},{2,24},{3,25},{4,26},{5,27},{6,28},{7,29},{8,30},{9,... | collective-permute-start | bytes 245768
  821.5 9.1 %collective-permute-start.22 = (f32[8,2560]{1,0:T(8,128)S(1)}, f32[8,2560]{1,0:T(8,128)S(1)}, u32[]{:S(2)}, u32[]{:S(2)}) collective-permute-start(f32[8,2560]{1,0:T(8,128)S(1)} %fusion.4), channel_id=1, source_target_pairs={{0,23},{1,24},{2,25},{3,26},{4,27},{5,28},{6,29},{7,30},{8,31},{9,... | collective-permute-start | bytes 245768
  823.4 8.8 collective-permute-start.23
  825.1 11.5 %collective-permute-start.24 = (f32[8,2560]{1,0:T(8,128)S(1)}, f32[8,2560]{1,0:T(8,128)S(1)}, u32[]{:S(2)}, u32[]{:S(2)}) collective-permute-start(f32[8,2560]{1,0:T(8,128)S(1)} %fusion.4), channel_id=1, source_target_pairs={{0,25},{1,26},{2,27},{3,28},{4,29},{5,30},{6,31},{7,32},{8,33},{9,... | collective-permute-start | bytes 245768
  826.7 11.3 %collective-permute-start.25 = (f32[8,2560]{1,0:T(8,128)S(1)}, f32[8,2560]{1,0:T(8,128)S(1)}, u32[]{:S(2)}, u32[]{:S(2)}) collective-permute-start(f32[8,2560]{1,0:T(8,128)S(1)} %fusion.4), channel_id=1, source_target_pairs={{0,26},{1,27},{2,28},{3,29},{4,30},{5,31},{6,32},{7,33},{8,34},{9,... | collective-permute-start | bytes 245768
  829.3 10.1 %collective-permute-start.26 = (f32[8,2560]{1,0:T(8,128)S(1)}, f32[8,2560]{1,0:T(8,128)S(1)}, u32[]{:S(2)}, u32[]{:S(2)}) collective-permute-start(f32[8,2560]{1,0:T(8,128)S(1)} %fusion.4), channel_id=1, source_target_pairs={{0,27},{1,28},{2,29},{3,30},{4,31},{5,32},{6,33},{7,34},{8,35},{9,... | collective-permute-start | bytes 245768
  830.6 12.4 %collective-permute-start.27 = (f32[8,2560]{1,0:T(8,128)S(1)}, f32[8,2560]{1,0:T(8,128)S(1)}, u32[]{:S(2)}, u32[]{:S(2)}) collective-permute-start(f32[8,2560]{1,0:T(8,128)S(1)} %fusion.4), channel_id=1, source_target_pairs={{0,28},{1,29},{2,30},{3,31},{4,32},{5,33},{6,34},{7,35},{8,36},{9,... | collective-permute-start | bytes 245768
  832.2 12.6 %collective-permute-start.28 = (f32[8,2560]{1,0:T(8,128)S(1)}, f32[8,2560]{1,0:T(8,128)S(1)}, u32[]{:S(2)}, u32[]{:S(2)}) collective-permute-start(f32[8,2560]{1,0:T(8,128)S(1)} %fusion.4), channel_id=1, source_target_pairs={{0,29},{1,30},{2,31},{3,32},{4,33},{5,34},{6,35},{7,36},{8,37},{9,... | collective-permute-start | bytes 245768
  836.6 11.2 %collective-permute-start.29 = (f32[8,2560]{1,0:T(8,128)S(1)}, f32[8,2560]{1,0:T(8,128)S(1)}, u32[]{:S(2)}, u32[]{:S(2)}) collective-permute-start(f32[8,2560]{1,0:T(8,128)S(1)} %fusion.4), channel_id=1, source_target_pairs={{0,30},{1,31},{2,32},{3,33},{4,34},{5,35},{6,36},{7,37},{8,38},{9,... | collective-permute-start | bytes 245768
  838.1 12.0 %collective-permute-start.3 = (f32[8,2560]{1,0:T(8,128)S(1)}, f32[8,2560]{1,0:T(8,128)S(1)}, u32[]{:S(2)}, u32[]{:S(2)}) collective-permute-start(f32[8,2560]{1,0:T(8,128)S(1)} %fusion.4), channel_id=1, source_target_pairs={{0,4},{1,5},{2,6},{3,7},{4,8},{5,9},{6,10},{7,11},{8,12},{9,13},{1... | collective-permute-start | bytes 245768
  839.4 13.5 %collective-permute-start.30 = (f32[8,2560]{1,0:T(8,128)S(1)}, f32[8,2560]{1,0:T(8,128)S(1)}, u32[]{:S(2)}, u32[]{:S(2)}) collective-permute-start(f32[8,2560]{1,0:T(8,128)S(1)} %fusion.4), channel_id=1, source_target_pairs={{0,31},{1,32},{2,33},{3,34},{4,35},{5,36},{6,37},{7,38},{8,39},{9,... | collective-permute-start | bytes 245768
  843.0 13.1 %collective-permute-start.4 = (f32[8,2560]{1,0:T(8,128)S(1)}, f32[8,2560]{1,0:T(8,128)S(1)}, u32[]{:S(2)}, u32[]{:S(2)}) collective-permute-start(f32[8,2560]{1,0:T(8,128)S(1)} %fusion.4), channel_id=1, source_target_pairs={{0,5},{1,6},{2,7},{3,8},{4,9},{5,10},{6,11},{7,12},{8,13},{9,14},{... | collective-permute-start | bytes 245768
  844.9 14.0 %collective-permute-start.5 = (f32[8,2560]{1,0:T(8,128)S(1)}, f32[8,2560]{1,0:T(8,128)S(1)}, u32[]{:S(2)}, u32[]{:S(2)}) collective-permute-start(f32[8,2560]{1,0:T(8,128)S(1)} %fusion.4), channel_id=1, source_target_pairs={{0,6},{1,7},{2,8},{3,9},{4,10},{5,11},{6,12},{7,13},{8,14},{9,15},... | collective-permute-start | bytes 245768
  847.9 11.0 %collective-permute-start.6 = (f32[8,2560]{1,0:T(8,128)S(1)}, f32[8,2560]{1,0:T(8,128)S(1)}, u32[]{:S(2)}, u32[]{:S(2)}) collective-permute-start(f32[8,2560]{1,0:T(8,128)S(1)} %fusion.4), channel_id=1, source_target_pairs={{0,7},{1,8},{2,9},{3,10},{4,11},{5,12},{6,13},{7,14},{8,15},{9,16}... | collective-permute-start | bytes 245768
  850.1 8.8 collective-permute-start.7
  (30 other events, 460.2 us)
Sparse Core Ops, SparseCore 0:
  9.7 26.0 all-gather.4
  37.5 27.8 all-gather.2
  385.2 36.6 reduce-scatter.3
where the time goes:
time: 901 us; the launch traced here: 893 us
  blocking collectives  365 us (41%)
  matrix products  153 us (17%)
  other arithmetic  104 us (12%)
  local copies, waits for them, and re-layouts  96.1 us (11%)
  starting transfers between devices  85.8 us (10%)
  waiting for transfers between devices  42.4 us (5%)
  loops' own time  31.4 us (3%)
  between operations  14.6 us (2%)
    unnamed x1, blocking collectives  365 us
    unnamed x32, starting transfers between devices  85.7 us
    scatter-add x8, other arithmetic, one_block(): term = term.at[ids].add(grad_slots)  81.3 us
    dot_general x8, matrix products, one_block(): message = jnp.dot(adj, rows_x, preferred_element_type=jnp.float32)  70.6 us
    dot_general x8, matrix products, slot_grads(): lax.dot_general(adj, back_rows, (((0,), (0,)), ((), ())), preferred_eleme...  60.9 us
    unnamed x57, local copies, waits for them, and re-layouts  33.6 us
    another operation x1, loops' own time, on_device(): lax.scan(one_block, start_state, jnp.arange(blocks, dtype=jnp.int32))  31.4 us
    gather x8, local copies, waits for them, and re-layouts, one_block(): rows_x = jnp.take(pool, ids, axis=0)  21.7 us
  transfers between devices with their start and end apart: 35, of which 3 were waited for; matrix products, arithmetic and copies ran while one was open for 48% of the time, Pallas kernels for 0%

commit v1 on v0

v1 whole, which is shorter than its diff:
```python
import jax
import jax.numpy as jnp
from jax import lax
from jax.experimental import pallas as pl
from jax.experimental.pallas import tpu as pltpu
from jax.sharding import PartitionSpec as P

I32 = jnp.int32
BF16 = jnp.bfloat16
F32 = jnp.float32
D_IN = 768
HID = 512
RELS = 5
COLS = RELS * HID
FANOUT = 16
SLOTS = 512
TGT = 1024
BLKS = 8
POOL = 2048
OWN = 256
NO_EDGE = RELS * POOL
TILE = 256
PLANES = 10
SLICE = COLS // 8
ROWS_OUT = 6
LANES = 128


def edge_kernel(valid_ref, rel_ref, ids_ref, nbr_ref, out_ref):
    lane = lax.broadcasted_iota(I32, (8, LANES), 1)
    sub = lax.broadcasted_iota(I32, (8, LANES), 0)
    meta = jnp.zeros((8, LANES), I32)
    for b in range(BLKS):
        rel = rel_ref[b]
        limit = valid_ref[0, b]
        meta = jnp.where((sub == b) & (lane == 0), rel, meta)
        meta = jnp.where((sub == b) & (lane == 1), (limit + (TILE - 1)) // TILE, meta)
        node = ids_ref[b : b + 1, :]
        code = rel * POOL + (node & 1792) + ((node & 7) << 5) + ((node >> 3) & 31)
        tables = [
            jnp.broadcast_to(code[:, i * LANES : (i + 1) * LANES], (8, LANES))
            for i in range(SLOTS // LANES)
        ]
        for t in range(TGT // LANES):
            cols = slice(t * LANES, (t + 1) * LANES)
            live = (lane + t * LANES) < limit
            halves = []
            for half in range(2):
                slot = nbr_ref[b, half * 8 : (half + 1) * 8, cols]
                low = slot & (LANES - 1)
                high = slot >> 7
                got = [
                    jnp.take_along_axis(table, low, axis=1, mode="promise_in_bounds")
                    for table in tables
                ]
                found = jnp.where(
                    high < 2,
                    jnp.where(high == 0, got[0], got[1]),
                    jnp.where(high == 2, got[2], got[3]),
                )
                halves.append(jnp.where(live, found, NO_EDGE))
            out_ref[b, :, cols] = halves[0] | (halves[1] << 16)
    out_ref[BLKS, :, 0:LANES] = meta
    out_ref[BLKS, :, LANES:TGT] = jnp.zeros((8, TGT - LANES), I32)


def edge_codes(valid_rows, block_rel, ids, nbr):
    return pl.pallas_call(
        edge_kernel,
        out_shape=jax.ShapeDtypeStruct((BLKS + 1, 8, TGT), I32),
        in_specs=[pl.BlockSpec(memory_space=pltpu.SMEM)] * 2
        + [pl.BlockSpec(memory_space=pltpu.VMEM)] * 2,
        out_specs=pl.BlockSpec(memory_space=pltpu.VMEM),
        cost_estimate=pl.CostEstimate(flops=0, bytes_accessed=1 << 20, transcendentals=0),
        name="edge_codes",
    )(valid_rows, block_rel, ids, nbr)


def full_add(a, b, c):
    x = a ^ b
    return x ^ c, (a & b) | (c & x)


def count_bits(masks, planes):
    carried = masks
    out = []
    for i in range(PLANES):
        cur = carried + [planes[i]]
        carried = []
        while len(cur) >= 3:
            s, c = full_add(cur[0], cur[1], cur[2])
            cur = cur[3:] + [s]
            carried.append(c)
        if len(cur) == 2:
            carried.append(cur[0] & cur[1])
            cur = [cur[0] ^ cur[1]]
        out.append(cur[0])
    return out


def swap_bits(a, b, shift, mask):
    t = (lax.shift_right_logical(a, jnp.int32(shift)) ^ b) & mask
    return a ^ (t << shift), b ^ t


def plane_bytes(planes):
    x = list(planes)
    for shift, mask in ((4, 0x0F0F0F0F), (2, 0x33333333), (1, 0x55555555)):
        for i in range(8):
            if not i & shift:
                x[i], x[i + shift] = swap_bits(x[i], x[i + shift], shift, mask)
    return x


def counts(planes):
    low = plane_bytes(planes[:8])
    rows = [None] * 32
    for off in range(8):
        high = None
        for i in range(8, PLANES):
            f = lax.shift_right_logical(planes[i], jnp.int32(off)) & 0x01010101
            f = f << (i - 8)
            high = f if high is None else high | f
        for q in range(4):
            a = lax.shift_right_logical(low[off], jnp.int32(8 * q)) & 255
            h = lax.shift_right_logical(high, jnp.int32(8 * q)) & 3
            rows[off + 8 * q] = (a | (h << 8)).astype(F32)
    return jnp.concatenate(rows, axis=0).astype(BF16)


def hidden_kernel(place_ref, *refs):
    edges = refs[:8]
    grads_ref, weight_ref = refs[8:10]
    source_ref = refs[10]
    pieces = refs[11:19]
    planes_ref, keys, meta, weight_vmem, adj, hidden, meta_sems, weight_sem = refs[19:]
    mine, x, core = place_ref[0], place_ref[1], place_ref[2]
    fetch = pltpu.make_async_copy(weight_ref, weight_vmem, weight_sem)
    fetch.start()
    metas = [
        pltpu.make_async_copy(edges[i].at[BLKS, :, pl.ds(0, LANES)], meta.at[i], meta_sems.at[i])
        for i in range(8)
    ]
    for copy in metas:
        copy.start()
    planes_ref[...] = jnp.zeros_like(planes_ref)
    row = lax.broadcasted_iota(I32, (8, TILE), 0)
    for copy in metas:
        copy.wait()
    for i in range(8):

        def one_block(b, carry, i=i):
            rel = meta[i, b, 0]
            tiles = meta[i, b, 1]
            word = edges[i][b]
            for half, code in enumerate((word & 0xFFFF, word >> 16)):
                keys[half, 0] = code >> 5
                keys[half, 1] = jnp.left_shift(jnp.int32(1), code & 31)
            target = row + (rel * (POOL // 32) + mine * (OWN // 32))

            def one_tile(t, carry):
                cols = pl.ds(pl.multiple_of(t * TILE, TILE), TILE)
                masks = []
                for half in range(2):
                    for s in range(8):
                        key = jnp.broadcast_to(keys[half, 0, pl.ds(s, 1), cols], (8, TILE))
                        bit = jnp.broadcast_to(keys[half, 1, pl.ds(s, 1), cols], (8, TILE))
                        masks.append(jnp.where(key == target, bit, 0))
                new = count_bits(masks, [planes_ref[rel, p, :, cols] for p in range(PLANES)])
                for p in range(PLANES):
                    planes_ref[rel, p, :, cols] = new[p]
                return carry

            return lax.fori_loop(0, tiles, one_tile, carry)

        lax.fori_loop(0, BLKS, one_block, 0)
    fetch.wait()
    total = None
    for r in range(RELS):

        def one_part(t, carry, r=r):
            cols = pl.ds(pl.multiple_of(t * LANES, LANES), LANES)
            adj[:, cols] = counts([planes_ref[r, p, :, cols] for p in range(PLANES)])
            return carry

        lax.fori_loop(0, TGT // LANES, one_part, 0)
        h = lax.dot_general(
            adj[...], grads_ref[...], (((1,), (1,)), ((), ())), preferred_element_type=F32
        )
        h = (h * (1.0 / FANOUT)).astype(BF16)
        term = lax.dot_general(
            h,
            weight_vmem[:, r * HID : (r + 1) * HID],
            (((1,), (1,)), ((), ())),
            preferred_element_type=F32,
        )
        total = term if total is None else total + term
        ht = h.T
        for q in range(HID // 64):
            at = r * (HID // 64) + q
            s, within = at // 5, at % 5
            pos = (s // 4 ^ core) * 4 + ((s % 4 - x) & 3)
            start = pl.multiple_of(pos * SLICE + within * 64, 64)
            hidden[pl.ds(start, 64), :] = ht[q * 64 : (q + 1) * 64, :]
    source_ref[...] = total.astype(BF16)
    for i in range(8):
        pieces[i][...] = hidden[i * SLICE : (i + 1) * SLICE, :]


def hidden_parts(place, edges, grads, weight):
    vmem = pl.BlockSpec(memory_space=pltpu.VMEM)
    return pl.pallas_call(
        hidden_kernel,
        out_shape=[jax.ShapeDtypeStruct((OWN, D_IN), BF16)]
        + [jax.ShapeDtypeStruct((SLICE, OWN), BF16)] * 8,
        in_specs=[pl.BlockSpec(memory_space=pltpu.SMEM)]
        + [vmem] * 9
        + [pl.BlockSpec(memory_space=pl.ANY)],
        out_specs=[vmem] * 9,
        scratch_shapes=[
            pltpu.VMEM((RELS, PLANES, 8, TGT), I32),
            pltpu.VMEM((2, 2, 8, TGT), I32),
            pltpu.SMEM((8, 8, LANES), I32),
            pltpu.VMEM((D_IN, COLS), BF16),
            pltpu.VMEM((OWN, TGT), BF16),
            pltpu.VMEM((COLS, OWN), BF16),
            pltpu.SemaphoreType.DMA((8,)),
            pltpu.SemaphoreType.DMA,
        ],
        compiler_params=pltpu.CompilerParams(vmem_limit_bytes=40 << 20),
        cost_estimate=pl.CostEstimate(
            flops=14_000_000_000, bytes_accessed=9 << 20, transcendentals=0
        ),
        name="hidden_parts",
    )(place, *edges, grads, weight)


def product_kernel(*refs):
    hiddens, pools = refs[:8], refs[8:16]
    out_ref, flat, chunks = refs[16:]
    total = None
    for i in range(8):
        term = jnp.dot(hiddens[i][...], pools[i][...], preferred_element_type=F32)
        total = term if total is None else total + term
    for r in range(ROWS_OUT):
        flat[:, r * SLICE : (r + 1) * SLICE] = total[:, r * LANES : (r + 1) * LANES].T
    for c in range(15):
        chunks[:, c, :] = flat[:, c * LANES : (c + 1) * LANES]
    chunks[:, 15, :] = jnp.zeros((LANES, LANES), F32)
    out_ref[...] = chunks[...].astype(BF16)


def products(hiddens, pools):
    vmem = pl.BlockSpec(memory_space=pltpu.VMEM)
    return pl.pallas_call(
        product_kernel,
        out_shape=jax.ShapeDtypeStruct((LANES, 16, LANES), BF16),
        in_specs=[vmem] * 16,
        out_specs=vmem,
        scratch_shapes=[
            pltpu.VMEM((LANES, ROWS_OUT * SLICE), F32),
            pltpu.VMEM((LANES, 16, LANES), F32),
        ],
        compiler_params=pltpu.CompilerParams(vmem_limit_bytes=40 << 20),
        cost_estimate=pl.CostEstimate(
            flops=1_000_000_000, bytes_accessed=5 << 20, transcendentals=0
        ),
        name="products",
    )(*hiddens, *pools)


def on_device(grad_out, src_feat, weight, nbr_slot, src_ids, valid_rows, block_rel):
    dp, rel = lax.axis_index("dp"), lax.axis_index("rel")
    place = jnp.stack([rel, dp // 4, rel % 2]).astype(I32)

    def along_z(v, k):
        return lax.ppermute(v, "rel", [(i, (i + 2 * k) % 8) for i in range(8)])

    def other_core(v):
        return lax.ppermute(v, "rel", [(i, i ^ 1) for i in range(8)])

    def along_x(v, k):
        return lax.ppermute(v, "dp", [(i, (i + 4 * k) % 16) for i in range(16)])

    grads = lax.all_gather(grad_out.T, "rel", axis=0, tiled=True)
    codes = edge_codes(valid_rows, block_rel, src_ids[0], nbr_slot.transpose(1, 2, 0))
    mine = [codes] + [along_z(codes, k) for k in (1, 2, 3)]
    edges = mine + [other_core(v) for v in mine]

    old = jnp.arange(D_IN, dtype=I32)[:, None]
    new = jnp.arange(D_IN, dtype=I32)[None, :]
    order = (old == (new % LANES) * ROWS_OUT + new // LANES).astype(BF16)
    feats = jnp.dot(src_feat, order, preferred_element_type=F32).astype(BF16)
    near = [feats] + [along_x(feats, k) for k in (1, 2, 3)]
    pools = near + [other_core(v) for v in near]

    source_grad, *parts = hidden_parts(place, edges, grads, weight)
    own = parts[:4]
    far = [other_core(v) for v in parts[4:]]
    hiddens = [own[0]] + [along_x(own[k], k) for k in (1, 2, 3)]
    hiddens += [far[0]] + [along_x(far[k], k) for k in (1, 2, 3)]
    chunks = products(hiddens, pools)
    got = lax.all_to_all(chunks, ("dp", "rel"), 0, 0, tiled=True)
    got = got.reshape(4, 16, 2, 16 * LANES).astype(F32)
    summed = jnp.sum(got, axis=1)[:, :, : ROWS_OUT * SLICE]
    summed = summed.reshape(4, 2, ROWS_OUT, SLICE).transpose(2, 1, 0, 3).reshape(ROWS_OUT, COLS)
    scale = float(TGT * 16) ** (-0.5)
    return source_grad, summed * scale


def solution(mesh):
    return jax.shard_map(
        on_device,
        mesh=mesh,
        in_specs=(
            P("dp", "rel"),
            P(("dp", "rel"), None),
            P(),
            P("dp", "rel", None),
            P("dp", "rel", None),
            P("dp", "rel"),
            P("rel"),
        ),
        out_specs=(P(("dp", "rel"), None), P(("dp", "rel"), None)),
        check_vma=False,
    )
```

time: 901 us -> 126 us (0.14)
  blocking collectives: 365 us -> 23.9 us
  matrix products: 153 us -> 0.63 us
  other arithmetic: 104 us -> 0.59 us
  local copies, waits for them, and re-layouts: 96.1 us -> 10.8 us
  starting transfers between devices: 85.8 us -> 21.1 us
  loops' own time: 31.4 us -> 0 us
  Pallas kernels: 0 us -> 21.7 us
  waiting for transfers between devices: 42.4 us -> 32.4 us
    unnamed x1 -> x0, blocking collectives: 365 us -> none
    dot_general x18 -> x1, matrix products: 153 us -> 0.63 us  [on_device(): feats = jnp.dot(src_feat, order, preferred_element_type=F32).astype(BF16)]
    unnamed x32 -> x0, starting transfers between devices: 85.7 us -> none
    scatter-add x8 -> x0, other arithmetic: 81.3 us -> none  [one_block(): term = term.at[ids].add(grad_slots)]
    all_gather x2 -> x1, waiting for transfers between devices: 40.6 us -> 0.01 us  [on_device(): grads = lax.all_gather(grad_out.T, 'rel', axis=0, tiled=True)]
    ppermute x0 -> x24, waiting for transfers between devices: none -> 31.8 us  [the longest x9 16.6 us: along_x(): return lax.ppermute(v, 'dp', [(i, (i + 4 * k) % 16) for i in range(16)])]
    another operation x1 -> x0, loops' own time: 31.4 us -> none  [on_device(): lax.scan(one_block, start_state, jnp.arange(blocks, dtype=jnp.int32))]
    unnamed x57 -> x20, local copies, waits for them, and re-layouts: 33.6 us -> 9.36 us
  transfers between devices with their start and end apart: 35 -> 25, of which waited for: 3 -> 7; matrix products, arithmetic and copies ran while one was open for 48% -> 1% of each run, Pallas kernels for 0% -> 16%
where the time goes in v1:
time: 126 us; the launch traced here: 125 us
  waiting for transfers between devices  32.4 us (26%)
  blocking collectives  23.9 us (19%)
  Pallas kernels  21.7 us (17%)
  starting transfers between devices  21.1 us (17%)
  between operations  14.2 us (11%)
  local copies, waits for them, and re-layouts  10.8 us (9%)
    all_to_all x1, blocking collectives, on_device(): got = lax.all_to_all(chunks, ('dp', 'rel'), 0, 0, tiled=True)  23.9 us
    pallas_call x1, Pallas kernels, hidden_parts(): pl.pallas_call(hidden_kernel, out_shape=[jax.ShapeDtypeStruct((OWN, D_IN)...  16.9 us
    ppermute x9, waiting for transfers between devices, along_x(): return lax.ppermute(v, 'dp', [(i, (i + 4 * k) % 16) for i in range(16)])  16.6 us
    ppermute x3, waiting for transfers between devices, along_z(): return lax.ppermute(v, 'rel', [(i, (i + 2 * k) % 8) for i in range(8)])  15.1 us
    ppermute x9, starting transfers between devices, along_x(): return lax.ppermute(v, 'dp', [(i, (i + 4 * k) % 16) for i in range(16)])  13.9 us
    unnamed x20, local copies, waits for them, and re-layouts  9.36 us
    ppermute x3, starting transfers between devices, along_z(): return lax.ppermute(v, 'rel', [(i, (i + 2 * k) % 8) for i in range(8)])  5.38 us
    pallas_call x1, Pallas kernels, edge_codes(): pl.pallas_call(edge_kernel, out_shape=jax.ShapeDtypeStruct((BLKS + 1, 8,...  2.8 us
  transfers between devices with their start and end apart: 25, of which 7 were waited for; matrix products, arithmetic and copies ran while one was open for 1% of the time, Pallas kernels for 16%

profile of v1, /device:TPU:0, one launch (start us, length us, event | category | flops | bytes accessed | tf_op | source)
XLA Modules:
  0.0 125.3 jit_solution(11360224270418291443)
XLA Ops:
  7.2 0.7 all-gather.2.cloned.1.call-update
  7.9 2.8 %edge_codes.1.refs_0_ = s32[9,8,1024]{2,1,0:T(8,128)} custom-call(s32[1,8]{1,0:T(1,128)} %valid_ref.1, s32[8]{0:T(128)} %rel_ref.1, s32[8,512]{1,0:T(8,128)} %bitcast.13, s32[8,16,1024]{2,1,0:T(8,128)} %bitcast.10), custom_call_target="tpu_custom_call" | custom-call | bytes 1048576 | tf_op jit(solution)/shard_map/edge_codes/pallas_call | solution.py:68
  10.7 4.1 %collective-permute-start.2 = (s32[9,8,1024]{2,1,0:T(8,128)}, s32[9,8,1024]{2,1,0:T(8,128)S(1)}, u32[]{:S(2)}, u32[]{:S(2)}) collective-permute-start(s32[9,8,1024]{2,1,0:T(8,128)} %edge_codes.1.refs_0_), channel_id=1, source_target_pairs={{0,6},{1,7},{2,0},{3,1},{4,2},{5,3},{6,4},{7,5},{8,14},{9,15},{10,... | collective-permute-start | bytes 884744 | tf_op jit(solution)/shard_map/ppermute | solution.py:277
  14.8 0.6 fusion.2.refs_8_
  15.5 2.8 %collective-permute-start.19 = (bf16[256,768]{1,0:T(8,128)(2,1)S(1)}, bf16[256,768]{1,0:T(8,128)(2,1)S(1)}, u32[]{:S(2)}, u32[]{:S(2)}) collective-permute-start(bf16[256,768]{1,0:T(8,128)(2,1)S(1)} %fusion.2.refs_8_), channel_id=1, source_target_pairs={{0,96},{8,104},{16,112},{24,120},{32,0},{40,8},{48,16},{56,24},{64... | collective-permute-start | bytes 1179656 | tf_op jit(solution)/shard_map/ppermute | solution.py:283
  18.3 1.3 %collective-permute-start = (s32[9,8,1024]{2,1,0:T(8,128)}, s32[9,8,1024]{2,1,0:T(8,128)}, u32[]{:S(2)}, u32[]{:S(2)}) collective-permute-start(s32[9,8,1024]{2,1,0:T(8,128)} %edge_codes.1.refs_0_), channel_id=1, source_target_pairs={{0,2},{1,3},{2,4},{3,5},{4,6},{5,7},{6,0},{7,1},{8,10},{9,11},{10,... | collective-permute-start | bytes 884744 | tf_op jit(solution)/shard_map/ppermute | solution.py:277
  19.6 0.7 copy-done.4
  20.3 0.8 collective-permute-start.18
  21.1 9.1 %collective-permute-done.2.refs_3_ = s32[9,8,1024]{2,1,0:T(8,128)S(1)} collective-permute-done((s32[9,8,1024]{2,1,0:T(8,128)}, s32[9,8,1024]{2,1,0:T(8,128)S(1)}, u32[]{:S(2)}, u32[]{:S(2)}) %collective-permute-start.2) | collective-permute-done | bytes 294944 | tf_op jit(solution)/shard_map/ppermute | solution.py:277
  30.2 2.2 %collective-permute-start.17 = (bf16[256,768]{1,0:T(8,128)(2,1)S(1)}, bf16[256,768]{1,0:T(8,128)(2,1)S(1)}, u32[]{:S(2)}, u32[]{:S(2)}) collective-permute-start(bf16[256,768]{1,0:T(8,128)(2,1)S(1)} %fusion.2.refs_8_), channel_id=1, source_target_pairs={{0,32},{8,40},{16,48},{24,56},{32,64},{40,72},{48,80},{56,88},{64,... | collective-permute-start | bytes 1179656 | tf_op jit(solution)/shard_map/ppermute | solution.py:283
  32.4 0.7 copy-done.6
  33.2 6.1 %collective-permute-done.refs_1_ = s32[9,8,1024]{2,1,0:T(8,128)} collective-permute-done((s32[9,8,1024]{2,1,0:T(8,128)}, s32[9,8,1024]{2,1,0:T(8,128)}, u32[]{:S(2)}, u32[]{:S(2)}) %collective-permute-start) | collective-permute-done | bytes 294944 | tf_op jit(solution)/shard_map/ppermute | solution.py:277
  39.2 0.7 copy-done.8
  40.6 1.6 %collective-permute-done.17.refs_9_ = bf16[256,768]{1,0:T(8,128)(2,1)S(1)} collective-permute-done((bf16[256,768]{1,0:T(8,128)(2,1)S(1)}, bf16[256,768]{1,0:T(8,128)(2,1)S(1)}, u32[]{:S(2)}, u32[]{:S(2)}) %collective-permute-start.17) | collective-permute-done | bytes 393248 | tf_op jit(solution)/shard_map/ppermute | solution.py:283
  42.8 1.0 copy-done.1
  43.7 2.1 %copy-done.2 = bf16[768,2560]{1,0:T(8,128)(2,1)S(1)} copy-done((bf16[768,2560]{1,0:T(8,128)(2,1)S(1)}, bf16[768,2560]{1,0:T(8,128)(2,1)}, u32[]{:S(2)}) %copy-start.2) | copy-done | bytes 3932184
  45.8 1.2 copy-done.3
  47.1 1.0 copy-done.5
  48.0 1.0 copy-done.7
  49.0 1.0 copy-done.9
  50.0 16.9 %hidden_parts.1 = (bf16[256,768]{1,0:T(8,128)(2,1)}, bf16[320,256]{1,0:T(8,128)(2,1)S(1)}, bf16[320,256]{1,0:T(8,128)(2,1)S(1)}, bf16[320,256]{1,0:T(8,128)(2,1)...) custom-call(s32[3]{0:T(128)S(1)} %pad_add_fusion.place_ref, ...), custom_call_target="tpu_custom_call" | custom-call | flops 14000000000 | bytes 9437184 | tf_op jit(solution)/shard_map/hidden_parts/pallas_call | solution.py:212
  67.4 2.6 %collective-permute-start.8 = (bf16[320,256]{1,0:T(8,128)(2,1)S(1)}, bf16[320,256]{1,0:T(8,128)(2,1)S(1)}, u32[]{:S(2)}, u32[]{:S(2)}) collective-permute-start(bf16[320,256]{1,0:T(8,128)(2,1)S(1)} %get-tuple-element.14), channel_id=1, source_target_pairs={{0,64},{8,72},{16,80},{24,88},{32,96},{40,104},{48,112},{56,120},{... | collective-permute-start | bytes 491528 | tf_op jit(solution)/shard_map/ppermute | solution.py:283
  70.5 7.7 %collective-permute-done.7.refs_1_ = bf16[320,256]{1,0:T(8,128)(2,1)S(1)} collective-permute-done((bf16[320,256]{1,0:T(8,128)(2,1)S(1)}, bf16[320,256]{1,0:T(8,128)(2,1)S(1)}, u32[]{:S(2)}, u32[]{:S(2)}) %collective-permute-start.7) | collective-permute-done | bytes 163872 | tf_op jit(solution)/shard_map/ppermute | solution.py:283
  78.2 2.3 %collective-permute-start.12 = (bf16[320,256]{1,0:T(8,128)(2,1)S(1)}, bf16[320,256]{1,0:T(8,128)(2,1)S(1)}, u32[]{:S(2)}, u32[]{:S(2)}) collective-permute-start(bf16[320,256]{1,0:T(8,128)(2,1)S(1)} %collective-permute-done.11), channel_id=1, source_target_pairs={{0,32},{8,40},{16,48},{24,56},{32,64},{40,72},{48,80},{56,88},{64,... | collective-permute-start | bytes 491528 | tf_op jit(solution)/shard_map/ppermute | solution.py:283
  80.5 2.8 %collective-permute-start.16 = (bf16[320,256]{1,0:T(8,128)(2,1)S(1)}, bf16[320,256]{1,0:T(8,128)(2,1)S(1)}, u32[]{:S(2)}, u32[]{:S(2)}) collective-permute-start(bf16[320,256]{1,0:T(8,128)(2,1)S(1)} %collective-permute-done.15), channel_id=1, source_target_pairs={{0,96},{8,104},{16,112},{24,120},{32,0},{40,8},{48,16},{56,24},{64... | collective-permute-start | bytes 491528 | tf_op jit(solution)/shard_map/ppermute | solution.py:283
  83.3 0.6 collective-permute-done.9.refs_3_
  83.9 5.7 %collective-permute-done.12.refs_5_ = bf16[320,256]{1,0:T(8,128)(2,1)S(1)} collective-permute-done((bf16[320,256]{1,0:T(8,128)(2,1)S(1)}, bf16[320,256]{1,0:T(8,128)(2,1)S(1)}, u32[]{:S(2)}, u32[]{:S(2)}) %collective-permute-start.12) | collective-permute-done | bytes 163872 | tf_op jit(solution)/shard_map/ppermute | solution.py:283
  89.6 1.0 collective-permute-done.16.refs_7_
  90.6 2.0 %products.1 = bf16[128,16,128]{2,1,0:T(8,128)(2,1)S(1)} custom-call(bf16[320,256]{1,0:T(8,128)(2,1)S(1)} %get-tuple-element.12.refs_0_, bf16[320,256]{1,0:T(8,128)(2,1)S(1)} %collective-permute-done.7.refs_1_, bf16[320,256]{1,0:T(8,128)(2,1)S(1)} %collective-permute-done.8.refs_2_, bf16[320,256]{1,0:T(8,128)(2,1)S(1)} %collective-permute-done.9.refs_3_, ...), custom_call_target="tpu_custom_call" | custom-call | flops 1000000000 | bytes 5242880 | tf_op jit(solution)/shard_map/products/pallas_call | solution.py:255
  92.6 23.9 %all_to_all.5 = bf16[128,16,128]{2,1,0:T(8,128)(2,1)S(1)} all-to-all(bf16[128,16,128]{2,1,0:T(8,128)(2,1)S(1)} %products.1), channel_id=1, replica_groups=mesh['dp'=16,'rel'=8] {'dp','rel'}, dimensions={0} | all-to-all | bytes 1048576 | tf_op jit(solution)/shard_map/all_to_all | solution.py:303
  116.5 0.5 reshape.68
  117.7 0.7 mul.32
  (52 shorter events, 3.1 us)
Async XLA Ops:
  7.2 7.7 %copy-start = (bf16[256,768]{1,0:T(8,128)(2,1)S(1)}, bf16[256,768]{1,0:T(8,128)(2,1)}, u32[]{:S(2)}) copy-start(bf16[256,768]{1,0:T(8,128)(2,1)} %param.8) | copy-start | bytes 1179652
  7.2 35.6 %all-gather.2.cloned.1.call-start = ((), (), s32[]{:S(2)}) async-start(), calls=%async_computation.1 | async-start | bytes 1179648 | tf_op jit(solution)/shard_map/all_gather | solution.py:285
  10.7 8.9 %collective-permute-start.3 = (s32[9,8,1024]{2,1,0:T(8,128)}, s32[9,8,1024]{2,1,0:T(8,128)S(1)}, u32[]{:S(2)}, u32[]{:S(2)}) collective-permute-start(s32[9,8,1024]{2,1,0:T(8,128)} %edge_codes.1.refs_0_), channel_id=1, source_target_pairs={{0,1},{1,0},{2,3},{3,2},{4,5},{5,4},{6,7},{7,6},{8,9},{9,8},{10,11... | collective-permute-start | bytes 884744 | tf_op jit(solution)/shard_map/ppermute | solution.py:280
  10.7 19.5 %collective-permute-start.2 = (s32[9,8,1024]{2,1,0:T(8,128)}, s32[9,8,1024]{2,1,0:T(8,128)S(1)}, u32[]{:S(2)}, u32[]{:S(2)}) collective-permute-start(s32[9,8,1024]{2,1,0:T(8,128)} %edge_codes.1.refs_0_), channel_id=1, source_target_pairs={{0,6},{1,7},{2,0},{3,1},{4,2},{5,3},{6,4},{7,5},{8,14},{9,15},{10,... | collective-permute-start | bytes 884744 | tf_op jit(solution)/shard_map/ppermute | solution.py:277
  15.5 24.5 %collective-permute-start.19 = (bf16[256,768]{1,0:T(8,128)(2,1)S(1)}, bf16[256,768]{1,0:T(8,128)(2,1)S(1)}, u32[]{:S(2)}, u32[]{:S(2)}) collective-permute-start(bf16[256,768]{1,0:T(8,128)(2,1)S(1)} %fusion.2.refs_8_), channel_id=1, source_target_pairs={{0,96},{8,104},{16,112},{24,120},{32,0},{40,8},{48,16},{56,24},{64... | collective-permute-start | bytes 1179656 | tf_op jit(solution)/shard_map/ppermute | solution.py:283
  18.3 14.1 %collective-permute-start.1 = (s32[9,8,1024]{2,1,0:T(8,128)}, s32[9,8,1024]{2,1,0:T(8,128)S(1)}, u32[]{:S(2)}, u32[]{:S(2)}) collective-permute-start(s32[9,8,1024]{2,1,0:T(8,128)} %edge_codes.1.refs_0_), channel_id=1, source_target_pairs={{0,4},{1,5},{2,6},{3,7},{4,0},{5,1},{6,2},{7,3},{8,12},{9,13},{10,... | collective-permute-start | bytes 884744 | tf_op jit(solution)/shard_map/ppermute | solution.py:277
  18.3 20.9 %collective-permute-start = (s32[9,8,1024]{2,1,0:T(8,128)}, s32[9,8,1024]{2,1,0:T(8,128)}, u32[]{:S(2)}, u32[]{:S(2)}) collective-permute-start(s32[9,8,1024]{2,1,0:T(8,128)} %edge_codes.1.refs_0_), channel_id=1, source_target_pairs={{0,2},{1,3},{2,4},{3,5},{4,6},{5,7},{6,0},{7,1},{8,10},{9,11},{10,... | collective-permute-start | bytes 884744 | tf_op jit(solution)/shard_map/ppermute | solution.py:277
  20.3 20.2 %collective-permute-start.18 = (bf16[256,768]{1,0:T(8,128)(2,1)S(1)}, bf16[256,768]{1,0:T(8,128)(2,1)S(1)}, u32[]{:S(2)}, u32[]{:S(2)}) collective-permute-start(bf16[256,768]{1,0:T(8,128)(2,1)S(1)} %fusion.2.refs_8_), channel_id=1, source_target_pairs={{0,64},{8,72},{16,80},{24,88},{32,96},{40,104},{48,112},{56,120},{... | collective-permute-start | bytes 1179656 | tf_op jit(solution)/shard_map/ppermute | solution.py:283
  30.2 12.0 %collective-permute-start.17 = (bf16[256,768]{1,0:T(8,128)(2,1)S(1)}, bf16[256,768]{1,0:T(8,128)(2,1)S(1)}, u32[]{:S(2)}, u32[]{:S(2)}) collective-permute-start(bf16[256,768]{1,0:T(8,128)(2,1)S(1)} %fusion.2.refs_8_), channel_id=1, source_target_pairs={{0,32},{8,40},{16,48},{24,56},{32,64},{40,72},{48,80},{56,88},{64,... | collective-permute-start | bytes 1179656 | tf_op jit(solution)/shard_map/ppermute | solution.py:283
  32.4 9.8 %collective-permute-start.6 = (s32[9,8,1024]{2,1,0:T(8,128)S(1)}, s32[9,8,1024]{2,1,0:T(8,128)}, u32[]{:S(2)}, u32[]{:S(2)}) collective-permute-start(s32[9,8,1024]{2,1,0:T(8,128)S(1)} %collective-permute-done.2.refs_3_), channel_id=1, source_target_pairs={{0,1},{1,0},{2,3},{3,2},{4,5},{5,4},{6,7},{7,6},{8,9},{9,8},{10,11... | collective-permute-start | bytes 884744 | tf_op jit(solution)/shard_map/ppermute | solution.py:280
  39.2 3.4 %collective-permute-start.5 = (s32[9,8,1024]{2,1,0:T(8,128)S(1)}, s32[9,8,1024]{2,1,0:T(8,128)}, u32[]{:S(2)}, u32[]{:S(2)}) collective-permute-start(s32[9,8,1024]{2,1,0:T(8,128)S(1)} %collective-permute-done.1.refs_2_), channel_id=1, source_target_pairs={{0,1},{1,0},{2,3},{3,2},{4,5},{5,4},{6,7},{7,6},{8,9},{9,8},{10,11... | collective-permute-start | bytes 884744 | tf_op jit(solution)/shard_map/ppermute | solution.py:280
  40.0 2.8 %collective-permute-start.4 = (s32[9,8,1024]{2,1,0:T(8,128)}, s32[9,8,1024]{2,1,0:T(8,128)}, u32[]{:S(2)}, u32[]{:S(2)}) collective-permute-start(s32[9,8,1024]{2,1,0:T(8,128)} %collective-permute-done.refs_1_), channel_id=1, source_target_pairs={{0,1},{1,0},{2,3},{3,2},{4,5},{5,4},{6,7},{7,6},{8,9},{9,8},{10,11... | collective-permute-start | bytes 884744 | tf_op jit(solution)/shard_map/ppermute | solution.py:280
  40.5 26.8 %collective-permute-start.20 = (bf16[256,768]{1,0:T(8,128)(2,1)S(1)}, bf16[256,768]{1,0:T(8,128)(2,1)S(1)}, u32[]{:S(2)}, u32[]{:S(2)}) collective-permute-start(bf16[256,768]{1,0:T(8,128)(2,1)S(1)} %fusion.2.refs_8_), channel_id=1, source_target_pairs={{0,1},{1,0},{2,3},{3,2},{4,5},{5,4},{6,7},{7,6},{8,9},{9,8},{10,11... | collective-permute-start | bytes 1179656 | tf_op jit(solution)/shard_map/ppermute | solution.py:280
  42.2 27.8 %collective-permute-start.23 = (bf16[256,768]{1,0:T(8,128)(2,1)S(1)}, bf16[256,768]{1,0:T(8,128)(2,1)S(1)}, u32[]{:S(2)}, u32[]{:S(2)}) collective-permute-start(bf16[256,768]{1,0:T(8,128)(2,1)S(1)} %collective-permute-done.19.refs_11_), channel_id=1, source_target_pairs={{0,1},{1,0},{2,3},{3,2},{4,5},{5,4},{6,7},{7,6},{8,9},{9,8},{10,11... | collective-permute-start | bytes 1179656 | tf_op jit(solution)/shard_map/ppermute | solution.py:280
  42.2 27.8 %collective-permute-start.22 = (bf16[256,768]{1,0:T(8,128)(2,1)S(1)}, bf16[256,768]{1,0:T(8,128)(2,1)S(1)}, u32[]{:S(2)}, u32[]{:S(2)}) collective-permute-start(bf16[256,768]{1,0:T(8,128)(2,1)S(1)} %collective-permute-done.18.refs_10_), channel_id=1, source_target_pairs={{0,1},{1,0},{2,3},{3,2},{4,5},{5,4},{6,7},{7,6},{8,9},{9,8},{10,11... | collective-permute-start | bytes 1179656 | tf_op jit(solution)/shard_map/ppermute | solution.py:280
  42.7 27.8 %collective-permute-start.21 = (bf16[256,768]{1,0:T(8,128)(2,1)S(1)}, bf16[256,768]{1,0:T(8,128)(2,1)S(1)}, u32[]{:S(2)}, u32[]{:S(2)}) collective-permute-start(bf16[256,768]{1,0:T(8,128)(2,1)S(1)} %collective-permute-done.17.refs_9_), channel_id=1, source_target_pairs={{0,1},{1,0},{2,3},{3,2},{4,5},{5,4},{6,7},{7,6},{8,9},{9,8},{10,11... | collective-permute-start | bytes 1179656 | tf_op jit(solution)/shard_map/ppermute | solution.py:280
  42.8 1.0 copy-start.1
  43.7 2.1 %copy-start.2 = (bf16[768,2560]{1,0:T(8,128)(2,1)S(1)}, bf16[768,2560]{1,0:T(8,128)(2,1)}, u32[]{:S(2)}) copy-start(bf16[768,2560]{1,0:T(8,128)(2,1)} %refs_9_.1) | copy-start | bytes 11796484
  45.8 1.2 copy-start.3
  47.1 1.0 copy-start.5
  48.0 1.0 copy-start.7
  49.0 1.0 copy-start.9
  66.9 11.3 %collective-permute-start.7 = (bf16[320,256]{1,0:T(8,128)(2,1)S(1)}, bf16[320,256]{1,0:T(8,128)(2,1)S(1)}, u32[]{:S(2)}, u32[]{:S(2)}) collective-permute-start(bf16[320,256]{1,0:T(8,128)(2,1)S(1)} %get-tuple-element.13), channel_id=1, source_target_pairs={{0,32},{8,40},{16,48},{24,56},{32,64},{40,72},{48,80},{56,88},{64,... | collective-permute-start | bytes 491528 | tf_op jit(solution)/shard_map/ppermute | solution.py:283
  67.4 10.9 %collective-permute-start.8 = (bf16[320,256]{1,0:T(8,128)(2,1)S(1)}, bf16[320,256]{1,0:T(8,128)(2,1)S(1)}, u32[]{:S(2)}, u32[]{:S(2)}) collective-permute-start(bf16[320,256]{1,0:T(8,128)(2,1)S(1)} %get-tuple-element.14), channel_id=1, source_target_pairs={{0,64},{8,72},{16,80},{24,88},{32,96},{40,104},{48,112},{56,120},{... | collective-permute-start | bytes 491528 | tf_op jit(solution)/shard_map/ppermute | solution.py:283
  69.9 8.3 %collective-permute-start.11 = (bf16[320,256]{1,0:T(8,128)(2,1)S(1)}, bf16[320,256]{1,0:T(8,128)(2,1)S(1)}, u32[]{:S(2)}, u32[]{:S(2)}) collective-permute-start(bf16[320,256]{1,0:T(8,128)(2,1)S(1)} %get-tuple-element.17), channel_id=1, source_target_pairs={{0,1},{1,0},{2,3},{3,2},{4,5},{5,4},{6,7},{7,6},{8,9},{9,8},{10,11... | collective-permute-start | bytes 491528 | tf_op jit(solution)/shard_map/ppermute | solution.py:280
  69.9 10.6 %collective-permute-start.13 = (bf16[320,256]{1,0:T(8,128)(2,1)S(1)}, bf16[320,256]{1,0:T(8,128)(2,1)S(1)}, u32[]{:S(2)}, u32[]{:S(2)}) collective-permute-start(bf16[320,256]{1,0:T(8,128)(2,1)S(1)} %get-tuple-element.18), channel_id=1, source_target_pairs={{0,1},{1,0},{2,3},{3,2},{4,5},{5,4},{6,7},{7,6},{8,9},{9,8},{10,11... | collective-permute-start | bytes 491528 | tf_op jit(solution)/shard_map/ppermute | solution.py:280
  70.4 10.1 %collective-permute-start.15 = (bf16[320,256]{1,0:T(8,128)(2,1)S(1)}, bf16[320,256]{1,0:T(8,128)(2,1)S(1)}, u32[]{:S(2)}, u32[]{:S(2)}) collective-permute-start(bf16[320,256]{1,0:T(8,128)(2,1)S(1)} %get-tuple-element.19), channel_id=1, source_target_pairs={{0,1},{1,0},{2,3},{3,2},{4,5},{5,4},{6,7},{7,6},{8,9},{9,8},{10,11... | collective-permute-start | bytes 491528 | tf_op jit(solution)/shard_map/ppermute | solution.py:280
  78.2 5.7 %collective-permute-start.9 = (bf16[320,256]{1,0:T(8,128)(2,1)S(1)}, bf16[320,256]{1,0:T(8,128)(2,1)S(1)}, u32[]{:S(2)}, u32[]{:S(2)}) collective-permute-start(bf16[320,256]{1,0:T(8,128)(2,1)S(1)} %get-tuple-element.15), channel_id=1, source_target_pairs={{0,96},{8,104},{16,112},{24,120},{32,0},{40,8},{48,16},{56,24},{64... | collective-permute-start | bytes 491528 | tf_op jit(solution)/shard_map/ppermute | solution.py:283
  78.2 5.7 %collective-permute-start.10 = (bf16[320,256]{1,0:T(8,128)(2,1)S(1)}, bf16[320,256]{1,0:T(8,128)(2,1)S(1)}, u32[]{:S(2)}, u32[]{:S(2)}) collective-permute-start(bf16[320,256]{1,0:T(8,128)(2,1)S(1)} %get-tuple-element.16), channel_id=1, source_target_pairs={{0,1},{1,0},{2,3},{3,2},{4,5},{5,4},{6,7},{7,6},{8,9},{9,8},{10,11... | collective-permute-start | bytes 491528 | tf_op jit(solution)/shard_map/ppermute | solution.py:280
  78.2 11.3 %collective-permute-start.12 = (bf16[320,256]{1,0:T(8,128)(2,1)S(1)}, bf16[320,256]{1,0:T(8,128)(2,1)S(1)}, u32[]{:S(2)}, u32[]{:S(2)}) collective-permute-start(bf16[320,256]{1,0:T(8,128)(2,1)S(1)} %collective-permute-done.11), channel_id=1, source_target_pairs={{0,32},{8,40},{16,48},{24,56},{32,64},{40,72},{48,80},{56,88},{64,... | collective-permute-start | bytes 491528 | tf_op jit(solution)/shard_map/ppermute | solution.py:283
  80.5 9.1 %collective-permute-start.14 = (bf16[320,256]{1,0:T(8,128)(2,1)S(1)}, bf16[320,256]{1,0:T(8,128)(2,1)S(1)}, u32[]{:S(2)}, u32[]{:S(2)}) collective-permute-start(bf16[320,256]{1,0:T(8,128)(2,1)S(1)} %collective-permute-done.13), channel_id=1, source_target_pairs={{0,64},{8,72},{16,80},{24,88},{32,96},{40,104},{48,112},{56,120},{... | collective-permute-start | bytes 491528 | tf_op jit(solution)/shard_map/ppermute | solution.py:283
  80.5 10.1 %collective-permute-start.16 = (bf16[320,256]{1,0:T(8,128)(2,1)S(1)}, bf16[320,256]{1,0:T(8,128)(2,1)S(1)}, u32[]{:S(2)}, u32[]{:S(2)}) collective-permute-start(bf16[320,256]{1,0:T(8,128)(2,1)S(1)} %collective-permute-done.15), channel_id=1, source_target_pairs={{0,96},{8,104},{16,112},{24,120},{32,0},{40,8},{48,16},{56,24},{64... | collective-permute-start | bytes 491528 | tf_op jit(solution)/shard_map/ppermute | solution.py:283
  (3 other events, 2.2 us)
Sparse Core Ops, SparseCore 0:
  9.7 30.0 all-gather.1

commit v2 on v1

--- a/solution.py
+++ b/solution.py
@@ -1,3 +1,5 @@
+import functools
+
 import jax
 import jax.numpy as jnp
 from jax import lax
@@ -21,9 +23,11 @@
 NO_EDGE = RELS * POOL
 TILE = 256
 PLANES = 10
-SLICE = COLS // 8
+HALF = COLS // 2
 ROWS_OUT = 6
 LANES = 128
+CHUNK = 64
+DEVICES = 128
 
 
 def edge_kernel(valid_ref, rel_ref, ids_ref, nbr_ref, out_ref):
@@ -128,31 +132,35 @@
     return jnp.concatenate(rows, axis=0).astype(BF16)
 
 
-def hidden_kernel(place_ref, *refs):
-    edges = refs[:8]
-    grads_ref, weight_ref = refs[8:10]
-    source_ref = refs[10]
-    pieces = refs[11:19]
-    planes_ref, keys, meta, weight_vmem, adj, hidden, meta_sems, weight_sem = refs[19:]
-    mine, x, core = place_ref[0], place_ref[1], place_ref[2]
-    fetch = pltpu.make_async_copy(weight_ref, weight_vmem, weight_sem)
-    fetch.start()
+def count_kernel(n, first, place_ref, *refs):
+    edges = refs[:n]
+    at = n if first else n + 1
+    planes_ref, words, keys, meta, meta_sems, word_sems = refs[at:]
+    if first:
+        planes_ref[...] = jnp.zeros_like(planes_ref)
+    else:
+        planes_ref[...] = refs[n][...]
+    mine = place_ref[0]
     metas = [
         pltpu.make_async_copy(edges[i].at[BLKS, :, pl.ds(0, LANES)], meta.at[i], meta_sems.at[i])
-        for i in range(8)
+        for i in range(n)
     ]
-    for copy in metas:
-        copy.start()
-    planes_ref[...] = jnp.zeros_like(planes_ref)
+    loads = [
+        pltpu.make_async_copy(edges[i].at[pl.ds(0, BLKS)], words.at[i], word_sems.at[i])
+        for i in range(n)
+    ]
+    for m, w in zip(metas, loads):
+        m.start()
+        w.start()
     row = lax.broadcasted_iota(I32, (8, TILE), 0)
-    for copy in metas:
-        copy.wait()
-    for i in range(8):
+    for i in range(n):
+        metas[i].wait()
+        loads[i].wait()
 
         def one_block(b, carry, i=i):
             rel = meta[i, b, 0]
             tiles = meta[i, b, 1]
-            word = edges[i][b]
+            word = words[i, b]
             for half, code in enumerate((word & 0xFFFF, word >> 16)):
                 keys[half, 0] = code >> 5
                 keys[half, 1] = jnp.left_shift(jnp.int32(1), code & 31)
@@ -174,8 +182,38 @@
             return lax.fori_loop(0, tiles, one_tile, carry)
 
         lax.fori_loop(0, BLKS, one_block, 0)
-    fetch.wait()
-    total = None
+
+
+def count_edges(place, edges, planes=None):
+    n = len(edges)
+    vmem = pl.BlockSpec(memory_space=pltpu.VMEM)
+    anywhere = pl.BlockSpec(memory_space=pl.ANY)
+    first = planes is None
+    return pl.pallas_call(
+        functools.partial(count_kernel, n, first),
+        out_shape=jax.ShapeDtypeStruct((RELS, PLANES, 8, TGT), I32),
+        in_specs=[pl.BlockSpec(memory_space=pltpu.SMEM)]
+        + [anywhere] * n
+        + ([] if first else [vmem]),
+        out_specs=vmem,
+        scratch_shapes=[
+            pltpu.VMEM((n, BLKS, 8, TGT), I32),
+            pltpu.VMEM((2, 2, 8, TGT), I32),
+            pltpu.SMEM((n, 8, LANES), I32),
+            pltpu.SemaphoreType.DMA((n,)),
+            pltpu.SemaphoreType.DMA((n,)),
+        ],
+        compiler_params=pltpu.CompilerParams(vmem_limit_bytes=14 << 20),
+        cost_estimate=pl.CostEstimate(
+            flops=n * 1_000_000_000, bytes_accessed=n << 19, transcendentals=0
+        ),
+        name="count_edges",
+    )(place, *edges, *([] if first else [planes]))
+
+
+def hidden_kernel(place_ref, planes_ref, grads_ref, own_ref, other_ref, adj):
+    core = place_ref[1]
+    half = HID // 2
     for r in range(RELS):
 
         def one_part(t, carry, r=r):
@@ -184,94 +222,125 @@
             return carry
 
         lax.fori_loop(0, TGT // LANES, one_part, 0)
-        h = lax.dot_general(
-            adj[...], grads_ref[...], (((1,), (1,)), ((), ())), preferred_element_type=F32
-        )
-        h = (h * (1.0 / FANOUT)).astype(BF16)
-        term = lax.dot_general(
-            h,
-            weight_vmem[:, r * HID : (r + 1) * HID],
-            (((1,), (1,)), ((), ())),
-            preferred_element_type=F32,
-        )
-        total = term if total is None else total + term
-        ht = h.T
-        for q in range(HID // 64):
-            at = r * (HID // 64) + q
-            s, within = at // 5, at % 5
-            pos = (s // 4 ^ core) * 4 + ((s % 4 - x) & 3)
-            start = pl.multiple_of(pos * SLICE + within * 64, 64)
-            hidden[pl.ds(start, 64), :] = ht[q * 64 : (q + 1) * 64, :]
-    source_ref[...] = total.astype(BF16)
-    for i in range(8):
-        pieces[i][...] = hidden[i * SLICE : (i + 1) * SLICE, :]
-
-
-def hidden_parts(place, edges, grads, weight):
+        for out_ref, which in ((other_ref, 1 - core), (own_ref, core)):
+            rows = pl.ds(pl.multiple_of(which * half, half), half)
+            h = lax.dot_general(
+                adj[...], grads_ref[rows, :], (((1,), (1,)), ((), ())), preferred_element_type=F32
+            )
+            out_ref[:, r * half : (r + 1) * half] = (h * (1.0 / FANOUT)).astype(BF16)
+
+
+def hidden_halves(place, planes, grads):
     vmem = pl.BlockSpec(memory_space=pltpu.VMEM)
     return pl.pallas_call(
         hidden_kernel,
-        out_shape=[jax.ShapeDtypeStruct((OWN, D_IN), BF16)]
-        + [jax.ShapeDtypeStruct((SLICE, OWN), BF16)] * 8,
-        in_specs=[pl.BlockSpec(memory_space=pltpu.SMEM)]
-        + [vmem] * 9
-        + [pl.BlockSpec(memory_space=pl.ANY)],
-        out_specs=[vmem] * 9,
-        scratch_shapes=[
-            pltpu.VMEM((RELS, PLANES, 8, TGT), I32),
-            pltpu.VMEM((2, 2, 8, TGT), I32),
-            pltpu.SMEM((8, 8, LANES), I32),
-            pltpu.VMEM((D_IN, COLS), BF16),
-            pltpu.VMEM((OWN, TGT), BF16),
-            pltpu.VMEM((COLS, OWN), BF16),
-            pltpu.SemaphoreType.DMA((8,)),
-            pltpu.SemaphoreType.DMA,
-        ],
-        compiler_params=pltpu.CompilerParams(vmem_limit_bytes=40 << 20),
+        out_shape=[jax.ShapeDtypeStruct((OWN, HALF), BF16)] * 2,
+        in_specs=[pl.BlockSpec(memory_space=pltpu.SMEM), vmem, vmem],
+        out_specs=[vmem] * 2,
+        scratch_shapes=[pltpu.VMEM((OWN, TGT), BF16)],
+        compiler_params=pltpu.CompilerParams(vmem_limit_bytes=16 << 20),
         cost_estimate=pl.CostEstimate(
-            flops=14_000_000_000, bytes_accessed=9 << 20, transcendentals=0
-        ),
-        name="hidden_parts",
-    )(place, *edges, grads, weight)
-
-
-def product_kernel(*refs):
-    hiddens, pools = refs[:8], refs[8:16]
-    out_ref, flat, chunks = refs[16:]
+            flops=4_000_000_000, bytes_accessed=4 << 20, transcendentals=0
+        ),
+        name="hidden_halves",
+    )(place, planes, grads)
+
+
+def source_kernel(place_ref, own_ref, other_ref, weight_ref, out_ref):
+    core = place_ref[1]
+    half = HID // 2
     total = None
-    for i in range(8):
-        term = jnp.dot(hiddens[i][...], pools[i][...], preferred_element_type=F32)
-        total = term if total is None else total + term
+    for r in range(RELS):
+        for h_ref, which in ((own_ref, core), (other_ref, 1 - core)):
+            cols = pl.ds(pl.multiple_of(r * HID + which * half, half), half)
+            term = lax.dot_general(
+                h_ref[:, r * half : (r + 1) * half],
+                weight_ref[:, cols],
+                (((1,), (1,)), ((), ())),
+                preferred_element_type=F32,
+            )
+            total = term if total is None else total + term
+    out_ref[...] = total.astype(BF16)
+
+
+def source_rows(place, own, other, weight):
+    vmem = pl.BlockSpec(memory_space=pltpu.VMEM)
+    return pl.pallas_call(
+        source_kernel,
+        out_shape=jax.ShapeDtypeStruct((OWN, D_IN), BF16),
+        in_specs=[pl.BlockSpec(memory_space=pltpu.SMEM)] + [vmem] * 3,
+        out_specs=vmem,
+        compiler_params=pltpu.CompilerParams(vmem_limit_bytes=16 << 20),
+        cost_estimate=pl.CostEstimate(
+            flops=1_000_000_000, bytes_accessed=6 << 20, transcendentals=0
+        ),
+        name="source_rows",
+    )(place, own, other, weight)
+
+
+def product_kernel(h0_ref, h1_ref, f0_ref, f1_ref, out_ref, chunks):
+    tiles = HALF // LANES
+    chunks[:, ROWS_OUT * tiles :, :] = jnp.zeros((DEVICES, CHUNK - ROWS_OUT * tiles, LANES), F32)
     for r in range(ROWS_OUT):
-        flat[:, r * SLICE : (r + 1) * SLICE] = total[:, r * LANES : (r + 1) * LANES].T
-    for c in range(15):
-        chunks[:, c, :] = flat[:, c * LANES : (c + 1) * LANES]
-    chunks[:, 15, :] = jnp.zeros((LANES, LANES), F32)
+        rows = slice(r * LANES, (r + 1) * LANES)
+        p = jnp.dot(f0_ref[rows, :], h0_ref[...], preferred_element_type=F32)
+        p += jnp.dot(f1_ref[rows, :], h1_ref[...], preferred_element_type=F32)
+        for c in range(tiles):
+            chunks[:, r * tiles + c, :] = p[:, c * LANES : (c + 1) * LANES]
     out_ref[...] = chunks[...].astype(BF16)
 
 
-def products(hiddens, pools):
+def products(h0, h1, f0, f1):
     vmem = pl.BlockSpec(memory_space=pltpu.VMEM)
     return pl.pallas_call(
         product_kernel,
-        out_shape=jax.ShapeDtypeStruct((LANES, 16, LANES), BF16),
-        in_specs=[vmem] * 16,
+        out_shape=jax.ShapeDtypeStruct((DEVICES, CHUNK, LANES), BF16),
+        in_specs=[vmem] * 4,
         out_specs=vmem,
-        scratch_shapes=[
-            pltpu.VMEM((LANES, ROWS_OUT * SLICE), F32),
-            pltpu.VMEM((LANES, 16, LANES), F32),
-        ],
-        compiler_params=pltpu.CompilerParams(vmem_limit_bytes=40 << 20),
+        scratch_shapes=[pltpu.VMEM((DEVICES, CHUNK, LANES), F32)],
+        compiler_params=pltpu.CompilerParams(vmem_limit_bytes=24 << 20),
         cost_estimate=pl.CostEstimate(
             flops=1_000_000_000, bytes_accessed=5 << 20, transcendentals=0
         ),
         name="products",
-    )(*hiddens, *pools)
+    )(h0, h1, f0, f1)
+
+
+def sum_kernel(scale, got_ref, out_ref, sums):
+    tiles = HALF // LANES
+    totals = [None, None]
+    for d in range(DEVICES):
+        term = got_ref[d].astype(F32)
+        core = d % 2
+        totals[core] = term if totals[core] is None else totals[core] + term
+    for core in range(2):
+        sums[core] = totals[core] * scale
+    for r in range(ROWS_OUT):
+        for rel in range(RELS):
+            for core in range(2):
+                for part in range(2):
+                    to = (rel * 4 + core * 2 + part) * LANES
+                    at = r * tiles + rel * 2 + part
+                    out_ref[r : r + 1, to : to + LANES] = sums[core, at : at + 1, :]
+
+
+def sum_chunks(got, scale):
+    vmem = pl.BlockSpec(memory_space=pltpu.VMEM)
+    return pl.pallas_call(
+        functools.partial(sum_kernel, scale),
+        out_shape=jax.ShapeDtypeStruct((ROWS_OUT, COLS), F32),
+        in_specs=[vmem],
+        out_specs=vmem,
+        scratch_shapes=[pltpu.VMEM((2, CHUNK, LANES), F32)],
+        compiler_params=pltpu.CompilerParams(vmem_limit_bytes=14 << 20),
+        cost_estimate=pl.CostEstimate(flops=1 << 20, bytes_accessed=2 << 20, transcendentals=0),
+        name="sum_chunks",
+    )(got)
 
 
 def on_device(grad_out, src_feat, weight, nbr_slot, src_ids, valid_rows, block_rel):
-    dp, rel = lax.axis_index("dp"), lax.axis_index("rel")
-    place = jnp.stack([rel, dp // 4, rel % 2]).astype(I32)
+    rel = lax.axis_index("rel")
+    place = jnp.stack([rel, rel & 1]).astype(I32)
 
     def along_z(v, k):
         return lax.ppermute(v, "rel", [(i, (i + 2 * k) % 8) for i in range(8)])
@@ -279,33 +348,27 @@
     def other_core(v):
         return lax.ppermute(v, "rel", [(i, i ^ 1) for i in range(8)])
 
-    def along_x(v, k):
-        return lax.ppermute(v, "dp", [(i, (i + 4 * k) % 16) for i in range(16)])
-
     grads = lax.all_gather(grad_out.T, "rel", axis=0, tiled=True)
     codes = edge_codes(valid_rows, block_rel, src_ids[0], nbr_slot.transpose(1, 2, 0))
-    mine = [codes] + [along_z(codes, k) for k in (1, 2, 3)]
-    edges = mine + [other_core(v) for v in mine]
+    far = [along_z(codes, k) for k in (2, 1, 3)]
+    near = [codes] + far
+    planes = count_edges(place, near)
+    planes = count_edges(place, [other_core(v) for v in near], planes)
 
     old = jnp.arange(D_IN, dtype=I32)[:, None]
     new = jnp.arange(D_IN, dtype=I32)[None, :]
     order = (old == (new % LANES) * ROWS_OUT + new // LANES).astype(BF16)
-    feats = jnp.dot(src_feat, order, preferred_element_type=F32).astype(BF16)
-    near = [feats] + [along_x(feats, k) for k in (1, 2, 3)]
-    pools = near + [other_core(v) for v in near]
-
-    source_grad, *parts = hidden_parts(place, edges, grads, weight)
-    own = parts[:4]
-    far = [other_core(v) for v in parts[4:]]
-    hiddens = [own[0]] + [along_x(own[k], k) for k in (1, 2, 3)]
-    hiddens += [far[0]] + [along_x(far[k], k) for k in (1, 2, 3)]
-    chunks = products(hiddens, pools)
-    got = lax.all_to_all(chunks, ("dp", "rel"), 0, 0, tiled=True)
-    got = got.reshape(4, 16, 2, 16 * LANES).astype(F32)
-    summed = jnp.sum(got, axis=1)[:, :, : ROWS_OUT * SLICE]
-    summed = summed.reshape(4, 2, ROWS_OUT, SLICE).transpose(2, 1, 0, 3).reshape(ROWS_OUT, COLS)
-    scale = float(TGT * 16) ** (-0.5)
-    return source_grad, summed * scale
+    feats = lax.dot_general(
+        order, src_feat, (((0,), (1,)), ((), ())), preferred_element_type=F32
+    ).astype(BF16)
+    feats_other = other_core(feats)
+
+    own, other = hidden_halves(place, planes, grads)
+    got = other_core(other)
+    source_grad = source_rows(place, own, other, weight)
+    chunks = products(own, got, feats, feats_other)
+    chunks = lax.all_to_all(chunks, ("dp", "rel"), 0, 0, tiled=True)
+    return source_grad, sum_chunks(chunks, float(TGT * 16) ** (-0.5))
 
 
 def solution(mesh):

time: 126 us -> 108 us (0.86)
  blocking collectives: 23.9 us -> 0 us
  waiting for transfers between devices: 32.4 us -> 41.1 us
  starting transfers between devices: 21.1 us -> 18.1 us
  Pallas kernels: 21.7 us -> 24.3 us
  local copies, waits for them, and re-layouts: 10.8 us -> 9.34 us
    all_to_all x0 -> x1, waiting for transfers between devices: none -> 24.9 us  [on_device(): chunks = lax.all_to_all(chunks, ('dp', 'rel'), 0, 0, tiled=True)]
    all_to_all x1 -> x0, blocking collectives: 23.9 us -> none  [on_device(): got = lax.all_to_all(chunks, ('dp', 'rel'), 0, 0, tiled=True)]
    ppermute x9 -> x0, waiting for transfers between devices: 16.6 us -> none  [along_x(): return lax.ppermute(v, 'dp', [(i, (i + 4 * k) % 16) for i in range(16)])]
    ppermute x9 -> x0, starting transfers between devices: 13.9 us -> none  [along_x(): return lax.ppermute(v, 'dp', [(i, (i + 4 * k) % 16) for i in range(16)])]
    all_to_all x0 -> x1, starting transfers between devices: none -> 10.1 us  [on_device(): chunks = lax.all_to_all(chunks, ('dp', 'rel'), 0, 0, tiled=True)]
    pallas_call x2 -> x6, Pallas kernels: 18.9 us -> 21.5 us  [the longest x2 9.97 us: count_edges(): pl.pallas_call(functools.partial(count_kernel, n, first), out_shape=jax.S...]
    ppermute x3, starting transfers between devices: 5.38 us -> 7.2 us  [along_z(): return lax.ppermute(v, 'rel', [(i, (i + 2 * k) % 8) for i in range(8)])]
    ppermute x12 -> x6, waiting for transfers between devices: 0.03 us -> 1.7 us  [other_core(): return lax.ppermute(v, 'rel', [(i, i ^ 1) for i in range(8)])]
  transfers between devices with their start and end apart: 25 -> 11, of which waited for: 7 -> 5; matrix products, arithmetic and copies ran while one was open for 1% -> 1% of each run, Pallas kernels for 16% -> 14%
where the time goes in v2:
time: 108 us
  waiting for transfers between devices  41.1 us (38%)
  Pallas kernels  24.3 us (22%)
  starting transfers between devices  18.1 us (17%)
  between operations  14.2 us (13%)
  local copies, waits for them, and re-layouts  9.34 us (9%)
    all_to_all x1, waiting for transfers between devices, on_device(): chunks = lax.all_to_all(chunks, ('dp', 'rel'), 0, 0, tiled=True)  24.9 us
    ppermute x3, waiting for transfers between devices, along_z(): return lax.ppermute(v, 'rel', [(i, (i + 2 * k) % 8) for i in range(8)])  13.8 us
    all_to_all x1, starting transfers between devices, on_device(): chunks = lax.all_to_all(chunks, ('dp', 'rel'), 0, 0, tiled=True)  10.1 us
    pallas_call x2, Pallas kernels, count_edges(): pl.pallas_call(functools.partial(count_kernel, n, first), out_shape=jax.S...  9.97 us
    unnamed x18, local copies, waits for them, and re-layouts  9.34 us
    ppermute x3, starting transfers between devices, along_z(): return lax.ppermute(v, 'rel', [(i, (i + 2 * k) % 8) for i in range(8)])  7.2 us
    pallas_call x1, Pallas kernels, hidden_halves(): pl.pallas_call(hidden_kernel, out_shape=[jax.ShapeDtypeStruct((OWN, HALF)...  4.9 us
    pallas_call x1, Pallas kernels, products(): pl.pallas_call(product_kernel, out_shape=jax.ShapeDtypeStruct((DEVICES, C...  3.21 us
  transfers between devices with their start and end apart: 11, of which 5 were waited for; matrix products, arithmetic and copies ran while one was open for 1% of the time, Pallas kernels for 14%

profile of v2, /device:TPU:0, one launch (start us, length us, event | category | flops | bytes accessed | tf_op | source)
XLA Modules:
  0.0 107.6 jit_solution(18389700977605129446)
XLA Ops:
  7.2 0.0 copy-start
  7.2 0.0 all-gather.2.cloned.1.call-start
  7.2 0.7 all-gather.2.cloned.1.call-update
  7.9 2.8 %edge_codes.1.refs_0_ = s32[9,8,1024]{2,1,0:T(8,128)} custom-call(s32[1,8]{1,0:T(1,128)} %valid_ref.1, s32[8]{0:T(128)} %rel_ref.1, s32[8,512]{1,0:T(8,128)} %bitcast.8, s32[8,16,1024]{2,1,0:T(8,128)} %bitcast.6), custom_call_target="tpu_custom_call" | custom-call | bytes 1048576 | tf_op jit(solution)/shard_map/edge_codes/pallas_call | solution.py:72
  10.7 4.0 %collective-permute-start.1 = (s32[9,8,1024]{2,1,0:T(8,128)}, s32[9,8,1024]{2,1,0:T(8,128)S(1)}, u32[]{:S(2)}, u32[]{:S(2)}) collective-permute-start(s32[9,8,1024]{2,1,0:T(8,128)} %edge_codes.1.refs_0_), channel_id=1, source_target_pairs={{0,4},{1,5},{2,6},{3,7},{4,0},{5,1},{6,2},{7,3},{8,12},{9,13},{10,... | collective-permute-start | bytes 884744 | tf_op jit(solution)/shard_map/ppermute | solution.py:346
  14.7 1.0 collective-permute-start.3
  15.7 2.2 %collective-permute-start.5 = (s32[9,8,1024]{2,1,0:T(8,128)}, s32[9,8,1024]{2,1,0:T(8,128)S(1)}, u32[]{:S(2)}, u32[]{:S(2)}) collective-permute-start(s32[9,8,1024]{2,1,0:T(8,128)} %edge_codes.1.refs_0_), channel_id=1, source_target_pairs={{0,6},{1,7},{2,0},{3,1},{4,2},{5,3},{6,4},{7,5},{8,14},{9,15},{10,... | collective-permute-start | bytes 884744 | tf_op jit(solution)/shard_map/ppermute | solution.py:346
  17.9 0.0 collective-permute-start
  17.9 0.1 pad_add_fusion.place_ref
  18.0 4.8 %collective-permute-done.1.refs_1_ = s32[9,8,1024]{2,1,0:T(8,128)S(1)} collective-permute-done((s32[9,8,1024]{2,1,0:T(8,128)}, s32[9,8,1024]{2,1,0:T(8,128)S(1)}, u32[]{:S(2)}, u32[]{:S(2)}) %collective-permute-start.1) | collective-permute-done | bytes 294944 | tf_op jit(solution)/shard_map/ppermute | solution.py:346
  22.8 7.6 %collective-permute-done.3.refs_2_ = s32[9,8,1024]{2,1,0:T(8,128)S(1)} collective-permute-done((s32[9,8,1024]{2,1,0:T(8,128)}, s32[9,8,1024]{2,1,0:T(8,128)S(1)}, u32[]{:S(2)}, u32[]{:S(2)}) %collective-permute-start.3) | collective-permute-done | bytes 294944 | tf_op jit(solution)/shard_map/ppermute | solution.py:346
  30.4 1.4 %collective-permute-done.5.refs_3_ = s32[9,8,1024]{2,1,0:T(8,128)S(1)} collective-permute-done((s32[9,8,1024]{2,1,0:T(8,128)}, s32[9,8,1024]{2,1,0:T(8,128)S(1)}, u32[]{:S(2)}, u32[]{:S(2)}) %collective-permute-start.5) | collective-permute-done | bytes 294944 | tf_op jit(solution)/shard_map/ppermute | solution.py:346
  31.8 1.0 copy-done.5
  32.8 5.3 %count_edges.2.refs_4_ = s32[5,10,8,1024]{3,2,1,0:T(8,128)S(1)} custom-call(s32[2]{0:T(128)S(1)} %pad_add_fusion.place_ref, s32[9,8,1024]{2,1,0:T(8,128)S(1)} %copy-done.5, s32[9,8,1024]{2,1,0:T(8,128)S(1)} %collective-permute-done.1.refs_1_, s32[9,8,1024]{2,1,0:T(8,128)S(1)} %collective-permute-done.3.refs_2_, s32[9,8,1024]{2,1,0:T(8,128)S(1)} %collective-permute-done.5.refs_3_), custom_call_target="tpu_custom_call" | custom-call | flops 4000000000 | bytes 2097152 | tf_op jit(solution)/shard_map/count_edges/pallas_call | solution.py:192
  38.1 4.6 %count_edges.3.planes_ref = s32[5,10,8,1024]{3,2,1,0:T(8,128)S(1)} custom-call(s32[2]{0:T(128)S(1)} %pad_add_fusion.place_ref, s32[9,8,1024]{2,1,0:T(8,128)S(1)} %collective-permute-done.refs_0_, s32[9,8,1024]{2,1,0:T(8,128)S(1)} %collective-permute-done.2.refs_1_, s32[9,8,1024]{2,1,0:T(8,128)S(1)} %collective-permute-done.4.refs_2_, ...), custom_call_target="tpu_custom_call" | custom-call | flops 4000000000 | bytes 2097152 | tf_op jit(solution)/shard_map/count_edges/pallas_call | solution.py:192
  42.8 1.2 %copy-done.7 = s32[5,10,8,1024]{3,2,1,0:T(8,128)} copy-done((s32[5,10,8,1024]{3,2,1,0:T(8,128)}, s32[5,10,8,1024]{3,2,1,0:T(8,128)S(1)}, u32[]{:S(2)}) %copy-start.7) | copy-done | bytes 1638424
  44.0 1.2 %copy-done.6 = bf16[512,1024]{1,0:T(8,128)(2,1)S(1)} copy-done((bf16[512,1024]{1,0:T(8,128)(2,1)S(1)}, bf16[512,1024]{1,0:T(8,128)(2,1)}, u32[]{:S(2)}) %copy-start.6) | copy-done | bytes 1048600
  45.2 1.4 %copy-done.8 = s32[5,10,8,1024]{3,2,1,0:T(8,128)S(1)} copy-done((s32[5,10,8,1024]{3,2,1,0:T(8,128)S(1)}, s32[5,10,8,1024]{3,2,1,0:T(8,128)}, u32[]{:S(2)}) %copy-start.8) | copy-done | bytes 1638424
  46.7 4.9 %hidden_halves.1 = (bf16[256,1280]{1,0:T(8,128)(2,1)S(1)}, bf16[256,1280]{1,0:T(8,128)(2,1)S(1)}) custom-call(s32[2]{0:T(128)S(1)} %pad_add_fusion.place_ref, s32[5,10,8,1024]{3,2,1,0:T(8,128)S(1)} %copy-done.8, bf16[512,1024]{1,0:T(8,128)(2,1)S(1)} %copy-done.6), custom_call_target="tpu_custom_call" | custom-call | flops 4000000000 | bytes 4194304 | tf_op jit(solution)/shard_map/hidden_halves/pallas_call | solution.py:235
  51.6 0.6 collective-permute-start.7
  52.2 0.5 convolution_convert_fusion.f0_ref
  52.7 0.1 collective-permute-start.8
  52.8 1.7 %collective-permute-done.8.f1_ref = bf16[768,256]{1,0:T(8,128)(2,1)S(1)} collective-permute-done((bf16[768,256]{1,0:T(8,128)(2,1)S(1)}, bf16[768,256]{1,0:T(8,128)(2,1)S(1)}, u32[]{:S(2)}, u32[]{:S(2)}) %collective-permute-start.8) | collective-permute-done | bytes 393248 | tf_op jit(solution)/shard_map/ppermute | solution.py:349
  54.5 3.2 %products.1 = bf16[128,64,128]{2,1,0:T(8,128)(2,1)S(1)} custom-call(bf16[256,1280]{1,0:T(8,128)(2,1)S(1)} %get-tuple-element.4.own_ref.h0_ref, bf16[256,1280]{1,0:T(8,128)(2,1)S(1)} %collective-permute-done.7.h1_ref, bf16[768,256]{1,0:T(8,128)(2,1)S(1)} %convolution_convert_fusion.f0_ref, bf16[768,256]{1,0:T(8,128)(2,1)S(1)} %collective-permute-done.8.f1_ref), custom_call_target="tpu_custom_call" | custom-call | flops 1000000000 | bytes 5242880 | tf_op jit(solution)/shard_map/products/pallas_call | solution.py:295
  57.7 1.3 %copy-done.1 = bf16[128,64,128]{2,1,0:T(8,128)(2,1)} copy-done((bf16[128,64,128]{2,1,0:T(8,128)(2,1)}, bf16[128,64,128]{2,1,0:T(8,128)(2,1)S(1)}, u32[]{:S(2)}) %copy-start.1) | copy-done | bytes 2097176
  59.1 10.1 %all-to-all-start = ((bf16[128,64,128]{2,1,0:T(8,128)(2,1)}), bf16[128,64,128]{2,1,0:T(8,128)(2,1)S(1)}, u32[]{:S(2)}, u32[]{:S(2)}) async-start(bf16[128,64,128]{2,1,0:T(8,128)(2,1)} %copy-done.1), calls=%async_computation | async-start | bytes 4194304 | tf_op jit(solution)/shard_map/all_to_all | solution.py:370
  69.2 0.0 copy-start.2
  69.2 2.1 %copy-done.2 = bf16[768,2560]{1,0:T(8,128)(2,1)S(1)} copy-done((bf16[768,2560]{1,0:T(8,128)(2,1)S(1)}, bf16[768,2560]{1,0:T(8,128)(2,1)}, u32[]{:S(2)}) %copy-start.2) | copy-done | bytes 3932184
  71.3 1.1 %copy-done.4 = bf16[256,1280]{1,0:T(8,128)(2,1)S(1)} copy-done((bf16[256,1280]{1,0:T(8,128)(2,1)S(1)}, bf16[256,1280]{1,0:T(8,128)(2,1)}, u32[]{:S(2)}) %copy-start.4) | copy-done | bytes 655384
  72.4 2.5 %source_rows.1 = bf16[256,768]{1,0:T(8,128)(2,1)} custom-call(s32[2]{0:T(128)S(1)} %pad_add_fusion.place_ref, bf16[256,1280]{1,0:T(8,128)(2,1)S(1)} %get-tuple-element.4.own_ref.h0_ref, bf16[256,1280]{1,0:T(8,128)(2,1)S(1)} %copy-done.4, bf16[768,2560]{1,0:T(8,128)(2,1)S(1)} %copy-done.2), custom_call_target="tpu_custom_call" | custom-call | flops 1000000000 | bytes 6291456 | tf_op jit(solution)/shard_map/source_rows/pallas_call | solution.py:268
  74.9 24.9 %all-to-all-done.got_ref = bf16[128,64,128]{2,1,0:T(8,128)(2,1)S(1)} async-done(((bf16[128,64,128]{2,1,0:T(8,128)(2,1)}), bf16[128,64,128]{2,1,0:T(8,128)(2,1)S(1)}, u32[]{:S(2)}, u32[]{:S(2)}) %all-to-all-start) | async-done | bytes 2097184 | tf_op jit(solution)/shard_map/all_to_all | solution.py:370
  99.8 1.0 sum_chunks.1
  (19 shorter events, 0.0 us)
Async XLA Ops:
  7.2 45.0 %copy-start = (bf16[256,768]{1,0:T(8,128)(2,1)S(1)}, bf16[256,768]{1,0:T(8,128)(2,1)}, u32[]{:S(2)}) copy-start(bf16[256,768]{1,0:T(8,128)(2,1)} %param.8) | copy-start | bytes 1179652
  7.2 36.8 %all-gather.2.cloned.1.call-start = ((), (), s32[]{:S(2)}) async-start(), calls=%async_computation.1 | async-start | bytes 1179648 | tf_op jit(solution)/shard_map/all_gather | solution.py:351
  10.7 12.0 %collective-permute-start.1 = (s32[9,8,1024]{2,1,0:T(8,128)}, s32[9,8,1024]{2,1,0:T(8,128)S(1)}, u32[]{:S(2)}, u32[]{:S(2)}) collective-permute-start(s32[9,8,1024]{2,1,0:T(8,128)} %edge_codes.1.refs_0_), channel_id=1, source_target_pairs={{0,4},{1,5},{2,6},{3,7},{4,0},{5,1},{6,2},{7,3},{8,12},{9,13},{10,... | collective-permute-start | bytes 884744 | tf_op jit(solution)/shard_map/ppermute | solution.py:346
  14.7 15.7 %collective-permute-start.3 = (s32[9,8,1024]{2,1,0:T(8,128)}, s32[9,8,1024]{2,1,0:T(8,128)S(1)}, u32[]{:S(2)}, u32[]{:S(2)}) collective-permute-start(s32[9,8,1024]{2,1,0:T(8,128)} %edge_codes.1.refs_0_), channel_id=1, source_target_pairs={{0,2},{1,3},{2,4},{3,5},{4,6},{5,7},{6,0},{7,1},{8,10},{9,11},{10,... | collective-permute-start | bytes 884744 | tf_op jit(solution)/shard_map/ppermute | solution.py:346
  15.7 16.1 %collective-permute-start.5 = (s32[9,8,1024]{2,1,0:T(8,128)}, s32[9,8,1024]{2,1,0:T(8,128)S(1)}, u32[]{:S(2)}, u32[]{:S(2)}) collective-permute-start(s32[9,8,1024]{2,1,0:T(8,128)} %edge_codes.1.refs_0_), channel_id=1, source_target_pairs={{0,6},{1,7},{2,0},{3,1},{4,2},{5,3},{6,4},{7,5},{8,14},{9,15},{10,... | collective-permute-start | bytes 884744 | tf_op jit(solution)/shard_map/ppermute | solution.py:346
  17.9 20.2 %collective-permute-start = (s32[9,8,1024]{2,1,0:T(8,128)}, s32[9,8,1024]{2,1,0:T(8,128)S(1)}, u32[]{:S(2)}, u32[]{:S(2)}) collective-permute-start(s32[9,8,1024]{2,1,0:T(8,128)} %edge_codes.1.refs_0_), channel_id=1, source_target_pairs={{0,1},{1,0},{2,3},{3,2},{4,5},{5,4},{6,7},{7,6},{8,9},{9,8},{10,11... | collective-permute-start | bytes 884744 | tf_op jit(solution)/shard_map/ppermute | solution.py:349
  22.8 15.3 %collective-permute-start.2 = (s32[9,8,1024]{2,1,0:T(8,128)S(1)}, s32[9,8,1024]{2,1,0:T(8,128)S(1)}, u32[]{:S(2)}, u32[]{:S(2)}) collective-permute-start(s32[9,8,1024]{2,1,0:T(8,128)S(1)} %collective-permute-done.1.refs_1_), channel_id=1, source_target_pairs={{0,1},{1,0},{2,3},{3,2},{4,5},{5,4},{6,7},{7,6},{8,9},{9,8},{10,11... | collective-permute-start | bytes 884744 | tf_op jit(solution)/shard_map/ppermute | solution.py:349
  30.4 7.7 %collective-permute-start.4 = (s32[9,8,1024]{2,1,0:T(8,128)S(1)}, s32[9,8,1024]{2,1,0:T(8,128)S(1)}, u32[]{:S(2)}, u32[]{:S(2)}) collective-permute-start(s32[9,8,1024]{2,1,0:T(8,128)S(1)} %collective-permute-done.3.refs_2_), channel_id=1, source_target_pairs={{0,1},{1,0},{2,3},{3,2},{4,5},{5,4},{6,7},{7,6},{8,9},{9,8},{10,11... | collective-permute-start | bytes 884744 | tf_op jit(solution)/shard_map/ppermute | solution.py:349
  31.8 6.3 %collective-permute-start.6 = (s32[9,8,1024]{2,1,0:T(8,128)S(1)}, s32[9,8,1024]{2,1,0:T(8,128)S(1)}, u32[]{:S(2)}, u32[]{:S(2)}) collective-permute-start(s32[9,8,1024]{2,1,0:T(8,128)S(1)} %collective-permute-done.5.refs_3_), channel_id=1, source_target_pairs={{0,1},{1,0},{2,3},{3,2},{4,5},{5,4},{6,7},{7,6},{8,9},{9,8},{10,11... | collective-permute-start | bytes 884744 | tf_op jit(solution)/shard_map/ppermute | solution.py:349
  31.8 1.0 copy-start.5
  42.8 1.2 %copy-start.7 = (s32[5,10,8,1024]{3,2,1,0:T(8,128)}, s32[5,10,8,1024]{3,2,1,0:T(8,128)S(1)}, u32[]{:S(2)}) copy-start(s32[5,10,8,1024]{3,2,1,0:T(8,128)S(1)} %count_edges.3.planes_ref) | copy-start | bytes 4915204
  44.0 1.2 %copy-start.6 = (bf16[512,1024]{1,0:T(8,128)(2,1)S(1)}, bf16[512,1024]{1,0:T(8,128)(2,1)}, u32[]{:S(2)}) copy-start(bf16[512,1024]{1,0:T(8,128)(2,1)} %all-gather.2.cloned.1.call-done.grads_ref) | copy-start | bytes 3145732
  45.2 1.4 %copy-start.8 = (s32[5,10,8,1024]{3,2,1,0:T(8,128)S(1)}, s32[5,10,8,1024]{3,2,1,0:T(8,128)}, u32[]{:S(2)}) copy-start(s32[5,10,8,1024]{3,2,1,0:T(8,128)} %copy-done.7) | copy-start | bytes 4915204
  51.6 2.9 %copy-start.3 = (bf16[256,1280]{1,0:T(8,128)(2,1)}, bf16[256,1280]{1,0:T(8,128)(2,1)S(1)}, u32[]{:S(2)}) copy-start(bf16[256,1280]{1,0:T(8,128)(2,1)S(1)} %get-tuple-element.5.other_ref) | copy-start | bytes 1966084
  51.6 2.9 %collective-permute-start.7 = (bf16[256,1280]{1,0:T(8,128)(2,1)S(1)}, bf16[256,1280]{1,0:T(8,128)(2,1)S(1)}, u32[]{:S(2)}, u32[]{:S(2)}) collective-permute-start(bf16[256,1280]{1,0:T(8,128)(2,1)S(1)} %get-tuple-element.5.other_ref), channel_id=1, source_target_pairs={{0,1},{1,0},{2,3},{3,2},{4,5},{5,4},{6,7},{7,6},{8,9},{9,8},{10,11... | collective-permute-start | bytes 1966088 | tf_op jit(solution)/shard_map/ppermute | solution.py:349
  52.7 1.8 %collective-permute-start.8 = (bf16[768,256]{1,0:T(8,128)(2,1)S(1)}, bf16[768,256]{1,0:T(8,128)(2,1)S(1)}, u32[]{:S(2)}, u32[]{:S(2)}) collective-permute-start(bf16[768,256]{1,0:T(8,128)(2,1)S(1)} %convolution_convert_fusion.f0_ref), channel_id=1, source_target_pairs={{0,1},{1,0},{2,3},{3,2},{4,5},{5,4},{6,7},{7,6},{8,9},{9,8},{10,11... | collective-permute-start | bytes 1179656 | tf_op jit(solution)/shard_map/ppermute | solution.py:349
  57.7 1.3 %copy-start.1 = (bf16[128,64,128]{2,1,0:T(8,128)(2,1)}, bf16[128,64,128]{2,1,0:T(8,128)(2,1)S(1)}, u32[]{:S(2)}) copy-start(bf16[128,64,128]{2,1,0:T(8,128)(2,1)S(1)} %products.1) | copy-start | bytes 6291460
  59.1 40.7 %all-to-all-start = ((bf16[128,64,128]{2,1,0:T(8,128)(2,1)}), bf16[128,64,128]{2,1,0:T(8,128)(2,1)S(1)}, u32[]{:S(2)}, u32[]{:S(2)}) async-start(bf16[128,64,128]{2,1,0:T(8,128)(2,1)} %copy-done.1), calls=%async_computation | async-start | bytes 4194304 | tf_op jit(solution)/shard_map/all_to_all | solution.py:370
  69.2 2.1 %copy-start.2 = (bf16[768,2560]{1,0:T(8,128)(2,1)S(1)}, bf16[768,2560]{1,0:T(8,128)(2,1)}, u32[]{:S(2)}) copy-start(bf16[768,2560]{1,0:T(8,128)(2,1)} %weight_ref.1) | copy-start | bytes 11796484
  71.3 1.1 %copy-start.4 = (bf16[256,1280]{1,0:T(8,128)(2,1)S(1)}, bf16[256,1280]{1,0:T(8,128)(2,1)}, u32[]{:S(2)}) copy-start(bf16[256,1280]{1,0:T(8,128)(2,1)} %copy-done.3) | copy-start | bytes 1966084
Sparse Core Ops, SparseCore 0:
  9.7 27.6 all-gather.1

commit v3 on v2

v3 whole, which is shorter than its diff:
```python
import functools

import jax
import jax.numpy as jnp
from jax import lax
from jax.experimental import pallas as pl
from jax.experimental.pallas import tpu as pltpu
from jax.sharding import PartitionSpec as P

I32 = jnp.int32
BF16 = jnp.bfloat16
F32 = jnp.float32
D_IN = 768
HID = 512
RELS = 5
COLS = RELS * HID
FANOUT = 16
SLOTS = 512
TGT = 1024
BLKS = 8
POOL = 2048
OWN = 256
NO_EDGE = RELS * POOL
PLANES = 10
HALF = COLS // 2
ROWS_OUT = 6
LANES = 128
CHUNK = 64
DEVICES = 128
TILES = TGT // LANES
STEP = 2
PIECE = HID // 8
COST_FIRST = 1_000_000_000
COST_COUNT = 20_000_000_000


def edge_kernel(valid_ref, rel_ref, ids_ref, nbr_ref, out_ref):
    lane = lax.broadcasted_iota(I32, (8, LANES), 1)
    sub = lax.broadcasted_iota(I32, (8, LANES), 0)
    meta = jnp.zeros((8, LANES), I32)
    for b in range(BLKS):
        rel = rel_ref[b]
        limit = valid_ref[0, b]
        meta = jnp.where((sub == b) & (lane == 0), rel, meta)
        meta = jnp.where((sub == b) & (lane == 1), (limit + (STEP * LANES - 1)) // (STEP * LANES), meta)
        node = ids_ref[b : b + 1, :]
        code = rel * POOL + (node & 1792) + ((node & 7) << 5) + ((node >> 3) & 31)
        tables = [
            jnp.broadcast_to(code[:, i * LANES : (i + 1) * LANES], (8, LANES))
            for i in range(SLOTS // LANES)
        ]
        for t in range(TGT // LANES):
            cols = slice(t * LANES, (t + 1) * LANES)
            live = (lane + t * LANES) < limit
            halves = []
            for half in range(2):
                slot = nbr_ref[b, half * 8 : (half + 1) * 8, cols]
                low = slot & (LANES - 1)
                high = slot >> 7
                got = [
                    jnp.take_along_axis(table, low, axis=1, mode="promise_in_bounds")
                    for table in tables
                ]
                found = jnp.where(
                    high < 2,
                    jnp.where(high == 0, got[0], got[1]),
                    jnp.where(high == 2, got[2], got[3]),
                )
                halves.append(jnp.where(live, found, NO_EDGE))
            out_ref[b * TILES + t] = halves[0] | (halves[1] << 16)
    out_ref[BLKS * TILES] = meta


def edge_codes(valid_rows, block_rel, ids, nbr):
    return pl.pallas_call(
        edge_kernel,
        out_shape=jax.ShapeDtypeStruct((BLKS * TILES + 1, 8, LANES), I32),
        in_specs=[pl.BlockSpec(memory_space=pltpu.SMEM)] * 2
        + [pl.BlockSpec(memory_space=pltpu.VMEM)] * 2,
        out_specs=pl.BlockSpec(memory_space=pltpu.VMEM),
        cost_estimate=pl.CostEstimate(flops=0, bytes_accessed=1 << 20, transcendentals=0),
        name="edge_codes",
    )(valid_rows, block_rel, ids, nbr)


def full_add(a, b, c):
    x = a ^ b
    return x ^ c, (a & b) | (c & x)


def count_bits(masks, planes):
    carried = masks
    out = []
    for i in range(PLANES):
        cur = carried + [planes[i]]
        carried = []
        while len(cur) >= 3:
            s, c = full_add(cur[0], cur[1], cur[2])
            cur = cur[3:] + [s]
            carried.append(c)
        if len(cur) == 2:
            carried.append(cur[0] & cur[1])
            cur = [cur[0] ^ cur[1]]
        out.append(cur[0])
    return out


def swap_bits(a, b, shift, mask):
    if a is None and b is None:
        return a, b
    if b is None:
        t = lax.shift_right_logical(a, jnp.int32(shift)) & mask
        return a & mask, t
    t = (lax.shift_right_logical(a, jnp.int32(shift)) ^ b) & mask
    return a ^ (t << shift), b ^ t


def plane_bytes(planes):
    x = list(planes)
    for shift, mask in ((4, 0x0F0F0F0F), (2, 0x33333333), (1, 0x55555555)):
        for i in range(8):
            if not i & shift:
                x[i], x[i + shift] = swap_bits(x[i], x[i + shift], shift, mask)
    return x


def counts(planes):
    low = plane_bytes(planes[:8])
    high = plane_bytes(planes[8:] + [None] * (16 - PLANES))
    pair = 0x00FF00FF
    rows = [None] * 32
    for off in range(8):
        even = (low[off] & pair) | ((high[off] & pair) << 8)
        odd = (lax.shift_right_logical(low[off], jnp.int32(8)) & pair) | (high[off] & ~pair)
        for q, word in enumerate((even, odd)):
            rows[off + 8 * q] = (word & 0xFFFF).astype(F32)
            rows[off + 8 * q + 16] = lax.shift_right_logical(word, jnp.int32(16)).astype(F32)
    return jnp.concatenate(rows, axis=0).astype(BF16)


def start_loads(edges, words, meta, word_sems, meta_sems):
    loads = []
    for i, edge in enumerate(edges):
        m = pltpu.make_async_copy(edge.at[BLKS * TILES], meta.at[i], meta_sems.at[i])
        w = pltpu.make_async_copy(edge.at[pl.ds(0, BLKS * TILES)], words.at[i], word_sems.at[i])
        m.start()
        w.start()
        loads.append((m, w))
    return loads


def count_all(mine, loads, words, meta, keys, planes_ref):
    row = lax.broadcasted_iota(I32, (STEP, 8, LANES), 1)
    for i, load in enumerate(loads):
        for copy in load:
            copy.wait()

        def one_block(b, carry, i=i):
            rel = meta[i, b, 0]
            steps = meta[i, b, 1]
            word = words[i, pl.ds(b * TILES, TILES)]
            for half, code in enumerate((word & 0xFFFF, word >> 16)):
                keys[half, 0] = code >> 5
                keys[half, 1] = jnp.left_shift(jnp.int32(1), code & 31)
            target = row + (rel * (POOL // 32) + mine * (OWN // 32))

            def one_step(t, carry):
                at = pl.ds(t * STEP, STEP)
                masks = []
                for half in range(2):
                    for s in range(8):
                        key = jnp.broadcast_to(keys[half, 0, at, s : s + 1, :], target.shape)
                        bit = jnp.broadcast_to(keys[half, 1, at, s : s + 1, :], target.shape)
                        masks.append(jnp.where(key == target, bit, 0))
                new = count_bits(masks, [planes_ref[rel, p, at] for p in range(PLANES)])
                for p in range(PLANES):
                    planes_ref[rel, p, at] = new[p]
                return carry

            return lax.fori_loop(0, steps, one_step, carry)

        lax.fori_loop(0, BLKS, one_block, 0)


PLANE_SHAPE = (RELS, PLANES, TILES, 8, LANES)


def count_scratch(n):
    return [
        pltpu.VMEM((n, BLKS * TILES, 8, LANES), I32),
        pltpu.VMEM((2, 2, TILES, 8, LANES), I32),
        pltpu.SMEM((n, 8, LANES), I32),
        pltpu.SemaphoreType.DMA((n,)),
        pltpu.SemaphoreType.DMA((n,)),
    ]


def first_kernel(n, place_ref, *refs):
    edges, grads = refs[:n], refs[n : n + 4]
    planes_ref, half_ref = refs[n + 4 : n + 6]
    words, keys, meta, word_sems, meta_sems, grad_sems = refs[n + 6 :]
    loads = start_loads(edges, words, meta, word_sems, meta_sems)
    copies = []
    for k in range(4):
        z = (place_ref[0] // 2 - k) & 3
        rows = pl.ds(pl.multiple_of(z * PIECE, PIECE), PIECE)
        copies.append(pltpu.make_async_copy(grads[k], half_ref.at[rows], grad_sems.at[k]))
        copies[k].start()
    planes_ref[...] = jnp.zeros_like(planes_ref)
    count_all(place_ref[0], loads, words, meta, keys, planes_ref)
    for copy in copies:
        copy.wait()


def count_first(place, edges, grads):
    n = len(edges)
    vmem = pl.BlockSpec(memory_space=pltpu.VMEM)
    return pl.pallas_call(
        functools.partial(first_kernel, n),
        out_shape=[
            jax.ShapeDtypeStruct(PLANE_SHAPE, I32),
            jax.ShapeDtypeStruct((HID // 2, TGT), BF16),
        ],
        in_specs=[pl.BlockSpec(memory_space=pltpu.SMEM)]
        + [pl.BlockSpec(memory_space=pl.ANY)] * (n + 4),
        out_specs=[vmem] * 2,
        scratch_shapes=count_scratch(n) + [pltpu.SemaphoreType.DMA((4,))],
        compiler_params=pltpu.CompilerParams(vmem_limit_bytes=14 << 20),
        cost_estimate=pl.CostEstimate(
            flops=COST_FIRST, bytes_accessed=1 << 20, transcendentals=0
        ),
        name="count_first",
    )(place, *edges, *grads)


def count_kernel(n, place_ref, *refs):
    edges = refs[:n]
    start_ref, planes_ref, words, keys, meta, word_sems, meta_sems = refs[n:]
    loads = start_loads(edges, words, meta, word_sems, meta_sems)
    planes_ref[...] = start_ref[...]
    count_all(place_ref[0], loads, words, meta, keys, planes_ref)


def count_edges(place, edges, planes):
    n = len(edges)
    vmem = pl.BlockSpec(memory_space=pltpu.VMEM)
    return pl.pallas_call(
        functools.partial(count_kernel, n),
        out_shape=jax.ShapeDtypeStruct(PLANE_SHAPE, I32),
        in_specs=[pl.BlockSpec(memory_space=pltpu.SMEM)]
        + [pl.BlockSpec(memory_space=pl.ANY)] * n
        + [vmem],
        out_specs=vmem,
        scratch_shapes=count_scratch(n),
        compiler_params=pltpu.CompilerParams(vmem_limit_bytes=14 << 20),
        cost_estimate=pl.CostEstimate(
            flops=COST_COUNT, bytes_accessed=n << 19, transcendentals=0
        ),
        name="count_edges",
    )(place, *edges, planes)


def hidden_kernel(n, place_ref, *refs):
    edges = refs[:n]
    mine_ref, far_ref, start_ref, own_ref, other_ref = refs[n : n + 5]
    words, keys, meta, word_sems, meta_sems, planes_ref, adj = refs[n + 5 :]
    loads = start_loads(edges, words, meta, word_sems, meta_sems)
    planes_ref[...] = start_ref[...]
    count_all(place_ref[0], loads, words, meta, keys, planes_ref)
    half = HID // 2
    for r in range(RELS):
        for t in range(TILES):
            adj[r % 2, :, t * LANES : (t + 1) * LANES] = counts(
                [planes_ref[r, p, t] for p in range(PLANES)]
            )
        for out_ref, grads_ref in ((other_ref, far_ref), (own_ref, mine_ref)):
            h = lax.dot_general(
                adj[r % 2], grads_ref[...], (((1,), (1,)), ((), ())), preferred_element_type=F32
            )
            out_ref[:, r * half : (r + 1) * half] = (h * (1.0 / FANOUT)).astype(BF16)


def hidden_halves(place, edges, mine, far, planes):
    n = len(edges)
    vmem = pl.BlockSpec(memory_space=pltpu.VMEM)
    return pl.pallas_call(
        functools.partial(hidden_kernel, n),
        out_shape=[jax.ShapeDtypeStruct((OWN, HALF), BF16)] * 2,
        in_specs=[pl.BlockSpec(memory_space=pltpu.SMEM)]
        + [pl.BlockSpec(memory_space=pl.ANY)] * n
        + [vmem] * 3,
        out_specs=[vmem] * 2,
        scratch_shapes=count_scratch(n)
        + [pltpu.VMEM(PLANE_SHAPE, I32), pltpu.VMEM((2, OWN, TGT), BF16)],
        compiler_params=pltpu.CompilerParams(vmem_limit_bytes=18 << 20),
        cost_estimate=pl.CostEstimate(
            flops=8_000_000_000, bytes_accessed=4 << 20, transcendentals=0
        ),
        name="hidden_halves",
    )(place, *edges, mine, far, planes)


def weave(low, high, odd):
    lane = lax.broadcasted_iota(I32, low.shape, 1)
    if odd:
        return jnp.where(lane < LANES // 2, pltpu.roll(low, LANES // 2, 1), high)
    return jnp.where(lane < LANES // 2, low, pltpu.roll(high, LANES // 2, 1))


def source_kernel(place_ref, own_ref, other_ref, weight_ref, out_ref, hidden):
    first = place_ref[1] == 0
    for i in range(HALF // LANES):
        cols = slice(i * LANES, (i + 1) * LANES)
        own, other = own_ref[:, cols].astype(F32), other_ref[:, cols].astype(F32)
        low, high = jnp.where(first, own, other), jnp.where(first, other, own)
        for odd in range(2):
            to = (2 * i + odd) * LANES
            hidden[:, to : to + LANES] = weave(low, high, odd).astype(BF16)
    out_ref[...] = lax.dot_general(
        hidden[...], weight_ref[...], (((1,), (1,)), ((), ())), preferred_element_type=F32
    ).astype(BF16)


def source_rows(place, own, other, weight):
    vmem = pl.BlockSpec(memory_space=pltpu.VMEM)
    return pl.pallas_call(
        source_kernel,
        out_shape=jax.ShapeDtypeStruct((OWN, D_IN), BF16),
        in_specs=[pl.BlockSpec(memory_space=pltpu.SMEM)] + [vmem] * 3,
        out_specs=vmem,
        scratch_shapes=[pltpu.VMEM((OWN, COLS), BF16)],
        compiler_params=pltpu.CompilerParams(vmem_limit_bytes=16 << 20),
        cost_estimate=pl.CostEstimate(
            flops=1_000_000_000, bytes_accessed=6 << 20, transcendentals=0
        ),
        name="source_rows",
    )(place, own, other, weight)


def product_kernel(h0_ref, h1_ref, f0_ref, f1_ref, out_ref, chunks, packed, sems):
    tiles = HALF // LANES
    chunks[:, ROWS_OUT * tiles :, :] = jnp.zeros((DEVICES, CHUNK - ROWS_OUT * tiles, LANES), F32)
    for r in range(ROWS_OUT):
        rows = slice(r * LANES, (r + 1) * LANES)
        p = jnp.dot(f0_ref[rows, :], h0_ref[...], preferred_element_type=F32)
        p += jnp.dot(f1_ref[rows, :], h1_ref[...], preferred_element_type=F32)
        for c in range(tiles):
            chunks[:, r * tiles + c, :] = p[:, c * LANES : (c + 1) * LANES]
    step = DEVICES // 4
    copies = []
    for i in range(4):
        part = pl.ds(i * step, step)
        packed[part] = chunks[part].astype(BF16)
        copies.append(pltpu.make_async_copy(packed.at[part], out_ref.at[part], sems.at[i]))
        copies[i].start()
    for copy in copies:
        copy.wait()


def products(h0, h1, f0, f1):
    vmem = pl.BlockSpec(memory_space=pltpu.VMEM)
    return pl.pallas_call(
        product_kernel,
        out_shape=jax.ShapeDtypeStruct((DEVICES, CHUNK, LANES), BF16),
        in_specs=[vmem] * 4,
        out_specs=pl.BlockSpec(memory_space=pltpu.HBM),
        scratch_shapes=[
            pltpu.VMEM((DEVICES, CHUNK, LANES), F32),
            pltpu.VMEM((DEVICES, CHUNK, LANES), BF16),
            pltpu.SemaphoreType.DMA((4,)),
        ],
        compiler_params=pltpu.CompilerParams(vmem_limit_bytes=24 << 20),
        cost_estimate=pl.CostEstimate(
            flops=1_000_000_000, bytes_accessed=5 << 20, transcendentals=0
        ),
        name="products",
    )(h0, h1, f0, f1)


def sum_kernel(scale, got_ref, out_ref, sums):
    tiles = HALF // LANES
    totals = [None, None]
    for d in range(DEVICES):
        term = got_ref[d].astype(F32)
        core = d % 2
        totals[core] = term if totals[core] is None else totals[core] + term
    for odd in range(2):
        sums[odd] = weave(totals[0] * scale, totals[1] * scale, odd)
    for r in range(ROWS_OUT):
        for i in range(tiles):
            for odd in range(2):
                to = (2 * i + odd) * LANES
                at = r * tiles + i
                out_ref[r : r + 1, to : to + LANES] = sums[odd, at : at + 1, :]


def sum_chunks(got, scale):
    vmem = pl.BlockSpec(memory_space=pltpu.VMEM)
    return pl.pallas_call(
        functools.partial(sum_kernel, scale),
        out_shape=jax.ShapeDtypeStruct((ROWS_OUT, COLS), F32),
        in_specs=[vmem],
        out_specs=vmem,
        scratch_shapes=[pltpu.VMEM((2, CHUNK, LANES), F32)],
        compiler_params=pltpu.CompilerParams(vmem_limit_bytes=14 << 20),
        cost_estimate=pl.CostEstimate(flops=1 << 20, bytes_accessed=2 << 20, transcendentals=0),
        name="sum_chunks",
    )(got)


def on_device(grad_out, src_feat, weight, nbr_slot, src_ids, valid_rows, block_rel):
    rel = lax.axis_index("rel")
    place = jnp.stack([rel, rel & 1]).astype(I32)

    def along_z(v, k):
        return lax.ppermute(v, "rel", [(i, (i + 2 * k) % 8) for i in range(8)])

    def other_core(v):
        return lax.ppermute(v, "rel", [(i, i ^ 1) for i in range(8)])

    codes = edge_codes(valid_rows, block_rel, src_ids[0], nbr_slot.transpose(1, 2, 0))
    far = {k: along_z(codes, k) for k in (2, 1, 3)}
    grads = [grad_out.T]
    grads += [along_z(grads[0], k) for k in (1, 2, 3)]
    planes, mine = count_first(place, [codes, other_core(codes)], grads)
    planes = count_edges(place, [far[k] for k in (2, 1, 3)], planes)

    old = jnp.arange(D_IN, dtype=I32)[:, None]
    new = jnp.arange(D_IN, dtype=I32)[None, :]
    order = (old == (new % LANES) * ROWS_OUT + new // LANES).astype(BF16)
    feats = lax.dot_general(
        order, src_feat, (((0,), (1,)), ((), ())), preferred_element_type=F32
    ).astype(BF16)
    feats_other = other_core(feats)

    swapped = [other_core(far[k]) for k in (2, 1, 3)]
    own, other = hidden_halves(place, swapped, mine, other_core(mine), planes)
    got = other_core(other)
    source_grad = source_rows(place, own, other, weight)
    chunks = products(own, got, feats, feats_other)
    chunks = lax.all_to_all(chunks, ("dp", "rel"), 0, 0, tiled=True)
    return source_grad, sum_chunks(chunks, float(TGT * 16) ** (-0.5))


def solution(mesh):
    return jax.shard_map(
        on_device,
        mesh=mesh,
        in_specs=(
            P("dp", "rel"),
            P(("dp", "rel"), None),
            P(),
            P("dp", "rel", None),
            P("dp", "rel", None),
            P("dp", "rel"),
            P("rel"),
        ),
        out_specs=(P(("dp", "rel"), None), P(("dp", "rel"), None)),
        check_vma=False,
    )
```

time: 108 us -> 94.3 us (0.87)
  between operations: 14.2 us -> 0.77 us
  starting transfers between devices: 18.1 us -> 23.1 us
  local copies, waits for them, and re-layouts: 9.34 us -> 6.38 us
  waiting for transfers between devices: 41.1 us -> 38.2 us
    ppermute x3 -> x6, starting transfers between devices: 7.2 us -> 11.2 us  [along_z(): return lax.ppermute(v, 'rel', [(i, (i + 2 * k) % 8) for i in range(8)])]
    unnamed x18 -> x14, local copies, waits for them, and re-layouts: 9.34 us -> 6.38 us
    ppermute x3 -> x6, waiting for transfers between devices: 13.8 us -> 12.2 us  [along_z(): return lax.ppermute(v, 'rel', [(i, (i + 2 * k) % 8) for i in range(8)])]
    ppermute x6 -> x7, starting transfers between devices: 0.71 us -> 1.94 us  [other_core(): return lax.ppermute(v, 'rel', [(i, i ^ 1) for i in range(8)])]
  transfers between devices with their start and end apart: 11 -> 14, of which waited for: 5 -> 4; matrix products, arithmetic and copies ran while one was open for 1% -> 1% of each run, Pallas kernels for 14% -> 14%
where the time goes in v3:
time: 94.3 us; the launch traced here: 93.6 us
  waiting for transfers between devices  38.2 us (41%)
  Pallas kernels  24.5 us (26%)
  starting transfers between devices  23.1 us (24%)
  local copies, waits for them, and re-layouts  6.38 us (7%)
    all_to_all x1, waiting for transfers between devices, on_device(): chunks = lax.all_to_all(chunks, ('dp', 'rel'), 0, 0, tiled=True)  24.7 us
    ppermute x6, waiting for transfers between devices, along_z(): return lax.ppermute(v, 'rel', [(i, (i + 2 * k) % 8) for i in range(8)])  12.2 us
    ppermute x6, starting transfers between devices, along_z(): return lax.ppermute(v, 'rel', [(i, (i + 2 * k) % 8) for i in range(8)])  11.2 us
    all_to_all x1, starting transfers between devices, on_device(): chunks = lax.all_to_all(chunks, ('dp', 'rel'), 0, 0, tiled=True)  9.98 us
    pallas_call x1, Pallas kernels, hidden_halves(): pl.pallas_call(functools.partial(hidden_kernel, n), out_shape=[jax.ShapeD...  7.1 us
    unnamed x14, local copies, waits for them, and re-layouts  6.38 us
    pallas_call x1, Pallas kernels, count_edges(): pl.pallas_call(functools.partial(count_kernel, n), out_shape=jax.ShapeDty...  4.12 us
    pallas_call x1, Pallas kernels, count_first(): pl.pallas_call(functools.partial(first_kernel, n), out_shape=[jax.ShapeDt...  3.4 us
  transfers between devices with their start and end apart: 14, of which 4 were waited for; matrix products, arithmetic and copies ran while one was open for 1% of the time, Pallas kernels for 14%

profile of v3, /device:TPU:0, one launch (start us, length us, event | category | flops | bytes accessed | tf_op | source)
XLA Modules:
  0.0 93.6 jit_solution(7183973635064088463)
XLA Ops:
  0.6 0.0 copy-start
  0.6 2.1 %collective-permute-start.7 = (bf16[64,1024]{1,0:T(8,128)(2,1)}, bf16[64,1024]{1,0:T(8,128)(2,1)S(1)}, u32[]{:S(2)}, u32[]{:S(2)}) collective-permute-start(bf16[64,1024]{1,0:T(8,128)(2,1)} %bitcast.6), channel_id=1, source_target_pairs={{0,2},{1,3},{2,4},{3,5},{4,6},{5,7},{6,0},{7,1},{8,10},{9,11},{10,... | collective-permute-start | bytes 393224 | tf_op jit(solution)/shard_map/ppermute | solution.py:416
  2.7 2.8 %edge_codes.1.refs_0_ = s32[65,8,128]{2,1,0:T(8,128)} custom-call(s32[1,8]{1,0:T(1,128)} %valid_ref.1, s32[8]{0:T(128)} %rel_ref.1, s32[8,512]{1,0:T(8,128)} %bitcast.11, s32[8,16,1024]{2,1,0:T(8,128)} %bitcast.10), custom_call_target="tpu_custom_call" | custom-call | bytes 1048576 | tf_op jit(solution)/shard_map/edge_codes/pallas_call | solution.py:75
  5.5 3.6 %collective-permute-start.8 = (bf16[64,1024]{1,0:T(8,128)(2,1)}, bf16[64,1024]{1,0:T(8,128)(2,1)S(1)}, u32[]{:S(2)}, u32[]{:S(2)}) collective-permute-start(bf16[64,1024]{1,0:T(8,128)(2,1)} %bitcast.7), channel_id=1, source_target_pairs={{0,4},{1,5},{2,6},{3,7},{4,0},{5,1},{6,2},{7,3},{8,12},{9,13},{10,... | collective-permute-start | bytes 393224 | tf_op jit(solution)/shard_map/ppermute | solution.py:416
  9.1 0.1 collective-permute-start
  9.2 1.8 %collective-permute-start.2 = (s32[65,8,128]{2,1,0:T(8,128)}, s32[65,8,128]{2,1,0:T(8,128)S(1)}, u32[]{:S(2)}, u32[]{:S(2)}) collective-permute-start(s32[65,8,128]{2,1,0:T(8,128)} %edge_codes.1.refs_0_), channel_id=1, source_target_pairs={{0,2},{1,3},{2,4},{3,5},{4,6},{5,7},{6,0},{7,1},{8,10},{9,11},{10,... | collective-permute-start | bytes 798728 | tf_op jit(solution)/shard_map/ppermute | solution.py:416
  11.0 1.5 %collective-permute-start.4 = (s32[65,8,128]{2,1,0:T(8,128)}, s32[65,8,128]{2,1,0:T(8,128)S(1)}, u32[]{:S(2)}, u32[]{:S(2)}) collective-permute-start(s32[65,8,128]{2,1,0:T(8,128)} %edge_codes.1.refs_0_), channel_id=1, source_target_pairs={{0,6},{1,7},{2,0},{3,1},{4,2},{5,3},{6,4},{7,5},{8,14},{9,15},{10,... | collective-permute-start | bytes 798728 | tf_op jit(solution)/shard_map/ppermute | solution.py:416
  12.4 1.1 %collective-permute-done.8.refs_4_ = bf16[64,1024]{1,0:T(8,128)(2,1)S(1)} collective-permute-done((bf16[64,1024]{1,0:T(8,128)(2,1)}, bf16[64,1024]{1,0:T(8,128)(2,1)S(1)}, u32[]{:S(2)}, u32[]{:S(2)}) %collective-permute-start.8) | collective-permute-done | bytes 131104 | tf_op jit(solution)/shard_map/ppermute | solution.py:416
  13.5 2.2 %collective-permute-start.9 = (bf16[64,1024]{1,0:T(8,128)(2,1)}, bf16[64,1024]{1,0:T(8,128)(2,1)S(1)}, u32[]{:S(2)}, u32[]{:S(2)}) collective-permute-start(bf16[64,1024]{1,0:T(8,128)(2,1)} %bitcast.8), channel_id=1, source_target_pairs={{0,6},{1,7},{2,0},{3,1},{4,2},{5,3},{6,4},{7,5},{8,14},{9,15},{10,... | collective-permute-start | bytes 393224 | tf_op jit(solution)/shard_map/ppermute | solution.py:416
  15.7 0.1 pad_add_fusion.place_ref
  15.8 11.1 %collective-permute-done.9.refs_5_ = bf16[64,1024]{1,0:T(8,128)(2,1)S(1)} collective-permute-done((bf16[64,1024]{1,0:T(8,128)(2,1)}, bf16[64,1024]{1,0:T(8,128)(2,1)S(1)}, u32[]{:S(2)}, u32[]{:S(2)}) %collective-permute-start.9) | collective-permute-done | bytes 131104 | tf_op jit(solution)/shard_map/ppermute | solution.py:416
  26.9 1.0 %copy-done.5 = s32[65,8,128]{2,1,0:T(8,128)S(1)} copy-done((s32[65,8,128]{2,1,0:T(8,128)S(1)}, s32[65,8,128]{2,1,0:T(8,128)}, u32[]{:S(2)}) %copy-start.5) | copy-done | bytes 266264
  27.9 0.9 copy-done.6
  28.8 3.4 %count_first.1 = (s32[5,10,8,8,128]{4,3,2,1,0:T(8,128)S(1)}, bf16[256,1024]{1,0:T(8,128)(2,1)S(1)}) custom-call(s32[2]{0:T(128)S(1)} %pad_add_fusion.place_ref, s32[65,8,128]{2,1,0:T(8,128)S(1)} %copy-done.5, s32[65,8,128]{2,1,0:T(8,128)S(1)} %collective-permute-done.6.refs_1_, bf16[64,1024]{1,0:T(8,128)(2,1)S(1)} %bitcast.9, ...), custom_call_target="tpu_custom_call" | custom-call | flops 1000000000 | bytes 1048576 | tf_op jit(solution)/shard_map/count_first/pallas_call | solution.py:218
  32.2 0.1 collective-permute-start.10
  32.3 0.5 collective-permute-start.1
  32.8 0.1 collective-permute-start.3
  32.9 0.4 collective-permute-start.5
  33.3 4.1 %count_edges.1.refs_5_ = s32[5,10,8,8,128]{4,3,2,1,0:T(8,128)S(1)} custom-call(s32[2]{0:T(128)S(1)} %pad_add_fusion.place_ref, s32[65,8,128]{2,1,0:T(8,128)S(1)} %collective-permute-done.refs_0_, s32[65,8,128]{2,1,0:T(8,128)S(1)} %collective-permute-done.2.refs_1_, s32[65,8,128]{2,1,0:T(8,128)S(1)} %collective-permute-done.4.refs_2_, ...), custom_call_target="tpu_custom_call" | custom-call | flops 20000000000 | bytes 1572864 | tf_op jit(solution)/shard_map/count_edges/pallas_call | solution.py:247
  37.4 7.1 %hidden_halves.1 = (bf16[256,1280]{1,0:T(8,128)(2,1)S(1)}, bf16[256,1280]{1,0:T(8,128)(2,1)S(1)}) custom-call(s32[2]{0:T(128)S(1)} %pad_add_fusion.place_ref, s32[65,8,128]{2,1,0:T(8,128)S(1)} %collective-permute-done.1.refs_0_, s32[65,8,128]{2,1,0:T(8,128)S(1)} %collective-permute-done.3.refs_1_, s32[65,8,128]{2,1,0:T(8,128)S(1)} %collective-permute-done.5.refs_2_, ...), custom_call_target="tpu_custom_call" | custom-call | flops 8000000000 | bytes 4194304 | tf_op jit(solution)/shard_map/hidden_halves/pallas_call | solution.py:286
  44.6 0.2 collective-permute-start.11
  44.8 0.5 convolution_convert_fusion.f0_ref
  45.3 0.7 collective-permute-start.12
  45.9 1.3 %collective-permute-done.12.f1_ref = bf16[768,256]{1,0:T(8,128)(2,1)S(1)} collective-permute-done((bf16[768,256]{1,0:T(8,128)(2,1)S(1)}, bf16[768,256]{1,0:T(8,128)(2,1)S(1)}, u32[]{:S(2)}, u32[]{:S(2)}) %collective-permute-start.12) | collective-permute-done | bytes 393248 | tf_op jit(solution)/shard_map/ppermute | solution.py:419
  47.3 3.4 %products.1 = bf16[128,64,128]{2,1,0:T(8,128)(2,1)S(1)} custom-call(bf16[256,1280]{1,0:T(8,128)(2,1)S(1)} %get-tuple-element.8.own_ref.h0_ref, bf16[256,1280]{1,0:T(8,128)(2,1)S(1)} %collective-permute-done.11.h1_ref, bf16[768,256]{1,0:T(8,128)(2,1)S(1)} %convolution_convert_fusion.f0_ref, bf16[768,256]{1,0:T(8,128)(2,1)S(1)} %collective-permute-done.12.f1_ref), custom_call_target="tpu_custom_call" | custom-call | flops 1000000000 | bytes 5242880 | tf_op jit(solution)/shard_map/products/pallas_call | solution.py:362
  50.7 1.3 %copy-done.1 = bf16[128,64,128]{2,1,0:T(8,128)(2,1)} copy-done((bf16[128,64,128]{2,1,0:T(8,128)(2,1)}, bf16[128,64,128]{2,1,0:T(8,128)(2,1)S(1)}, u32[]{:S(2)}) %copy-start.1) | copy-done | bytes 2097176
  52.0 10.0 %all-to-all-start = ((bf16[128,64,128]{2,1,0:T(8,128)(2,1)}), bf16[128,64,128]{2,1,0:T(8,128)(2,1)S(1)}, u32[]{:S(2)}, u32[]{:S(2)}) async-start(bf16[128,64,128]{2,1,0:T(8,128)(2,1)} %copy-done.1), calls=%async_computation | async-start | bytes 4194304 | tf_op jit(solution)/shard_map/all_to_all | solution.py:441
  62.0 2.1 %copy-done.2 = bf16[768,2560]{1,0:T(8,128)(2,1)S(1)} copy-done((bf16[768,2560]{1,0:T(8,128)(2,1)S(1)}, bf16[768,2560]{1,0:T(8,128)(2,1)}, u32[]{:S(2)}) %copy-start.2) | copy-done | bytes 3932184
  64.1 1.1 %copy-done.4 = bf16[256,1280]{1,0:T(8,128)(2,1)S(1)} copy-done((bf16[256,1280]{1,0:T(8,128)(2,1)S(1)}, bf16[256,1280]{1,0:T(8,128)(2,1)}, u32[]{:S(2)}) %copy-start.4) | copy-done | bytes 655384
  65.2 2.7 %source_rows.1 = bf16[256,768]{1,0:T(8,128)(2,1)} custom-call(s32[2]{0:T(128)S(1)} %pad_add_fusion.place_ref, bf16[256,1280]{1,0:T(8,128)(2,1)S(1)} %get-tuple-element.8.own_ref.h0_ref, bf16[256,1280]{1,0:T(8,128)(2,1)S(1)} %copy-done.4, bf16[768,2560]{1,0:T(8,128)(2,1)S(1)} %copy-done.2), custom_call_target="tpu_custom_call" | custom-call | flops 1000000000 | bytes 6291456 | tf_op jit(solution)/shard_map/source_rows/pallas_call | solution.py:326
  67.9 24.7 %all-to-all-done.got_ref = bf16[128,64,128]{2,1,0:T(8,128)(2,1)S(1)} async-done(((bf16[128,64,128]{2,1,0:T(8,128)(2,1)}), bf16[128,64,128]{2,1,0:T(8,128)(2,1)S(1)}, u32[]{:S(2)}, u32[]{:S(2)}) %all-to-all-start) | async-done | bytes 2097184 | tf_op jit(solution)/shard_map/all_to_all | solution.py:441
  92.6 1.0 %sum_chunks.1 = f32[6,2560]{1,0:T(8,128)} custom-call(bf16[128,64,128]{2,1,0:T(8,128)(2,1)S(1)} %all-to-all-done.got_ref), custom_call_target="tpu_custom_call" | custom-call | flops 1048576 | bytes 2097152 | tf_op jit(solution)/shard_map/sum_chunks/pallas_call | solution.py:399
  (20 shorter events, 0.1 us)
Async XLA Ops:
  0.6 44.1 %copy-start = (bf16[256,768]{1,0:T(8,128)(2,1)S(1)}, bf16[256,768]{1,0:T(8,128)(2,1)}, u32[]{:S(2)}) copy-start(bf16[256,768]{1,0:T(8,128)(2,1)} %param.8) | copy-start | bytes 1179652
  0.6 10.3 %collective-permute-start.7 = (bf16[64,1024]{1,0:T(8,128)(2,1)}, bf16[64,1024]{1,0:T(8,128)(2,1)S(1)}, u32[]{:S(2)}, u32[]{:S(2)}) collective-permute-start(bf16[64,1024]{1,0:T(8,128)(2,1)} %bitcast.6), channel_id=1, source_target_pairs={{0,2},{1,3},{2,4},{3,5},{4,6},{5,7},{6,0},{7,1},{8,10},{9,11},{10,... | collective-permute-start | bytes 393224 | tf_op jit(solution)/shard_map/ppermute | solution.py:416
  5.5 21.4 %collective-permute-start.6 = (s32[65,8,128]{2,1,0:T(8,128)}, s32[65,8,128]{2,1,0:T(8,128)S(1)}, u32[]{:S(2)}, u32[]{:S(2)}) collective-permute-start(s32[65,8,128]{2,1,0:T(8,128)} %edge_codes.1.refs_0_), channel_id=1, source_target_pairs={{0,1},{1,0},{2,3},{3,2},{4,5},{5,4},{6,7},{7,6},{8,9},{9,8},{10,11... | collective-permute-start | bytes 798728 | tf_op jit(solution)/shard_map/ppermute | solution.py:419
  5.5 8.0 %collective-permute-start.8 = (bf16[64,1024]{1,0:T(8,128)(2,1)}, bf16[64,1024]{1,0:T(8,128)(2,1)S(1)}, u32[]{:S(2)}, u32[]{:S(2)}) collective-permute-start(bf16[64,1024]{1,0:T(8,128)(2,1)} %bitcast.7), channel_id=1, source_target_pairs={{0,4},{1,5},{2,6},{3,7},{4,0},{5,1},{6,2},{7,3},{8,12},{9,13},{10,... | collective-permute-start | bytes 393224 | tf_op jit(solution)/shard_map/ppermute | solution.py:416
  9.1 23.2 %collective-permute-start = (s32[65,8,128]{2,1,0:T(8,128)}, s32[65,8,128]{2,1,0:T(8,128)S(1)}, u32[]{:S(2)}, u32[]{:S(2)}) collective-permute-start(s32[65,8,128]{2,1,0:T(8,128)} %edge_codes.1.refs_0_), channel_id=1, source_target_pairs={{0,4},{1,5},{2,6},{3,7},{4,0},{5,1},{6,2},{7,3},{8,12},{9,13},{10,... | collective-permute-start | bytes 798728 | tf_op jit(solution)/shard_map/ppermute | solution.py:416
  9.2 23.6 %collective-permute-start.2 = (s32[65,8,128]{2,1,0:T(8,128)}, s32[65,8,128]{2,1,0:T(8,128)S(1)}, u32[]{:S(2)}, u32[]{:S(2)}) collective-permute-start(s32[65,8,128]{2,1,0:T(8,128)} %edge_codes.1.refs_0_), channel_id=1, source_target_pairs={{0,2},{1,3},{2,4},{3,5},{4,6},{5,7},{6,0},{7,1},{8,10},{9,11},{10,... | collective-permute-start | bytes 798728 | tf_op jit(solution)/shard_map/ppermute | solution.py:416
  11.0 21.9 %collective-permute-start.4 = (s32[65,8,128]{2,1,0:T(8,128)}, s32[65,8,128]{2,1,0:T(8,128)S(1)}, u32[]{:S(2)}, u32[]{:S(2)}) collective-permute-start(s32[65,8,128]{2,1,0:T(8,128)} %edge_codes.1.refs_0_), channel_id=1, source_target_pairs={{0,6},{1,7},{2,0},{3,1},{4,2},{5,3},{6,4},{7,5},{8,14},{9,15},{10,... | collective-permute-start | bytes 798728 | tf_op jit(solution)/shard_map/ppermute | solution.py:416
  13.5 13.4 %collective-permute-start.9 = (bf16[64,1024]{1,0:T(8,128)(2,1)}, bf16[64,1024]{1,0:T(8,128)(2,1)S(1)}, u32[]{:S(2)}, u32[]{:S(2)}) collective-permute-start(bf16[64,1024]{1,0:T(8,128)(2,1)} %bitcast.8), channel_id=1, source_target_pairs={{0,6},{1,7},{2,0},{3,1},{4,2},{5,3},{6,4},{7,5},{8,14},{9,15},{10,... | collective-permute-start | bytes 393224 | tf_op jit(solution)/shard_map/ppermute | solution.py:416
  26.9 1.0 %copy-start.5 = (s32[65,8,128]{2,1,0:T(8,128)S(1)}, s32[65,8,128]{2,1,0:T(8,128)}, u32[]{:S(2)}) copy-start(s32[65,8,128]{2,1,0:T(8,128)} %edge_codes.1.refs_0_) | copy-start | bytes 798724
  27.9 0.9 copy-start.6
  32.2 5.3 %collective-permute-start.10 = (bf16[256,1024]{1,0:T(8,128)(2,1)S(1)}, bf16[256,1024]{1,0:T(8,128)(2,1)S(1)}, u32[]{:S(2)}, u32[]{:S(2)}) collective-permute-start(bf16[256,1024]{1,0:T(8,128)(2,1)S(1)} %get-tuple-element.6.refs_3_), channel_id=1, source_target_pairs={{0,1},{1,0},{2,3},{3,2},{4,5},{5,4},{6,7},{7,6},{8,9},{9,8},{10,11... | collective-permute-start | bytes 1572872 | tf_op jit(solution)/shard_map/ppermute | solution.py:419
  32.3 5.1 %collective-permute-start.1 = (s32[65,8,128]{2,1,0:T(8,128)S(1)}, s32[65,8,128]{2,1,0:T(8,128)S(1)}, u32[]{:S(2)}, u32[]{:S(2)}) collective-permute-start(s32[65,8,128]{2,1,0:T(8,128)S(1)} %collective-permute-done.refs_0_), channel_id=1, source_target_pairs={{0,1},{1,0},{2,3},{3,2},{4,5},{5,4},{6,7},{7,6},{8,9},{9,8},{10,11... | collective-permute-start | bytes 798728 | tf_op jit(solution)/shard_map/ppermute | solution.py:419
  32.8 4.7 %collective-permute-start.3 = (s32[65,8,128]{2,1,0:T(8,128)S(1)}, s32[65,8,128]{2,1,0:T(8,128)S(1)}, u32[]{:S(2)}, u32[]{:S(2)}) collective-permute-start(s32[65,8,128]{2,1,0:T(8,128)S(1)} %collective-permute-done.2.refs_1_), channel_id=1, source_target_pairs={{0,1},{1,0},{2,3},{3,2},{4,5},{5,4},{6,7},{7,6},{8,9},{9,8},{10,11... | collective-permute-start | bytes 798728 | tf_op jit(solution)/shard_map/ppermute | solution.py:419
  32.9 4.6 %collective-permute-start.5 = (s32[65,8,128]{2,1,0:T(8,128)S(1)}, s32[65,8,128]{2,1,0:T(8,128)S(1)}, u32[]{:S(2)}, u32[]{:S(2)}) collective-permute-start(s32[65,8,128]{2,1,0:T(8,128)S(1)} %collective-permute-done.4.refs_2_), channel_id=1, source_target_pairs={{0,1},{1,0},{2,3},{3,2},{4,5},{5,4},{6,7},{7,6},{8,9},{9,8},{10,11... | collective-permute-start | bytes 798728 | tf_op jit(solution)/shard_map/ppermute | solution.py:419
  44.5 2.8 %copy-start.3 = (bf16[256,1280]{1,0:T(8,128)(2,1)}, bf16[256,1280]{1,0:T(8,128)(2,1)S(1)}, u32[]{:S(2)}) copy-start(bf16[256,1280]{1,0:T(8,128)(2,1)S(1)} %get-tuple-element.9.other_ref) | copy-start | bytes 1966084
  44.6 2.7 %collective-permute-start.11 = (bf16[256,1280]{1,0:T(8,128)(2,1)S(1)}, bf16[256,1280]{1,0:T(8,128)(2,1)S(1)}, u32[]{:S(2)}, u32[]{:S(2)}) collective-permute-start(bf16[256,1280]{1,0:T(8,128)(2,1)S(1)} %get-tuple-element.9.other_ref), channel_id=1, source_target_pairs={{0,1},{1,0},{2,3},{3,2},{4,5},{5,4},{6,7},{7,6},{8,9},{9,8},{10,11... | collective-permute-start | bytes 1966088 | tf_op jit(solution)/shard_map/ppermute | solution.py:419
  45.3 2.0 %collective-permute-start.12 = (bf16[768,256]{1,0:T(8,128)(2,1)S(1)}, bf16[768,256]{1,0:T(8,128)(2,1)S(1)}, u32[]{:S(2)}, u32[]{:S(2)}) collective-permute-start(bf16[768,256]{1,0:T(8,128)(2,1)S(1)} %convolution_convert_fusion.f0_ref), channel_id=1, source_target_pairs={{0,1},{1,0},{2,3},{3,2},{4,5},{5,4},{6,7},{7,6},{8,9},{9,8},{10,11... | collective-permute-start | bytes 1179656 | tf_op jit(solution)/shard_map/ppermute | solution.py:419
  50.7 1.3 %copy-start.1 = (bf16[128,64,128]{2,1,0:T(8,128)(2,1)}, bf16[128,64,128]{2,1,0:T(8,128)(2,1)S(1)}, u32[]{:S(2)}) copy-start(bf16[128,64,128]{2,1,0:T(8,128)(2,1)S(1)} %products.1) | copy-start | bytes 6291460
  52.0 40.6 %all-to-all-start = ((bf16[128,64,128]{2,1,0:T(8,128)(2,1)}), bf16[128,64,128]{2,1,0:T(8,128)(2,1)S(1)}, u32[]{:S(2)}, u32[]{:S(2)}) async-start(bf16[128,64,128]{2,1,0:T(8,128)(2,1)} %copy-done.1), calls=%async_computation | async-start | bytes 4194304 | tf_op jit(solution)/shard_map/all_to_all | solution.py:441
  62.0 2.1 %copy-start.2 = (bf16[768,2560]{1,0:T(8,128)(2,1)S(1)}, bf16[768,2560]{1,0:T(8,128)(2,1)}, u32[]{:S(2)}) copy-start(bf16[768,2560]{1,0:T(8,128)(2,1)} %weight_ref.1) | copy-start | bytes 11796484
  64.1 1.1 %copy-start.4 = (bf16[256,1280]{1,0:T(8,128)(2,1)S(1)}, bf16[256,1280]{1,0:T(8,128)(2,1)}, u32[]{:S(2)}) copy-start(bf16[256,1280]{1,0:T(8,128)(2,1)} %copy-done.3) | copy-start | bytes 1966084

commit v4 on v3

--- a/solution.py
+++ b/solution.py
@@ -22,16 +22,14 @@
 OWN = 256
 NO_EDGE = RELS * POOL
 PLANES = 10
-HALF = COLS // 2
 ROWS_OUT = 6
 LANES = 128
-CHUNK = 64
-DEVICES = 128
+CHUNK = 120
+PEERS = 64
+PRODUCT_VMEM = 24
 TILES = TGT // LANES
 STEP = 2
 PIECE = HID // 8
-COST_FIRST = 1_000_000_000
-COST_COUNT = 20_000_000_000
 
 
 def edge_kernel(valid_ref, rel_ref, ids_ref, nbr_ref, out_ref):
@@ -195,11 +193,18 @@
     ]
 
 
-def first_kernel(n, place_ref, *refs):
-    edges, grads = refs[:n], refs[n : n + 4]
-    planes_ref, half_ref = refs[n + 4 : n + 6]
-    words, keys, meta, word_sems, meta_sems, grad_sems = refs[n + 6 :]
+def count_kernel(n, place_ref, *refs):
+    edges = refs[:n]
+    planes_ref, words, keys, meta, word_sems, meta_sems = refs[n + 1 :]
     loads = start_loads(edges, words, meta, word_sems, meta_sems)
+    planes_ref[...] = refs[n][...]
+    count_all(place_ref[0], loads, words, meta, keys, planes_ref)
+
+
+def first_kernel(place_ref, edge_ref, *refs):
+    grads = refs[:4]
+    planes_ref, half_ref, words, keys, meta, word_sems, meta_sems, grad_sems = refs[4:]
+    loads = start_loads([edge_ref], words, meta, word_sems, meta_sems)
     copies = []
     for k in range(4):
         z = (place_ref[0] // 2 - k) & 3
@@ -212,33 +217,24 @@
         copy.wait()
 
 
-def count_first(place, edges, grads):
-    n = len(edges)
-    vmem = pl.BlockSpec(memory_space=pltpu.VMEM)
-    return pl.pallas_call(
-        functools.partial(first_kernel, n),
+def count_first(place, edge, grads):
+    vmem = pl.BlockSpec(memory_space=pltpu.VMEM)
+    return pl.pallas_call(
+        first_kernel,
         out_shape=[
             jax.ShapeDtypeStruct(PLANE_SHAPE, I32),
             jax.ShapeDtypeStruct((HID // 2, TGT), BF16),
         ],
         in_specs=[pl.BlockSpec(memory_space=pltpu.SMEM)]
-        + [pl.BlockSpec(memory_space=pl.ANY)] * (n + 4),
+        + [pl.BlockSpec(memory_space=pl.ANY)] * 5,
         out_specs=[vmem] * 2,
-        scratch_shapes=count_scratch(n) + [pltpu.SemaphoreType.DMA((4,))],
+        scratch_shapes=count_scratch(1) + [pltpu.SemaphoreType.DMA((4,))],
         compiler_params=pltpu.CompilerParams(vmem_limit_bytes=14 << 20),
         cost_estimate=pl.CostEstimate(
-            flops=COST_FIRST, bytes_accessed=1 << 20, transcendentals=0
+            flops=2_000_000_000, bytes_accessed=1 << 20, transcendentals=0
         ),
         name="count_first",
-    )(place, *edges, *grads)
-
-
-def count_kernel(n, place_ref, *refs):
-    edges = refs[:n]
-    start_ref, planes_ref, words, keys, meta, word_sems, meta_sems = refs[n:]
-    loads = start_loads(edges, words, meta, word_sems, meta_sems)
-    planes_ref[...] = start_ref[...]
-    count_all(place_ref[0], loads, words, meta, keys, planes_ref)
+    )(place, edge, *grads)
 
 
 def count_edges(place, edges, planes):
@@ -254,122 +250,115 @@
         scratch_shapes=count_scratch(n),
         compiler_params=pltpu.CompilerParams(vmem_limit_bytes=14 << 20),
         cost_estimate=pl.CostEstimate(
-            flops=COST_COUNT, bytes_accessed=n << 19, transcendentals=0
+            flops=n * 1_500_000_000, bytes_accessed=n << 19, transcendentals=0
         ),
         name="count_edges",
     )(place, *edges, planes)
 
 
-def hidden_kernel(n, place_ref, *refs):
-    edges = refs[:n]
-    mine_ref, far_ref, start_ref, own_ref, other_ref = refs[n : n + 5]
-    words, keys, meta, word_sems, meta_sems, planes_ref, adj = refs[n + 5 :]
-    loads = start_loads(edges, words, meta, word_sems, meta_sems)
-    planes_ref[...] = start_ref[...]
-    count_all(place_ref[0], loads, words, meta, keys, planes_ref)
-    half = HID // 2
+def after_kernel(value_ref, earlier_ref, out_ref):
+    pass
+
+
+def after(value, earlier):
+    anywhere = pl.BlockSpec(memory_space=pl.ANY)
+    return pl.pallas_call(
+        after_kernel,
+        out_shape=jax.ShapeDtypeStruct(value.shape, value.dtype),
+        in_specs=[anywhere] * 2,
+        out_specs=anywhere,
+        input_output_aliases={0: 0},
+        compiler_params=pltpu.CompilerParams(vmem_limit_bytes=1 << 20),
+        name="after",
+    )(value, earlier)
+
+
+def hidden_kernel(place_ref, mine_ref, far_ref, planes_ref, out_ref, adj, grads_vmem, sems):
+    copies = []
+    for i in range(8):
+        core = place_ref[1] if i < 4 else 1 - place_ref[1]
+        half = mine_ref if i < 4 else far_ref
+        rows = pl.ds(pl.multiple_of((i % 4 * 2 + core) * PIECE, PIECE), PIECE)
+        piece = half.at[pl.ds(i % 4 * PIECE, PIECE)]
+        copies.append(pltpu.make_async_copy(piece, grads_vmem.at[rows], sems.at[i]))
+        copies[i].start()
     for r in range(RELS):
         for t in range(TILES):
             adj[r % 2, :, t * LANES : (t + 1) * LANES] = counts(
                 [planes_ref[r, p, t] for p in range(PLANES)]
             )
-        for out_ref, grads_ref in ((other_ref, far_ref), (own_ref, mine_ref)):
-            h = lax.dot_general(
-                adj[r % 2], grads_ref[...], (((1,), (1,)), ((), ())), preferred_element_type=F32
-            )
-            out_ref[:, r * half : (r + 1) * half] = (h * (1.0 / FANOUT)).astype(BF16)
-
-
-def hidden_halves(place, edges, mine, far, planes):
-    n = len(edges)
-    vmem = pl.BlockSpec(memory_space=pltpu.VMEM)
-    return pl.pallas_call(
-        functools.partial(hidden_kernel, n),
-        out_shape=[jax.ShapeDtypeStruct((OWN, HALF), BF16)] * 2,
+        if r == 0:
+            for copy in copies:
+                copy.wait()
+        h = lax.dot_general(
+            adj[r % 2], grads_vmem[...], (((1,), (1,)), ((), ())), preferred_element_type=F32
+        )
+        out_ref[:, r * HID : (r + 1) * HID] = (h * (1.0 / FANOUT)).astype(BF16)
+
+
+def hidden_rows(place, mine, far, planes):
+    vmem = pl.BlockSpec(memory_space=pltpu.VMEM)
+    return pl.pallas_call(
+        hidden_kernel,
+        out_shape=jax.ShapeDtypeStruct((OWN, COLS), BF16),
         in_specs=[pl.BlockSpec(memory_space=pltpu.SMEM)]
-        + [pl.BlockSpec(memory_space=pl.ANY)] * n
-        + [vmem] * 3,
-        out_specs=[vmem] * 2,
-        scratch_shapes=count_scratch(n)
-        + [pltpu.VMEM(PLANE_SHAPE, I32), pltpu.VMEM((2, OWN, TGT), BF16)],
-        compiler_params=pltpu.CompilerParams(vmem_limit_bytes=18 << 20),
+        + [pl.BlockSpec(memory_space=pl.ANY)] * 2
+        + [vmem],
+        out_specs=vmem,
+        scratch_shapes=[
+            pltpu.VMEM((2, OWN, TGT), BF16),
+            pltpu.VMEM((HID, TGT), BF16),
+            pltpu.SemaphoreType.DMA((8,)),
+        ],
+        compiler_params=pltpu.CompilerParams(vmem_limit_bytes=14 << 20),
         cost_estimate=pl.CostEstimate(
-            flops=8_000_000_000, bytes_accessed=4 << 20, transcendentals=0
-        ),
-        name="hidden_halves",
-    )(place, *edges, mine, far, planes)
-
-
-def weave(low, high, odd):
-    lane = lax.broadcasted_iota(I32, low.shape, 1)
-    if odd:
-        return jnp.where(lane < LANES // 2, pltpu.roll(low, LANES // 2, 1), high)
-    return jnp.where(lane < LANES // 2, low, pltpu.roll(high, LANES // 2, 1))
-
-
-def source_kernel(place_ref, own_ref, other_ref, weight_ref, out_ref, hidden):
-    first = place_ref[1] == 0
-    for i in range(HALF // LANES):
-        cols = slice(i * LANES, (i + 1) * LANES)
-        own, other = own_ref[:, cols].astype(F32), other_ref[:, cols].astype(F32)
-        low, high = jnp.where(first, own, other), jnp.where(first, other, own)
-        for odd in range(2):
-            to = (2 * i + odd) * LANES
-            hidden[:, to : to + LANES] = weave(low, high, odd).astype(BF16)
+            flops=3_000_000_000, bytes_accessed=4 << 20, transcendentals=0
+        ),
+        name="hidden_rows",
+    )(place, mine, far, planes)
+
+
+def source_kernel(hidden_ref, weight_ref, out_ref):
     out_ref[...] = lax.dot_general(
-        hidden[...], weight_ref[...], (((1,), (1,)), ((), ())), preferred_element_type=F32
+        hidden_ref[...], weight_ref[...], (((1,), (1,)), ((), ())), preferred_element_type=F32
     ).astype(BF16)
 
 
-def source_rows(place, own, other, weight):
+def source_rows(hidden, weight):
     vmem = pl.BlockSpec(memory_space=pltpu.VMEM)
     return pl.pallas_call(
         source_kernel,
         out_shape=jax.ShapeDtypeStruct((OWN, D_IN), BF16),
-        in_specs=[pl.BlockSpec(memory_space=pltpu.SMEM)] + [vmem] * 3,
+        in_specs=[vmem] * 2,
         out_specs=vmem,
-        scratch_shapes=[pltpu.VMEM((OWN, COLS), BF16)],
         compiler_params=pltpu.CompilerParams(vmem_limit_bytes=16 << 20),
         cost_estimate=pl.CostEstimate(
             flops=1_000_000_000, bytes_accessed=6 << 20, transcendentals=0
         ),
         name="source_rows",
-    )(place, own, other, weight)
-
-
-def product_kernel(h0_ref, h1_ref, f0_ref, f1_ref, out_ref, chunks, packed, sems):
-    tiles = HALF // LANES
-    chunks[:, ROWS_OUT * tiles :, :] = jnp.zeros((DEVICES, CHUNK - ROWS_OUT * tiles, LANES), F32)
+    )(hidden, weight)
+
+
+def product_kernel(h0_ref, h1_ref, f0_ref, f1_ref, out_ref, chunks):
+    tiles = COLS // LANES
     for r in range(ROWS_OUT):
-        rows = slice(r * LANES, (r + 1) * LANES)
+        rows = slice(r * PEERS, (r + 1) * PEERS)
         p = jnp.dot(f0_ref[rows, :], h0_ref[...], preferred_element_type=F32)
         p += jnp.dot(f1_ref[rows, :], h1_ref[...], preferred_element_type=F32)
         for c in range(tiles):
             chunks[:, r * tiles + c, :] = p[:, c * LANES : (c + 1) * LANES]
-    step = DEVICES // 4
-    copies = []
-    for i in range(4):
-        part = pl.ds(i * step, step)
-        packed[part] = chunks[part].astype(BF16)
-        copies.append(pltpu.make_async_copy(packed.at[part], out_ref.at[part], sems.at[i]))
-        copies[i].start()
-    for copy in copies:
-        copy.wait()
+    out_ref[...] = chunks[...].astype(BF16)
 
 
 def products(h0, h1, f0, f1):
     vmem = pl.BlockSpec(memory_space=pltpu.VMEM)
     return pl.pallas_call(
         product_kernel,
-        out_shape=jax.ShapeDtypeStruct((DEVICES, CHUNK, LANES), BF16),
+        out_shape=jax.ShapeDtypeStruct((PEERS, CHUNK, LANES), BF16),
         in_specs=[vmem] * 4,
-        out_specs=pl.BlockSpec(memory_space=pltpu.HBM),
-        scratch_shapes=[
-            pltpu.VMEM((DEVICES, CHUNK, LANES), F32),
-            pltpu.VMEM((DEVICES, CHUNK, LANES), BF16),
-            pltpu.SemaphoreType.DMA((4,)),
-        ],
-        compiler_params=pltpu.CompilerParams(vmem_limit_bytes=24 << 20),
+        out_specs=vmem,
+        scratch_shapes=[pltpu.VMEM((PEERS, CHUNK, LANES), F32)],
+        compiler_params=pltpu.CompilerParams(vmem_limit_bytes=PRODUCT_VMEM << 20),
         cost_estimate=pl.CostEstimate(
             flops=1_000_000_000, bytes_accessed=5 << 20, transcendentals=0
         ),
@@ -378,20 +367,15 @@
 
 
 def sum_kernel(scale, got_ref, out_ref, sums):
-    tiles = HALF // LANES
-    totals = [None, None]
-    for d in range(DEVICES):
-        term = got_ref[d].astype(F32)
-        core = d % 2
-        totals[core] = term if totals[core] is None else totals[core] + term
-    for odd in range(2):
-        sums[odd] = weave(totals[0] * scale, totals[1] * scale, odd)
+    tiles = COLS // LANES
+    total = got_ref[0].astype(F32)
+    for d in range(1, PEERS):
+        total += got_ref[d].astype(F32)
+    sums[...] = total * scale
     for r in range(ROWS_OUT):
         for i in range(tiles):
-            for odd in range(2):
-                to = (2 * i + odd) * LANES
-                at = r * tiles + i
-                out_ref[r : r + 1, to : to + LANES] = sums[odd, at : at + 1, :]
+            at = r * tiles + i
+            out_ref[r : r + 1, i * LANES : (i + 1) * LANES] = sums[at : at + 1, :]
 
 
 def sum_chunks(got, scale):
@@ -401,7 +385,7 @@
         out_shape=jax.ShapeDtypeStruct((ROWS_OUT, COLS), F32),
         in_specs=[vmem],
         out_specs=vmem,
-        scratch_shapes=[pltpu.VMEM((2, CHUNK, LANES), F32)],
+        scratch_shapes=[pltpu.VMEM((CHUNK, LANES), F32)],
         compiler_params=pltpu.CompilerParams(vmem_limit_bytes=14 << 20),
         cost_estimate=pl.CostEstimate(flops=1 << 20, bytes_accessed=2 << 20, transcendentals=0),
         name="sum_chunks",
@@ -410,7 +394,8 @@
 
 def on_device(grad_out, src_feat, weight, nbr_slot, src_ids, valid_rows, block_rel):
     rel = lax.axis_index("rel")
-    place = jnp.stack([rel, rel & 1]).astype(I32)
+    core = rel & 1
+    place = jnp.stack([rel, core]).astype(I32)
 
     def along_z(v, k):
         return lax.ppermute(v, "rel", [(i, (i + 2 * k) % 8) for i in range(8)])
@@ -419,26 +404,38 @@
         return lax.ppermute(v, "rel", [(i, i ^ 1) for i in range(8)])
 
     codes = edge_codes(valid_rows, block_rel, src_ids[0], nbr_slot.transpose(1, 2, 0))
-    far = {k: along_z(codes, k) for k in (2, 1, 3)}
-    grads = [grad_out.T]
-    grads += [along_z(grads[0], k) for k in (1, 2, 3)]
-    planes, mine = count_first(place, [codes, other_core(codes)], grads)
-    planes = count_edges(place, [far[k] for k in (2, 1, 3)], planes)
+    far = {k: along_z(codes, k) for k in (1, 3, 2)}
+    grads = {0: grad_out.T}
+    for k in (1, 3, 2):
+        grads[k] = along_z(grads[0], k)
+    planes, mine = count_first(place, codes, [grads[k] for k in range(4)])
+    planes = count_edges(place, [other_core(codes), far[1], far[3]], planes)
+    planes = count_edges(place, [other_core(far[1]), other_core(far[3])], planes)
+    last = after(far[2], planes)
+    planes = count_edges(place, [last], planes)
+    planes = count_edges(place, [other_core(last)], planes)
 
     old = jnp.arange(D_IN, dtype=I32)[:, None]
-    new = jnp.arange(D_IN, dtype=I32)[None, :]
-    order = (old == (new % LANES) * ROWS_OUT + new // LANES).astype(BF16)
-    feats = lax.dot_general(
-        order, src_feat, (((0,), (1,)), ((), ())), preferred_element_type=F32
-    ).astype(BF16)
-    feats_other = other_core(feats)
-
-    swapped = [other_core(far[k]) for k in (2, 1, 3)]
-    own, other = hidden_halves(place, swapped, mine, other_core(mine), planes)
-    got = other_core(other)
-    source_grad = source_rows(place, own, other, weight)
-    chunks = products(own, got, feats, feats_other)
-    chunks = lax.all_to_all(chunks, ("dp", "rel"), 0, 0, tiled=True)
+    new = jnp.arange(D_IN // 2, dtype=I32)[None, :]
+
+    def half_feats(which):
+        device = (new % PEERS) * 2 + which
+        order = (old == device * ROWS_OUT + new // PEERS).astype(BF16)
+        return lax.dot_general(
+            order, src_feat, (((0,), (1,)), ((), ())), preferred_element_type=F32
+        ).astype(BF16)
+
+    feats = half_feats(core)
+    feats_other = other_core(half_feats(1 - core))
+
+    hidden = hidden_rows(place, mine, other_core(mine), planes)
+    got = other_core(hidden)
+    source_grad = source_rows(hidden, weight)
+    chunks = products(hidden, got, feats, feats_other)
+    groups = [[2 * i + c for i in range(PEERS)] for c in range(2)]
+    chunks = lax.all_to_all(
+        chunks, ("dp", "rel"), 0, 0, tiled=True, axis_index_groups=groups
+    )
     return source_grad, sum_chunks(chunks, float(TGT * 16) ** (-0.5))
 
 

time: 94.3 us -> 90.9 us (0.964)
  waiting for transfers between devices: 38.2 us -> 31.4 us
  Pallas kernels: 24.5 us -> 28.9 us
  starting transfers between devices: 23.1 us -> 21.9 us
    pallas_call x1 -> x4, Pallas kernels: 4.12 us -> 11.8 us  [count_edges(): pl.pallas_call(functools.partial(count_kernel, n), out_shape=jax.ShapeDty...]
    ppermute x6, waiting for transfers between devices: 12.2 us -> 6.3 us  [along_z(): return lax.ppermute(v, 'rel', [(i, (i + 2 * k) % 8) for i in range(8)])]
    pallas_call x3 -> x4, Pallas kernels: 13.9 us -> 11.4 us  [the longest x1 4.84 us: hidden_rows(): pl.pallas_call(hidden_kernel, out_shape=jax.ShapeDtypeStruct((OWN, COLS),...]
    all_to_all x1, waiting for transfers between devices: 24.7 us -> 23.2 us  [on_device(): lax.all_to_all(chunks, ('dp', 'rel'), 0, 0, tiled=True, axis_index_groups...]
    ppermute x6, starting transfers between devices: 11.2 us -> 9.93 us  [along_z(): return lax.ppermute(v, 'rel', [(i, (i + 2 * k) % 8) for i in range(8)])]
  transfers between devices with their start and end apart: 14 -> 14, of which waited for: 4 -> 3; matrix products, arithmetic and copies ran while one was open for 1% -> 1% of each run, Pallas kernels for 14% -> 21%
where the time goes in v4:
time: 90.9 us; the launch traced here: 90.5 us
  waiting for transfers between devices  31.4 us (35%)
  Pallas kernels  28.9 us (32%)
  starting transfers between devices  21.9 us (24%)
  local copies, waits for them, and re-layouts  6.59 us (7%)
    all_to_all x1, waiting for transfers between devices, on_device(): lax.all_to_all(chunks, ('dp', 'rel'), 0, 0, tiled=True, axis_index_groups...  23.2 us
    pallas_call x4, Pallas kernels, count_edges(): pl.pallas_call(functools.partial(count_kernel, n), out_shape=jax.ShapeDty...  11.8 us
    ppermute x6, starting transfers between devices, along_z(): return lax.ppermute(v, 'rel', [(i, (i + 2 * k) % 8) for i in range(8)])  9.93 us
    all_to_all x1, starting transfers between devices, on_device(): lax.all_to_all(chunks, ('dp', 'rel'), 0, 0, tiled=True, axis_index_groups...  9.82 us
    unnamed x14, local copies, waits for them, and re-layouts  6.59 us
    ppermute x6, waiting for transfers between devices, along_z(): return lax.ppermute(v, 'rel', [(i, (i + 2 * k) % 8) for i in range(8)])  6.3 us
    pallas_call x1, Pallas kernels, hidden_rows(): pl.pallas_call(hidden_kernel, out_shape=jax.ShapeDtypeStruct((OWN, COLS),...  4.84 us
    pallas_call x1, Pallas kernels, products(): pl.pallas_call(product_kernel, out_shape=jax.ShapeDtypeStruct((PEERS, CHU...  4.22 us
  transfers between devices with their start and end apart: 14, of which 3 were waited for; matrix products, arithmetic and copies ran while one was open for 1% of the time, Pallas kernels for 21%

profile of v4, /device:TPU:0, one launch (start us, length us, event | category | flops | bytes accessed | tf_op | source)
XLA Modules:
  0.0 90.5 jit_solution(16969159436914019329)
XLA Ops:
  0.6 2.1 %collective-permute-start = (bf16[64,1024]{1,0:T(8,128)(2,1)}, bf16[64,1024]{1,0:T(8,128)(2,1)S(1)}, u32[]{:S(2)}, u32[]{:S(2)}) collective-permute-start(bf16[64,1024]{1,0:T(8,128)(2,1)} %bitcast.7), channel_id=1, source_target_pairs={{0,2},{1,3},{2,4},{3,5},{4,6},{5,7},{6,0},{7,1},{8,10},{9,11},{10,... | collective-permute-start | bytes 393224 | tf_op jit(solution)/shard_map/ppermute | solution.py:401
  2.7 3.6 %collective-permute-start.1 = (bf16[64,1024]{1,0:T(8,128)(2,1)}, bf16[64,1024]{1,0:T(8,128)(2,1)S(1)}, u32[]{:S(2)}, u32[]{:S(2)}) collective-permute-start(bf16[64,1024]{1,0:T(8,128)(2,1)} %bitcast.8), channel_id=1, source_target_pairs={{0,4},{1,5},{2,6},{3,7},{4,0},{5,1},{6,2},{7,3},{8,12},{9,13},{10,... | collective-permute-start | bytes 393224 | tf_op jit(solution)/shard_map/ppermute | solution.py:401
  6.3 1.0 %collective-permute-start.2 = (bf16[64,1024]{1,0:T(8,128)(2,1)}, bf16[64,1024]{1,0:T(8,128)(2,1)S(1)}, u32[]{:S(2)}, u32[]{:S(2)}) collective-permute-start(bf16[64,1024]{1,0:T(8,128)(2,1)} %bitcast.9), channel_id=1, source_target_pairs={{0,6},{1,7},{2,0},{3,1},{4,2},{5,3},{6,4},{7,5},{8,14},{9,15},{10,... | collective-permute-start | bytes 393224 | tf_op jit(solution)/shard_map/ppermute | solution.py:401
  7.3 2.8 %edge_codes.1.edge_ref = s32[65,8,128]{2,1,0:T(8,128)} custom-call(s32[1,8]{1,0:T(1,128)} %valid_ref.1, s32[8]{0:T(128)} %rel_ref.1, s32[8,512]{1,0:T(8,128)} %bitcast.12, s32[8,16,1024]{2,1,0:T(8,128)} %bitcast.11), custom_call_target="tpu_custom_call" | custom-call | bytes 1048576 | tf_op jit(solution)/shard_map/edge_codes/pallas_call | solution.py:73
  10.1 1.0 %collective-permute-start.5 = (s32[65,8,128]{2,1,0:T(8,128)}, s32[65,8,128]{2,1,0:T(8,128)S(1)}, u32[]{:S(2)}, u32[]{:S(2)}) collective-permute-start(s32[65,8,128]{2,1,0:T(8,128)} %edge_codes.1.edge_ref), channel_id=1, source_target_pairs={{0,2},{1,3},{2,4},{3,5},{4,6},{5,7},{6,0},{7,1},{8,10},{9,11},{10,... | collective-permute-start | bytes 798728 | tf_op jit(solution)/shard_map/ppermute | solution.py:401
  11.1 2.2 %collective-permute-start.7 = (s32[65,8,128]{2,1,0:T(8,128)}, s32[65,8,128]{2,1,0:T(8,128)S(1)}, u32[]{:S(2)}, u32[]{:S(2)}) collective-permute-start(s32[65,8,128]{2,1,0:T(8,128)} %edge_codes.1.edge_ref), channel_id=1, source_target_pairs={{0,6},{1,7},{2,0},{3,1},{4,2},{5,3},{6,4},{7,5},{8,14},{9,15},{10,... | collective-permute-start | bytes 798728 | tf_op jit(solution)/shard_map/ppermute | solution.py:401
  13.3 0.1 pad_add_fusion.place_ref
  13.5 1.0 %copy-done.5 = s32[65,8,128]{2,1,0:T(8,128)S(1)} copy-done((s32[65,8,128]{2,1,0:T(8,128)S(1)}, s32[65,8,128]{2,1,0:T(8,128)}, u32[]{:S(2)}) %copy-start.5) | copy-done | bytes 266264
  14.4 0.9 copy-done.6
  15.3 2.3 %count_first.1 = (s32[5,10,8,8,128]{4,3,2,1,0:T(8,128)S(1)}, bf16[256,1024]{1,0:T(8,128)(2,1)S(1)}) custom-call(s32[2]{0:T(128)S(1)} %pad_add_fusion.place_ref, s32[65,8,128]{2,1,0:T(8,128)S(1)} %copy-done.5, bf16[64,1024]{1,0:T(8,128)(2,1)S(1)} %bitcast.10, bf16[64,1024]{1,0:T(8,128)(2,1)S(1)} %collective-permute-done.refs_1_, ...), custom_call_target="tpu_custom_call" | custom-call | flops 2000000000 | bytes 1048576 | tf_op jit(solution)/shard_map/count_first/pallas_call | solution.py:222
  17.7 0.7 collective-permute-start.3
  18.4 6.3 %collective-permute-done.5.refs_1_ = s32[65,8,128]{2,1,0:T(8,128)S(1)} collective-permute-done((s32[65,8,128]{2,1,0:T(8,128)}, s32[65,8,128]{2,1,0:T(8,128)S(1)}, u32[]{:S(2)}, u32[]{:S(2)}) %collective-permute-start.5) | collective-permute-done | bytes 266272 | tf_op jit(solution)/shard_map/ppermute | solution.py:401
  24.7 0.5 collective-permute-start.8
  25.2 4.2 %count_edges.4.refs_2_ = s32[5,10,8,8,128]{4,3,2,1,0:T(8,128)S(1)} custom-call(s32[2]{0:T(128)S(1)} %pad_add_fusion.place_ref, s32[65,8,128]{2,1,0:T(8,128)S(1)} %collective-permute-done.9.refs_0_, s32[65,8,128]{2,1,0:T(8,128)S(1)} %collective-permute-done.5.refs_1_, s32[65,8,128]{2,1,0:T(8,128)S(1)} %collective-permute-done.7.refs_2_, ...), custom_call_target="tpu_custom_call" | custom-call | flops 4499999744 | bytes 1572864 | tf_op jit(solution)/shard_map/count_edges/pallas_call | solution.py:243
  29.4 3.4 %count_edges.5.earlier_ref.refs_1_ = s32[5,10,8,8,128]{4,3,2,1,0:T(8,128)S(1)} custom-call(s32[2]{0:T(128)S(1)} %pad_add_fusion.place_ref, s32[65,8,128]{2,1,0:T(8,128)S(1)} %collective-permute-done.6.refs_0_, s32[65,8,128]{2,1,0:T(8,128)S(1)} %collective-permute-done.8.refs_1_, s32[5,10,8,8,128]{4,3,2,1,0:T(8,128)S(1)} %count_edges.4.refs_2_), custom_call_target="tpu_custom_call" | custom-call | flops 3000000000 | bytes 1048576 | tf_op jit(solution)/shard_map/count_edges/pallas_call | solution.py:243
  32.8 0.1 collective-permute-start.10
  32.9 2.3 %count_edges.6.refs_1_ = s32[5,10,8,8,128]{4,3,2,1,0:T(8,128)S(1)} custom-call(s32[2]{0:T(128)S(1)} %pad_add_fusion.place_ref, s32[65,8,128]{2,1,0:T(8,128)S(1)} %after.1.refs_0_, s32[5,10,8,8,128]{4,3,2,1,0:T(8,128)S(1)} %count_edges.5.earlier_ref.refs_1_), custom_call_target="tpu_custom_call" | custom-call | flops 1500000000 | bytes 524288 | tf_op jit(solution)/shard_map/count_edges/pallas_call | solution.py:243
  35.2 1.9 %count_edges.7.planes_ref = s32[5,10,8,8,128]{4,3,2,1,0:T(8,128)S(1)} custom-call(s32[2]{0:T(128)S(1)} %pad_add_fusion.place_ref, s32[65,8,128]{2,1,0:T(8,128)S(1)} %collective-permute-done.10.refs_0_, s32[5,10,8,8,128]{4,3,2,1,0:T(8,128)S(1)} %count_edges.6.refs_1_), custom_call_target="tpu_custom_call" | custom-call | flops 1500000000 | bytes 524288 | tf_op jit(solution)/shard_map/count_edges/pallas_call | solution.py:243
  37.2 4.8 %hidden_rows.1.hidden_ref.h0_ref = bf16[256,2560]{1,0:T(8,128)(2,1)S(1)} custom-call(s32[2]{0:T(128)S(1)} %pad_add_fusion.place_ref, bf16[256,1024]{1,0:T(8,128)(2,1)S(1)} %get-tuple-element.4.mine_ref, bf16[256,1024]{1,0:T(8,128)(2,1)S(1)} %collective-permute-done.3.far_ref, s32[5,10,8,8,128]{4,3,2,1,0:T(8,128)S(1)} %count_edges.7.planes_ref), custom_call_target="tpu_custom_call" | custom-call | flops 3000000000 | bytes 4194304 | tf_op jit(solution)/shard_map/hidden_rows/pallas_call | solution.py:301
  42.0 0.6 collective-permute-start.11
  42.6 0.4 convolution_convert_fusion
  43.0 0.3 collective-permute-start.12
  43.3 0.4 convolution_convert_fusion.1.f0_ref
  43.6 1.9 %collective-permute-done.12.f1_ref = bf16[384,256]{1,0:T(8,128)(2,1)S(1)} collective-permute-done((bf16[384,256]{1,0:T(8,128)(2,1)S(1)}, bf16[384,256]{1,0:T(8,128)(2,1)S(1)}, u32[]{:S(2)}, u32[]{:S(2)}) %collective-permute-start.12) | collective-permute-done | bytes 196640 | tf_op jit(solution)/shard_map/ppermute | solution.py:404
  45.5 4.2 %products.1 = bf16[64,120,128]{2,1,0:T(8,128)(2,1)S(1)} custom-call(bf16[256,2560]{1,0:T(8,128)(2,1)S(1)} %hidden_rows.1.hidden_ref.h0_ref, bf16[256,2560]{1,0:T(8,128)(2,1)S(1)} %collective-permute-done.11.h1_ref, bf16[384,256]{1,0:T(8,128)(2,1)S(1)} %convolution_convert_fusion.1.f0_ref, bf16[384,256]{1,0:T(8,128)(2,1)S(1)} %collective-permute-done.12.f1_ref), custom_call_target="tpu_custom_call" | custom-call | flops 1000000000 | bytes 5242880 | tf_op jit(solution)/shard_map/products/pallas_call | solution.py:355
  49.8 1.3 %copy-done.1 = bf16[64,120,128]{2,1,0:T(8,128)(2,1)} copy-done((bf16[64,120,128]{2,1,0:T(8,128)(2,1)}, bf16[64,120,128]{2,1,0:T(8,128)(2,1)S(1)}, u32[]{:S(2)}) %copy-start.1) | copy-done | bytes 1966104
  51.1 9.8 %all-to-all-start = ((bf16[64,120,128]{2,1,0:T(8,128)(2,1)}), bf16[64,120,128]{2,1,0:T(8,128)(2,1)S(1)}, u32[]{:S(2)}, u32[]{:S(2)}) async-start(bf16[64,120,128]{2,1,0:T(8,128)(2,1)} %copy-done.1), calls=%async_computation | async-start | bytes 3932160 | tf_op jit(solution)/shard_map/all_to_all | solution.py:436
  60.9 1.3 %copy-done.3 = bf16[256,2560]{1,0:T(8,128)(2,1)S(1)} copy-done((bf16[256,2560]{1,0:T(8,128)(2,1)S(1)}, bf16[256,2560]{1,0:T(8,128)(2,1)}, u32[]{:S(2)}) %copy-start.3) | copy-done | bytes 1310744
  62.2 2.1 %copy-done.4 = bf16[768,2560]{1,0:T(8,128)(2,1)S(1)} copy-done((bf16[768,2560]{1,0:T(8,128)(2,1)S(1)}, bf16[768,2560]{1,0:T(8,128)(2,1)}, u32[]{:S(2)}) %copy-start.4) | copy-done | bytes 3932184
  64.3 2.0 %source_rows.1 = bf16[256,768]{1,0:T(8,128)(2,1)} custom-call(bf16[256,2560]{1,0:T(8,128)(2,1)S(1)} %copy-done.3, bf16[768,2560]{1,0:T(8,128)(2,1)S(1)} %copy-done.4), custom_call_target="tpu_custom_call" | custom-call | flops 1000000000 | bytes 6291456 | tf_op jit(solution)/shard_map/source_rows/pallas_call | solution.py:329
  66.3 23.2 %all-to-all-done.got_ref = bf16[64,120,128]{2,1,0:T(8,128)(2,1)S(1)} async-done(((bf16[64,120,128]{2,1,0:T(8,128)(2,1)}), bf16[64,120,128]{2,1,0:T(8,128)(2,1)S(1)}, u32[]{:S(2)}, u32[]{:S(2)}) %all-to-all-start) | async-done | bytes 1966112 | tf_op jit(solution)/shard_map/all_to_all | solution.py:436
  89.5 0.9 %sum_chunks.1 = f32[6,2560]{1,0:T(8,128)} custom-call(bf16[64,120,128]{2,1,0:T(8,128)(2,1)S(1)} %all-to-all-done.got_ref), custom_call_target="tpu_custom_call" | custom-call | flops 1048576 | bytes 2097152 | tf_op jit(solution)/shard_map/sum_chunks/pallas_call | solution.py:383
  (26 shorter events, 0.1 us)
Async XLA Ops:
  0.6 42.0 %copy-start = (bf16[256,768]{1,0:T(8,128)(2,1)S(1)}, bf16[256,768]{1,0:T(8,128)(2,1)}, u32[]{:S(2)}) copy-start(bf16[256,768]{1,0:T(8,128)(2,1)} %param.8) | copy-start | bytes 1179652
  0.6 12.7 %collective-permute-start = (bf16[64,1024]{1,0:T(8,128)(2,1)}, bf16[64,1024]{1,0:T(8,128)(2,1)S(1)}, u32[]{:S(2)}, u32[]{:S(2)}) collective-permute-start(bf16[64,1024]{1,0:T(8,128)(2,1)} %bitcast.7), channel_id=1, source_target_pairs={{0,2},{1,3},{2,4},{3,5},{4,6},{5,7},{6,0},{7,1},{8,10},{9,11},{10,... | collective-permute-start | bytes 393224 | tf_op jit(solution)/shard_map/ppermute | solution.py:401
  2.7 10.7 %collective-permute-start.1 = (bf16[64,1024]{1,0:T(8,128)(2,1)}, bf16[64,1024]{1,0:T(8,128)(2,1)S(1)}, u32[]{:S(2)}, u32[]{:S(2)}) collective-permute-start(bf16[64,1024]{1,0:T(8,128)(2,1)} %bitcast.8), channel_id=1, source_target_pairs={{0,4},{1,5},{2,6},{3,7},{4,0},{5,1},{6,2},{7,3},{8,12},{9,13},{10,... | collective-permute-start | bytes 393224 | tf_op jit(solution)/shard_map/ppermute | solution.py:401
  6.3 7.2 %collective-permute-start.2 = (bf16[64,1024]{1,0:T(8,128)(2,1)}, bf16[64,1024]{1,0:T(8,128)(2,1)S(1)}, u32[]{:S(2)}, u32[]{:S(2)}) collective-permute-start(bf16[64,1024]{1,0:T(8,128)(2,1)} %bitcast.9), channel_id=1, source_target_pairs={{0,6},{1,7},{2,0},{3,1},{4,2},{5,3},{6,4},{7,5},{8,14},{9,15},{10,... | collective-permute-start | bytes 393224 | tf_op jit(solution)/shard_map/ppermute | solution.py:401
  10.1 14.6 %collective-permute-start.5 = (s32[65,8,128]{2,1,0:T(8,128)}, s32[65,8,128]{2,1,0:T(8,128)S(1)}, u32[]{:S(2)}, u32[]{:S(2)}) collective-permute-start(s32[65,8,128]{2,1,0:T(8,128)} %edge_codes.1.edge_ref), channel_id=1, source_target_pairs={{0,2},{1,3},{2,4},{3,5},{4,6},{5,7},{6,0},{7,1},{8,10},{9,11},{10,... | collective-permute-start | bytes 798728 | tf_op jit(solution)/shard_map/ppermute | solution.py:401
  11.1 13.5 %collective-permute-start.7 = (s32[65,8,128]{2,1,0:T(8,128)}, s32[65,8,128]{2,1,0:T(8,128)S(1)}, u32[]{:S(2)}, u32[]{:S(2)}) collective-permute-start(s32[65,8,128]{2,1,0:T(8,128)} %edge_codes.1.edge_ref), channel_id=1, source_target_pairs={{0,6},{1,7},{2,0},{3,1},{4,2},{5,3},{6,4},{7,5},{8,14},{9,15},{10,... | collective-permute-start | bytes 798728 | tf_op jit(solution)/shard_map/ppermute | solution.py:401
  13.3 11.8 %collective-permute-start.9 = (s32[65,8,128]{2,1,0:T(8,128)}, s32[65,8,128]{2,1,0:T(8,128)S(1)}, u32[]{:S(2)}, u32[]{:S(2)}) collective-permute-start(s32[65,8,128]{2,1,0:T(8,128)} %edge_codes.1.edge_ref), channel_id=1, source_target_pairs={{0,1},{1,0},{2,3},{3,2},{4,5},{5,4},{6,7},{7,6},{8,9},{9,8},{10,11... | collective-permute-start | bytes 798728 | tf_op jit(solution)/shard_map/ppermute | solution.py:404
  13.4 19.3 %collective-permute-start.4 = (s32[65,8,128]{2,1,0:T(8,128)}, s32[65,8,128]{2,1,0:T(8,128)S(1)}, u32[]{:S(2)}, u32[]{:S(2)}) collective-permute-start(s32[65,8,128]{2,1,0:T(8,128)} %edge_codes.1.edge_ref), channel_id=1, source_target_pairs={{0,4},{1,5},{2,6},{3,7},{4,0},{5,1},{6,2},{7,3},{8,12},{9,13},{10,... | collective-permute-start | bytes 798728 | tf_op jit(solution)/shard_map/ppermute | solution.py:401
  13.5 1.0 %copy-start.5 = (s32[65,8,128]{2,1,0:T(8,128)S(1)}, s32[65,8,128]{2,1,0:T(8,128)}, u32[]{:S(2)}) copy-start(s32[65,8,128]{2,1,0:T(8,128)} %edge_codes.1.edge_ref) | copy-start | bytes 798724
  14.4 0.9 copy-start.6
  17.7 19.5 %collective-permute-start.3 = (bf16[256,1024]{1,0:T(8,128)(2,1)S(1)}, bf16[256,1024]{1,0:T(8,128)(2,1)S(1)}, u32[]{:S(2)}, u32[]{:S(2)}) collective-permute-start(bf16[256,1024]{1,0:T(8,128)(2,1)S(1)} %get-tuple-element.4.mine_ref), channel_id=1, source_target_pairs={{0,1},{1,0},{2,3},{3,2},{4,5},{5,4},{6,7},{7,6},{8,9},{9,8},{10,11... | collective-permute-start | bytes 1572872 | tf_op jit(solution)/shard_map/ppermute | solution.py:404
  24.7 4.7 %collective-permute-start.6 = (s32[65,8,128]{2,1,0:T(8,128)S(1)}, s32[65,8,128]{2,1,0:T(8,128)S(1)}, u32[]{:S(2)}, u32[]{:S(2)}) collective-permute-start(s32[65,8,128]{2,1,0:T(8,128)S(1)} %collective-permute-done.5.refs_1_), channel_id=1, source_target_pairs={{0,1},{1,0},{2,3},{3,2},{4,5},{5,4},{6,7},{7,6},{8,9},{9,8},{10,11... | collective-permute-start | bytes 798728 | tf_op jit(solution)/shard_map/ppermute | solution.py:404
  24.7 4.7 %collective-permute-start.8 = (s32[65,8,128]{2,1,0:T(8,128)S(1)}, s32[65,8,128]{2,1,0:T(8,128)S(1)}, u32[]{:S(2)}, u32[]{:S(2)}) collective-permute-start(s32[65,8,128]{2,1,0:T(8,128)S(1)} %collective-permute-done.7.refs_2_), channel_id=1, source_target_pairs={{0,1},{1,0},{2,3},{3,2},{4,5},{5,4},{6,7},{7,6},{8,9},{9,8},{10,11... | collective-permute-start | bytes 798728 | tf_op jit(solution)/shard_map/ppermute | solution.py:404
  32.8 2.4 %collective-permute-start.10 = (s32[65,8,128]{2,1,0:T(8,128)S(1)}, s32[65,8,128]{2,1,0:T(8,128)S(1)}, u32[]{:S(2)}, u32[]{:S(2)}) collective-permute-start(s32[65,8,128]{2,1,0:T(8,128)S(1)} %after.1.refs_0_), channel_id=1, source_target_pairs={{0,1},{1,0},{2,3},{3,2},{4,5},{5,4},{6,7},{7,6},{8,9},{9,8},{10,11... | collective-permute-start | bytes 798728 | tf_op jit(solution)/shard_map/ppermute | solution.py:404
  42.0 7.7 %copy-start.2 = (bf16[256,2560]{1,0:T(8,128)(2,1)}, bf16[256,2560]{1,0:T(8,128)(2,1)S(1)}, u32[]{:S(2)}) copy-start(bf16[256,2560]{1,0:T(8,128)(2,1)S(1)} %hidden_rows.1.hidden_ref.h0_ref) | copy-start | bytes 3932164
  42.0 3.5 %collective-permute-start.11 = (bf16[256,2560]{1,0:T(8,128)(2,1)S(1)}, bf16[256,2560]{1,0:T(8,128)(2,1)S(1)}, u32[]{:S(2)}, u32[]{:S(2)}) collective-permute-start(bf16[256,2560]{1,0:T(8,128)(2,1)S(1)} %hidden_rows.1.hidden_ref.h0_ref), channel_id=1, source_target_pairs={{0,1},{1,0},{2,3},{3,2},{4,5},{5,4},{6,7},{7,6},{8,9},{9,8},{10,11... | collective-permute-start | bytes 3932168 | tf_op jit(solution)/shard_map/ppermute | solution.py:404
  43.0 2.6 %collective-permute-start.12 = (bf16[384,256]{1,0:T(8,128)(2,1)S(1)}, bf16[384,256]{1,0:T(8,128)(2,1)S(1)}, u32[]{:S(2)}, u32[]{:S(2)}) collective-permute-start(bf16[384,256]{1,0:T(8,128)(2,1)S(1)} %convolution_convert_fusion), channel_id=1, source_target_pairs={{0,1},{1,0},{2,3},{3,2},{4,5},{5,4},{6,7},{7,6},{8,9},{9,8},{10,11... | collective-permute-start | bytes 589832 | tf_op jit(solution)/shard_map/ppermute | solution.py:404
  49.8 1.3 %copy-start.1 = (bf16[64,120,128]{2,1,0:T(8,128)(2,1)}, bf16[64,120,128]{2,1,0:T(8,128)(2,1)S(1)}, u32[]{:S(2)}) copy-start(bf16[64,120,128]{2,1,0:T(8,128)(2,1)S(1)} %products.1) | copy-start | bytes 5898244
  51.1 38.5 %all-to-all-start = ((bf16[64,120,128]{2,1,0:T(8,128)(2,1)}), bf16[64,120,128]{2,1,0:T(8,128)(2,1)S(1)}, u32[]{:S(2)}, u32[]{:S(2)}) async-start(bf16[64,120,128]{2,1,0:T(8,128)(2,1)} %copy-done.1), calls=%async_computation | async-start | bytes 3932160 | tf_op jit(solution)/shard_map/all_to_all | solution.py:436
  60.9 1.3 %copy-start.3 = (bf16[256,2560]{1,0:T(8,128)(2,1)S(1)}, bf16[256,2560]{1,0:T(8,128)(2,1)}, u32[]{:S(2)}) copy-start(bf16[256,2560]{1,0:T(8,128)(2,1)} %copy-done.2) | copy-start | bytes 3932164
  62.2 2.1 %copy-start.4 = (bf16[768,2560]{1,0:T(8,128)(2,1)S(1)}, bf16[768,2560]{1,0:T(8,128)(2,1)}, u32[]{:S(2)}) copy-start(bf16[768,2560]{1,0:T(8,128)(2,1)} %weight_ref.1) | copy-start | bytes 11796484

commit v5 on v4

--- a/solution.py
+++ b/solution.py
@@ -26,13 +26,17 @@
 LANES = 128
 CHUNK = 120
 PEERS = 64
-PRODUCT_VMEM = 24
+HALF = COLS // 2
 TILES = TGT // LANES
 STEP = 2
 PIECE = HID // 8
-
-
-def edge_kernel(valid_ref, rel_ref, ids_ref, nbr_ref, out_ref):
+COST_EDGES = 1_000_000
+COST_LAST = 1_000_000
+
+
+def edge_kernel(valid_ref, rel_ref, ids_ref, nbr_ref, grads_ref, out_ref, copy_ref, sem):
+    copy = pltpu.make_async_copy(grads_ref, copy_ref, sem)
+    copy.start()
     lane = lax.broadcasted_iota(I32, (8, LANES), 1)
     sub = lax.broadcasted_iota(I32, (8, LANES), 0)
     meta = jnp.zeros((8, LANES), I32)
@@ -67,18 +71,25 @@
                 halves.append(jnp.where(live, found, NO_EDGE))
             out_ref[b * TILES + t] = halves[0] | (halves[1] << 16)
     out_ref[BLKS * TILES] = meta
-
-
-def edge_codes(valid_rows, block_rel, ids, nbr):
+    copy.wait()
+
+
+def edge_codes(valid_rows, block_rel, ids, nbr, grads):
+    anywhere = pl.BlockSpec(memory_space=pl.ANY)
     return pl.pallas_call(
         edge_kernel,
-        out_shape=jax.ShapeDtypeStruct((BLKS * TILES + 1, 8, LANES), I32),
+        out_shape=[
+            jax.ShapeDtypeStruct((BLKS * TILES + 1, 8, LANES), I32),
+            jax.ShapeDtypeStruct(grads.shape, grads.dtype),
+        ],
         in_specs=[pl.BlockSpec(memory_space=pltpu.SMEM)] * 2
-        + [pl.BlockSpec(memory_space=pltpu.VMEM)] * 2,
-        out_specs=pl.BlockSpec(memory_space=pltpu.VMEM),
+        + [pl.BlockSpec(memory_space=pltpu.VMEM)] * 2
+        + [anywhere],
+        out_specs=[pl.BlockSpec(memory_space=pltpu.VMEM), anywhere],
+        scratch_shapes=[pltpu.SemaphoreType.DMA],
         cost_estimate=pl.CostEstimate(flops=0, bytes_accessed=1 << 20, transcendentals=0),
         name="edge_codes",
-    )(valid_rows, block_rel, ids, nbr)
+    )(valid_rows, block_rel, ids, nbr, grads)
 
 
 def full_add(a, b, c):
@@ -201,40 +212,28 @@
     count_all(place_ref[0], loads, words, meta, keys, planes_ref)
 
 
-def first_kernel(place_ref, edge_ref, *refs):
-    grads = refs[:4]
-    planes_ref, half_ref, words, keys, meta, word_sems, meta_sems, grad_sems = refs[4:]
+def first_kernel(place_ref, edge_ref, planes_ref, words, keys, meta, word_sems, meta_sems):
     loads = start_loads([edge_ref], words, meta, word_sems, meta_sems)
-    copies = []
-    for k in range(4):
-        z = (place_ref[0] // 2 - k) & 3
-        rows = pl.ds(pl.multiple_of(z * PIECE, PIECE), PIECE)
-        copies.append(pltpu.make_async_copy(grads[k], half_ref.at[rows], grad_sems.at[k]))
-        copies[k].start()
     planes_ref[...] = jnp.zeros_like(planes_ref)
     count_all(place_ref[0], loads, words, meta, keys, planes_ref)
-    for copy in copies:
-        copy.wait()
-
-
-def count_first(place, edge, grads):
-    vmem = pl.BlockSpec(memory_space=pltpu.VMEM)
+
+
+def count_first(place, edge):
     return pl.pallas_call(
         first_kernel,
-        out_shape=[
-            jax.ShapeDtypeStruct(PLANE_SHAPE, I32),
-            jax.ShapeDtypeStruct((HID // 2, TGT), BF16),
+        out_shape=jax.ShapeDtypeStruct(PLANE_SHAPE, I32),
+        in_specs=[
+            pl.BlockSpec(memory_space=pltpu.SMEM),
+            pl.BlockSpec(memory_space=pl.ANY),
         ],
-        in_specs=[pl.BlockSpec(memory_space=pltpu.SMEM)]
-        + [pl.BlockSpec(memory_space=pl.ANY)] * 5,
-        out_specs=[vmem] * 2,
-        scratch_shapes=count_scratch(1) + [pltpu.SemaphoreType.DMA((4,))],
+        out_specs=pl.BlockSpec(memory_space=pltpu.VMEM),
+        scratch_shapes=count_scratch(1),
         compiler_params=pltpu.CompilerParams(vmem_limit_bytes=14 << 20),
         cost_estimate=pl.CostEstimate(
             flops=2_000_000_000, bytes_accessed=1 << 20, transcendentals=0
         ),
         name="count_first",
-    )(place, edge, *grads)
+    )(place, edge)
 
 
 def count_edges(place, edges, planes):
@@ -250,132 +249,185 @@
         scratch_shapes=count_scratch(n),
         compiler_params=pltpu.CompilerParams(vmem_limit_bytes=14 << 20),
         cost_estimate=pl.CostEstimate(
-            flops=n * 1_500_000_000, bytes_accessed=n << 19, transcendentals=0
+            flops=n * COST_EDGES, bytes_accessed=1 << 10, transcendentals=0
         ),
         name="count_edges",
     )(place, *edges, planes)
 
 
-def after_kernel(value_ref, earlier_ref, out_ref):
-    pass
-
-
-def after(value, earlier):
-    anywhere = pl.BlockSpec(memory_space=pl.ANY)
-    return pl.pallas_call(
-        after_kernel,
-        out_shape=jax.ShapeDtypeStruct(value.shape, value.dtype),
-        in_specs=[anywhere] * 2,
-        out_specs=anywhere,
-        input_output_aliases={0: 0},
-        compiler_params=pltpu.CompilerParams(vmem_limit_bytes=1 << 20),
-        name="after",
-    )(value, earlier)
-
-
-def hidden_kernel(place_ref, mine_ref, far_ref, planes_ref, out_ref, adj, grads_vmem, sems):
-    copies = []
-    for i in range(8):
-        core = place_ref[1] if i < 4 else 1 - place_ref[1]
-        half = mine_ref if i < 4 else far_ref
-        rows = pl.ds(pl.multiple_of((i % 4 * 2 + core) * PIECE, PIECE), PIECE)
-        piece = half.at[pl.ds(i % 4 * PIECE, PIECE)]
-        copies.append(pltpu.make_async_copy(piece, grads_vmem.at[rows], sems.at[i]))
-        copies[i].start()
+def last_kernel(place_ref, edge_ref, start_ref, adj_ref, *scratch):
+    words, keys, meta, word_sems, meta_sems, planes_ref = scratch
+    loads = start_loads([edge_ref], words, meta, word_sems, meta_sems)
+    planes_ref[...] = start_ref[...]
+    count_all(place_ref[0], loads, words, meta, keys, planes_ref)
     for r in range(RELS):
         for t in range(TILES):
-            adj[r % 2, :, t * LANES : (t + 1) * LANES] = counts(
+            adj_ref[r, :, t * LANES : (t + 1) * LANES] = counts(
                 [planes_ref[r, p, t] for p in range(PLANES)]
             )
-        if r == 0:
-            for copy in copies:
-                copy.wait()
+
+
+def count_last(place, edge, planes):
+    vmem = pl.BlockSpec(memory_space=pltpu.VMEM)
+    return pl.pallas_call(
+        last_kernel,
+        out_shape=jax.ShapeDtypeStruct((RELS, OWN, TGT), BF16),
+        in_specs=[
+            pl.BlockSpec(memory_space=pltpu.SMEM),
+            pl.BlockSpec(memory_space=pl.ANY),
+            vmem,
+        ],
+        out_specs=vmem,
+        scratch_shapes=count_scratch(1) + [pltpu.VMEM(PLANE_SHAPE, I32)],
+        compiler_params=pltpu.CompilerParams(vmem_limit_bytes=14 << 20),
+        cost_estimate=pl.CostEstimate(
+            flops=COST_LAST, bytes_accessed=1 << 10, transcendentals=0
+        ),
+        name="count_last",
+    )(place, edge, planes)
+
+
+def after_kernel(*refs):
+    pass
+
+
+def after(values, earlier):
+    n = len(values)
+    anywhere = pl.BlockSpec(memory_space=pl.ANY)
+    return pl.pallas_call(
+        after_kernel,
+        out_shape=[jax.ShapeDtypeStruct(v.shape, v.dtype) for v in values],
+        in_specs=[anywhere] * (n + 1),
+        out_specs=[anywhere] * n,
+        input_output_aliases={i: i for i in range(n)},
+        compiler_params=pltpu.CompilerParams(vmem_limit_bytes=1 << 20),
+        cost_estimate=pl.CostEstimate(flops=1000, bytes_accessed=1 << 10, transcendentals=0),
+        name="after",
+    )(*values, earlier)
+
+
+def hidden_kernel(place_ref, *refs):
+    grads = refs[:4]
+    adj_ref, out_ref, grads_vmem, sems = refs[4:]
+    copies = []
+    for k in range(4):
+        z = (place_ref[0] // 2 - k) & 3
+        rows = pl.ds(pl.multiple_of(z * PIECE, PIECE), PIECE)
+        copies.append(pltpu.make_async_copy(grads[k], grads_vmem.at[rows], sems.at[k]))
+        copies[k].start()
+    for copy in copies:
+        copy.wait()
+    half = HID // 2
+    for r in range(RELS):
         h = lax.dot_general(
-            adj[r % 2], grads_vmem[...], (((1,), (1,)), ((), ())), preferred_element_type=F32
+            adj_ref[r], grads_vmem[...], (((1,), (1,)), ((), ())), preferred_element_type=F32
         )
-        out_ref[:, r * HID : (r + 1) * HID] = (h * (1.0 / FANOUT)).astype(BF16)
-
-
-def hidden_rows(place, mine, far, planes):
+        out_ref[:, r * half : (r + 1) * half] = (h * (1.0 / FANOUT)).astype(BF16)
+
+
+def hidden_half(place, grads, adj):
     vmem = pl.BlockSpec(memory_space=pltpu.VMEM)
     return pl.pallas_call(
         hidden_kernel,
-        out_shape=jax.ShapeDtypeStruct((OWN, COLS), BF16),
+        out_shape=jax.ShapeDtypeStruct((OWN, HALF), BF16),
         in_specs=[pl.BlockSpec(memory_space=pltpu.SMEM)]
-        + [pl.BlockSpec(memory_space=pl.ANY)] * 2
+        + [pl.BlockSpec(memory_space=pl.ANY)] * 4
         + [vmem],
         out_specs=vmem,
-        scratch_shapes=[
-            pltpu.VMEM((2, OWN, TGT), BF16),
-            pltpu.VMEM((HID, TGT), BF16),
-            pltpu.SemaphoreType.DMA((8,)),
-        ],
-        compiler_params=pltpu.CompilerParams(vmem_limit_bytes=14 << 20),
+        scratch_shapes=[pltpu.VMEM((HID // 2, TGT), BF16), pltpu.SemaphoreType.DMA((4,))],
+        compiler_params=pltpu.CompilerParams(vmem_limit_bytes=10 << 20),
         cost_estimate=pl.CostEstimate(
-            flops=3_000_000_000, bytes_accessed=4 << 20, transcendentals=0
-        ),
-        name="hidden_rows",
-    )(place, mine, far, planes)
-
-
-def source_kernel(hidden_ref, weight_ref, out_ref):
+            flops=1_000_000_000, bytes_accessed=4 << 20, transcendentals=0
+        ),
+        name="hidden_half",
+    )(place, *grads, adj)
+
+
+def weave(low, high, odd):
+    lane = lax.broadcasted_iota(I32, low.shape, 1)
+    if odd:
+        return jnp.where(lane < LANES // 2, pltpu.roll(low, LANES // 2, 1), high)
+    return jnp.where(lane < LANES // 2, low, pltpu.roll(high, LANES // 2, 1))
+
+
+def source_kernel(place_ref, mine_ref, far_ref, weight_ref, out_ref, hidden):
+    first = place_ref[1] == 0
+    for i in range(HALF // LANES):
+        cols = slice(i * LANES, (i + 1) * LANES)
+        mine, far = mine_ref[:, cols].astype(F32), far_ref[:, cols].astype(F32)
+        low, high = jnp.where(first, mine, far), jnp.where(first, far, mine)
+        for odd in range(2):
+            to = (2 * i + odd) * LANES
+            hidden[:, to : to + LANES] = weave(low, high, odd).astype(BF16)
     out_ref[...] = lax.dot_general(
-        hidden_ref[...], weight_ref[...], (((1,), (1,)), ((), ())), preferred_element_type=F32
+        hidden[...], weight_ref[...], (((1,), (1,)), ((), ())), preferred_element_type=F32
     ).astype(BF16)
 
 
-def source_rows(hidden, weight):
+def source_rows(place, mine, far, weight):
     vmem = pl.BlockSpec(memory_space=pltpu.VMEM)
     return pl.pallas_call(
         source_kernel,
         out_shape=jax.ShapeDtypeStruct((OWN, D_IN), BF16),
-        in_specs=[vmem] * 2,
+        in_specs=[pl.BlockSpec(memory_space=pltpu.SMEM)] + [vmem] * 3,
         out_specs=vmem,
+        scratch_shapes=[pltpu.VMEM((OWN, COLS), BF16)],
         compiler_params=pltpu.CompilerParams(vmem_limit_bytes=16 << 20),
         cost_estimate=pl.CostEstimate(
             flops=1_000_000_000, bytes_accessed=6 << 20, transcendentals=0
         ),
         name="source_rows",
-    )(hidden, weight)
-
-
-def product_kernel(h0_ref, h1_ref, f0_ref, f1_ref, out_ref, chunks):
-    tiles = COLS // LANES
-    for r in range(ROWS_OUT):
-        rows = slice(r * PEERS, (r + 1) * PEERS)
-        p = jnp.dot(f0_ref[rows, :], h0_ref[...], preferred_element_type=F32)
-        p += jnp.dot(f1_ref[rows, :], h1_ref[...], preferred_element_type=F32)
-        for c in range(tiles):
-            chunks[:, r * tiles + c, :] = p[:, c * LANES : (c + 1) * LANES]
+    )(place, mine, far, weight)
+
+
+def product_kernel(place_ref, mine_ref, far_ref, got_mine_ref, got_far_ref, f0_ref, f1_ref, *out):
+    out_ref, chunks = out
+    core = place_ref[1]
+    tiles = HALF // LANES
+    wide = 2 * LANES
+    for which, own_ref, got_ref in ((core, mine_ref, got_far_ref), (1 - core, far_ref, got_mine_ref)):
+        for b in range(HALF // wide):
+            cols = slice(b * wide, (b + 1) * wide)
+            p = jnp.dot(f0_ref[...], own_ref[:, cols], preferred_element_type=F32)
+            p += jnp.dot(f1_ref[...], got_ref[:, cols], preferred_element_type=F32)
+            for r in range(ROWS_OUT):
+                for c in range(2):
+                    at = r * 2 * tiles + which * tiles + 2 * b + c
+                    part = p[r * PEERS : (r + 1) * PEERS, c * LANES : (c + 1) * LANES]
+                    chunks[:, pl.ds(at, 1), :] = part[:, None, :]
     out_ref[...] = chunks[...].astype(BF16)
 
 
-def products(h0, h1, f0, f1):
+def products(place, mine, far, got_mine, got_far, f0, f1):
     vmem = pl.BlockSpec(memory_space=pltpu.VMEM)
     return pl.pallas_call(
         product_kernel,
         out_shape=jax.ShapeDtypeStruct((PEERS, CHUNK, LANES), BF16),
-        in_specs=[vmem] * 4,
+        in_specs=[pl.BlockSpec(memory_space=pltpu.SMEM)] + [vmem] * 6,
         out_specs=vmem,
         scratch_shapes=[pltpu.VMEM((PEERS, CHUNK, LANES), F32)],
-        compiler_params=pltpu.CompilerParams(vmem_limit_bytes=PRODUCT_VMEM << 20),
+        compiler_params=pltpu.CompilerParams(vmem_limit_bytes=20 << 20),
         cost_estimate=pl.CostEstimate(
             flops=1_000_000_000, bytes_accessed=5 << 20, transcendentals=0
         ),
         name="products",
-    )(h0, h1, f0, f1)
+    )(place, mine, far, got_mine, got_far, f0, f1)
 
 
 def sum_kernel(scale, got_ref, out_ref, sums):
-    tiles = COLS // LANES
     total = got_ref[0].astype(F32)
     for d in range(1, PEERS):
         total += got_ref[d].astype(F32)
     sums[...] = total * scale
+    tiles = HALF // LANES
     for r in range(ROWS_OUT):
-        for i in range(tiles):
-            at = r * tiles + i
-            out_ref[r : r + 1, i * LANES : (i + 1) * LANES] = sums[at : at + 1, :]
+        at = r * 2 * tiles
+        low, high = sums[at : at + tiles, :], sums[at + tiles : at + 2 * tiles, :]
+        for odd in range(2):
+            both = weave(low, high, odd)
+            for i in range(tiles):
+                to = (2 * i + odd) * LANES
+                out_ref[r : r + 1, to : to + LANES] = both[i : i + 1, :]
 
 
 def sum_chunks(got, scale):
@@ -403,17 +455,20 @@
     def other_core(v):
         return lax.ppermute(v, "rel", [(i, i ^ 1) for i in range(8)])
 
-    codes = edge_codes(valid_rows, block_rel, src_ids[0], nbr_slot.transpose(1, 2, 0))
+    codes, own_grads = edge_codes(
+        valid_rows, block_rel, src_ids[0], nbr_slot.transpose(1, 2, 0), grad_out.T
+    )
     far = {k: along_z(codes, k) for k in (1, 3, 2)}
-    grads = {0: grad_out.T}
-    for k in (1, 3, 2):
-        grads[k] = along_z(grads[0], k)
-    planes, mine = count_first(place, codes, [grads[k] for k in range(4)])
+    grads = [along_z(own_grads, k) for k in (1, 2, 3)]
+    planes = count_first(place, codes)
     planes = count_edges(place, [other_core(codes), far[1], far[3]], planes)
     planes = count_edges(place, [other_core(far[1]), other_core(far[3])], planes)
-    last = after(far[2], planes)
+    last, grads[0], grads[2] = after([far[2], grads[0], grads[2]], planes)
     planes = count_edges(place, [last], planes)
-    planes = count_edges(place, [other_core(last)], planes)
+    adj = count_last(place, other_core(last), planes)
+    grads = [own_grads] + list(after(grads, adj))
+    mine = hidden_half(place, grads, adj)
+    other = hidden_half(place, [other_core(v) for v in grads], adj)
 
     old = jnp.arange(D_IN, dtype=I32)[:, None]
     new = jnp.arange(D_IN // 2, dtype=I32)[None, :]
@@ -428,10 +483,9 @@
     feats = half_feats(core)
     feats_other = other_core(half_feats(1 - core))
 
-    hidden = hidden_rows(place, mine, other_core(mine), planes)
-    got = other_core(hidden)
-    source_grad = source_rows(hidden, weight)
-    chunks = products(hidden, got, feats, feats_other)
+    got_mine, got_other = other_core(mine), other_core(other)
+    source_grad = source_rows(place, mine, other, weight)
+    chunks = products(place, mine, other, got_mine, got_other, feats, feats_other)
     groups = [[2 * i + c for i in range(PEERS)] for c in range(2)]
     chunks = lax.all_to_all(
         chunks, ("dp", "rel"), 0, 0, tiled=True, axis_index_groups=groups

time: 90.9 us -> 99.5 us (1.095)
  Pallas kernels: 28.9 us -> 34.3 us
  starting transfers between devices: 21.9 us -> 24.2 us
  waiting for transfers between devices: 31.4 us -> 33 us
    pallas_call x4 -> x7, Pallas kernels: 9.98 us -> 17.2 us  [the longest x1 6.9 us: edge_codes(): pl.pallas_call(edge_kernel, out_shape=[jax.ShapeDtypeStruct((BLKS * TILES...]
    ppermute x6, waiting for transfers between devices: 6.3 us -> 9.29 us  [along_z(): return lax.ppermute(v, 'rel', [(i, (i + 2 * k) % 8) for i in range(8)])]
    pallas_call x4 -> x3, Pallas kernels: 11.8 us -> 9.72 us  [count_edges(): pl.pallas_call(functools.partial(count_kernel, n), out_shape=jax.ShapeDty...]
    ppermute x6, starting transfers between devices: 9.93 us -> 11.3 us  [along_z(): return lax.ppermute(v, 'rel', [(i, (i + 2 * k) % 8) for i in range(8)])]
    ppermute x7 -> x11, waiting for transfers between devices: 1.89 us -> 0.85 us  [other_core(): return lax.ppermute(v, 'rel', [(i, i ^ 1) for i in range(8)])]
    unnamed x14 -> x18, local copies, waits for them, and re-layouts: 6.59 us -> 5.99 us
    ppermute x7 -> x11, starting transfers between devices: 2.12 us -> 2.26 us  [other_core(): return lax.ppermute(v, 'rel', [(i, i ^ 1) for i in range(8)])]
  transfers between devices with their start and end apart: 14 -> 18, of which waited for: 3 -> 5; matrix products, arithmetic and copies ran while one was open for 1% -> 1% of each run, Pallas kernels for 21% -> 23%
where the time goes in v5:
time: 99.5 us; the launch traced here: 99.2 us
  Pallas kernels  34.3 us (34%)
  waiting for transfers between devices  33 us (33%)
  starting transfers between devices  24.2 us (24%)
  local copies, waits for them, and re-layouts  5.99 us (6%)
    all_to_all x1, waiting for transfers between devices, on_device(): lax.all_to_all(chunks, ('dp', 'rel'), 0, 0, tiled=True, axis_index_groups...  22.8 us
    ppermute x6, starting transfers between devices, along_z(): return lax.ppermute(v, 'rel', [(i, (i + 2 * k) % 8) for i in range(8)])  11.3 us
    all_to_all x1, starting transfers between devices, on_device(): lax.all_to_all(chunks, ('dp', 'rel'), 0, 0, tiled=True, axis_index_groups...  10.7 us
    pallas_call x3, Pallas kernels, count_edges(): pl.pallas_call(functools.partial(count_kernel, n), out_shape=jax.ShapeDty...  9.72 us
    ppermute x6, waiting for transfers between devices, along_z(): return lax.ppermute(v, 'rel', [(i, (i + 2 * k) % 8) for i in range(8)])  9.29 us
    pallas_call x1, Pallas kernels, edge_codes(): pl.pallas_call(edge_kernel, out_shape=[jax.ShapeDtypeStruct((BLKS * TILES...  6.9 us
    unnamed x18, local copies, waits for them, and re-layouts  5.99 us
    pallas_call x2, Pallas kernels, hidden_half(): pl.pallas_call(hidden_kernel, out_shape=jax.ShapeDtypeStruct((OWN, HALF),...  4.74 us
  transfers between devices with their start and end apart: 18, of which 5 were waited for; matrix products, arithmetic and copies ran while one was open for 1% of the time, Pallas kernels for 23%

profile of v5, /device:TPU:0, one launch (start us, length us, event | category | flops | bytes accessed | tf_op | source)
XLA Modules:
  0.0 99.2 jit_solution(5622998925595615026)
XLA Ops:
  0.6 6.9 %edge_codes.1 = (s32[65,8,128]{2,1,0:T(8,128)}, bf16[64,1024]{1,0:T(8,128)(2,1)}) custom-call(s32[1,8]{1,0:T(1,128)} %valid_ref.1, s32[8]{0:T(128)} %rel_ref.1, s32[8,512]{1,0:T(8,128)} %bitcast.9, s32[8,16,1024]{2,1,0:T(8,128)} %bitcast.7, bf16[64,1024]{1,0:T(8,128)(2,1)} %bitcast.8), custom_call_target="tpu_custom_call" | custom-call | bytes 1048576 | tf_op jit(solution)/shard_map/edge_codes/pallas_call | solution.py:79
  7.6 2.1 %collective-permute-start.3 = (s32[65,8,128]{2,1,0:T(8,128)}, s32[65,8,128]{2,1,0:T(8,128)S(1)}, u32[]{:S(2)}, u32[]{:S(2)}) collective-permute-start(s32[65,8,128]{2,1,0:T(8,128)} %get-tuple-element.11.edge_ref), channel_id=1, source_target_pairs={{0,2},{1,3},{2,4},{3,5},{4,6},{5,7},{6,0},{7,1},{8,10},{9,11},{10,... | collective-permute-start | bytes 798728 | tf_op jit(solution)/shard_map/ppermute | solution.py:453
  9.6 2.2 %collective-permute-start.5 = (s32[65,8,128]{2,1,0:T(8,128)}, s32[65,8,128]{2,1,0:T(8,128)S(1)}, u32[]{:S(2)}, u32[]{:S(2)}) collective-permute-start(s32[65,8,128]{2,1,0:T(8,128)} %get-tuple-element.11.edge_ref), channel_id=1, source_target_pairs={{0,6},{1,7},{2,0},{3,1},{4,2},{5,3},{6,4},{7,5},{8,14},{9,15},{10,... | collective-permute-start | bytes 798728 | tf_op jit(solution)/shard_map/ppermute | solution.py:453
  11.8 1.8 %collective-permute-start = (s32[65,8,128]{2,1,0:T(8,128)}, s32[65,8,128]{2,1,0:T(8,128)S(1)}, u32[]{:S(2)}, u32[]{:S(2)}) collective-permute-start(s32[65,8,128]{2,1,0:T(8,128)} %get-tuple-element.11.edge_ref), channel_id=1, source_target_pairs={{0,4},{1,5},{2,6},{3,7},{4,0},{5,1},{6,2},{7,3},{8,12},{9,13},{10,... | collective-permute-start | bytes 798728 | tf_op jit(solution)/shard_map/ppermute | solution.py:453
  13.6 1.0 %collective-permute-start.1 = (bf16[64,1024]{1,0:T(8,128)(2,1)}, bf16[64,1024]{1,0:T(8,128)(2,1)S(1)}, u32[]{:S(2)}, u32[]{:S(2)}) collective-permute-start(bf16[64,1024]{1,0:T(8,128)(2,1)} %get-tuple-element.10.refs_0_), channel_id=1, source_target_pairs={{0,2},{1,3},{2,4},{3,5},{4,6},{5,7},{6,0},{7,1},{8,10},{9,11},{10,... | collective-permute-start | bytes 393224 | tf_op jit(solution)/shard_map/ppermute | solution.py:453
  14.6 4.5 %collective-permute-done.3.refs_1_ = s32[65,8,128]{2,1,0:T(8,128)S(1)} collective-permute-done((s32[65,8,128]{2,1,0:T(8,128)}, s32[65,8,128]{2,1,0:T(8,128)S(1)}, u32[]{:S(2)}, u32[]{:S(2)}) %collective-permute-start.3) | collective-permute-done | bytes 266272 | tf_op jit(solution)/shard_map/ppermute | solution.py:453
  19.2 4.4 %collective-permute-done.5.refs_2_ = s32[65,8,128]{2,1,0:T(8,128)S(1)} collective-permute-done((s32[65,8,128]{2,1,0:T(8,128)}, s32[65,8,128]{2,1,0:T(8,128)S(1)}, u32[]{:S(2)}, u32[]{:S(2)}) %collective-permute-start.5) | collective-permute-done | bytes 266272 | tf_op jit(solution)/shard_map/ppermute | solution.py:453
  23.6 3.6 %collective-permute-start.2 = (bf16[64,1024]{1,0:T(8,128)(2,1)}, bf16[64,1024]{1,0:T(8,128)(2,1)S(1)}, u32[]{:S(2)}, u32[]{:S(2)}) collective-permute-start(bf16[64,1024]{1,0:T(8,128)(2,1)} %get-tuple-element.10.refs_0_), channel_id=1, source_target_pairs={{0,6},{1,7},{2,0},{3,1},{4,2},{5,3},{6,4},{7,5},{8,14},{9,15},{10,... | collective-permute-start | bytes 393224 | tf_op jit(solution)/shard_map/ppermute | solution.py:453
  27.2 0.9 copy-done.8
  28.1 1.9 %count_first.1.refs_3_ = s32[5,10,8,8,128]{4,3,2,1,0:T(8,128)S(1)} custom-call(s32[2]{0:T(128)S(1)} %pad_add_fusion.place_ref, s32[65,8,128]{2,1,0:T(8,128)S(1)} %copy-done.8), custom_call_target="tpu_custom_call" | custom-call | flops 2000000000 | bytes 1048576 | tf_op jit(solution)/shard_map/count_first/pallas_call | solution.py:222
  30.1 4.1 %count_edges.3.refs_2_ = s32[5,10,8,8,128]{4,3,2,1,0:T(8,128)S(1)} custom-call(s32[2]{0:T(128)S(1)} %pad_add_fusion.place_ref, s32[65,8,128]{2,1,0:T(8,128)S(1)} %collective-permute-done.7.refs_0_, s32[65,8,128]{2,1,0:T(8,128)S(1)} %collective-permute-done.3.refs_1_, s32[65,8,128]{2,1,0:T(8,128)S(1)} %collective-permute-done.5.refs_2_, ...), custom_call_target="tpu_custom_call" | custom-call | flops 3000000 | bytes 1024 | tf_op jit(solution)/shard_map/count_edges/pallas_call | solution.py:242
  34.2 3.2 %count_edges.4.refs_3_.refs_1_ = s32[5,10,8,8,128]{4,3,2,1,0:T(8,128)S(1)} custom-call(s32[2]{0:T(128)S(1)} %pad_add_fusion.place_ref, s32[65,8,128]{2,1,0:T(8,128)S(1)} %collective-permute-done.4.refs_0_, s32[65,8,128]{2,1,0:T(8,128)S(1)} %collective-permute-done.6.refs_1_, s32[5,10,8,8,128]{4,3,2,1,0:T(8,128)S(1)} %count_edges.3.refs_2_), custom_call_target="tpu_custom_call" | custom-call | flops 2000000 | bytes 1024 | tf_op jit(solution)/shard_map/count_edges/pallas_call | solution.py:242
  37.7 0.6 copy-done.7
  38.3 0.6 collective-permute-start.8
  38.9 2.4 %count_edges.5.start_ref = s32[5,10,8,8,128]{4,3,2,1,0:T(8,128)S(1)} custom-call(s32[2]{0:T(128)S(1)} %pad_add_fusion.place_ref, s32[65,8,128]{2,1,0:T(8,128)S(1)} %get-tuple-element.14.refs_0_, s32[5,10,8,8,128]{4,3,2,1,0:T(8,128)S(1)} %count_edges.4.refs_3_.refs_1_), custom_call_target="tpu_custom_call" | custom-call | flops 1000000 | bytes 1024 | tf_op jit(solution)/shard_map/count_edges/pallas_call | solution.py:242
  41.4 3.6 %count_last.1.refs_3_.refs_4_ = bf16[5,256,1024]{2,1,0:T(8,128)(2,1)S(1)} custom-call(s32[2]{0:T(128)S(1)} %pad_add_fusion.place_ref, s32[65,8,128]{2,1,0:T(8,128)S(1)} %collective-permute-done.9.edge_ref, s32[5,10,8,8,128]{4,3,2,1,0:T(8,128)S(1)} %count_edges.5.start_ref), custom_call_target="tpu_custom_call" | custom-call | flops 1000000 | bytes 1024 | tf_op jit(solution)/shard_map/count_last/pallas_call | solution.py:272
  45.0 0.4 collective-permute-done.8.refs_1_
  46.1 2.2 %hidden_half.2.mine_ref = bf16[256,1280]{1,0:T(8,128)(2,1)S(1)} custom-call(s32[2]{0:T(128)S(1)} %pad_add_fusion.place_ref, bf16[64,1024]{1,0:T(8,128)(2,1)S(1)} %copy-done.7, bf16[64,1024]{1,0:T(8,128)(2,1)S(1)} %get-tuple-element.15.refs_1_, bf16[64,1024]{1,0:T(8,128)(2,1)S(1)} %get-tuple-element.16.refs_2_, ...), custom_call_target="tpu_custom_call" | custom-call | flops 1000000000 | bytes 4194304 | tf_op jit(solution)/shard_map/hidden_half/pallas_call | solution.py:330
  48.3 0.4 collective-permute-start.14
  48.7 2.6 %hidden_half.3.far_ref = bf16[256,1280]{1,0:T(8,128)(2,1)S(1)} custom-call(s32[2]{0:T(128)S(1)} %pad_add_fusion.place_ref, bf16[64,1024]{1,0:T(8,128)(2,1)} %collective-permute-done.10.refs_0_, bf16[64,1024]{1,0:T(8,128)(2,1)} %collective-permute-done.11.refs_1_, bf16[64,1024]{1,0:T(8,128)(2,1)} %collective-permute-done.12.refs_2_, ...), custom_call_target="tpu_custom_call" | custom-call | flops 1000000000 | bytes 4194304 | tf_op jit(solution)/shard_map/hidden_half/pallas_call | solution.py:330
  51.6 0.4 convolution_convert_fusion
  52.0 0.6 collective-permute-start.16
  52.6 0.4 convolution_convert_fusion.1.f0_ref
  52.9 0.8 collective-permute-done.16.f1_ref
  53.8 3.6 %products.1 = bf16[64,120,128]{2,1,0:T(8,128)(2,1)S(1)} custom-call(s32[2]{0:T(128)S(1)} %pad_add_fusion.place_ref, bf16[256,1280]{1,0:T(8,128)(2,1)S(1)} %hidden_half.2.mine_ref, bf16[256,1280]{1,0:T(8,128)(2,1)S(1)} %hidden_half.3.far_ref, bf16[256,1280]{1,0:T(8,128)(2,1)S(1)} %collective-permute-done.14.got_mine_ref, ...), custom_call_target="tpu_custom_call" | custom-call | flops 1000000000 | bytes 5242880 | tf_op jit(solution)/shard_map/products/pallas_call | solution.py:403
  57.4 1.3 %copy-done.1 = bf16[64,120,128]{2,1,0:T(8,128)(2,1)} copy-done((bf16[64,120,128]{2,1,0:T(8,128)(2,1)}, bf16[64,120,128]{2,1,0:T(8,128)(2,1)S(1)}, u32[]{:S(2)}) %copy-start.1) | copy-done | bytes 1966104
  58.7 10.7 %all-to-all-start = ((bf16[64,120,128]{2,1,0:T(8,128)(2,1)}), bf16[64,120,128]{2,1,0:T(8,128)(2,1)S(1)}, u32[]{:S(2)}, u32[]{:S(2)}) async-start(bf16[64,120,128]{2,1,0:T(8,128)(2,1)} %copy-done.1), calls=%async_computation | async-start | bytes 3932160 | tf_op jit(solution)/shard_map/all_to_all | solution.py:490
  69.4 1.1 %copy-done.5 = bf16[256,1280]{1,0:T(8,128)(2,1)S(1)} copy-done((bf16[256,1280]{1,0:T(8,128)(2,1)S(1)}, bf16[256,1280]{1,0:T(8,128)(2,1)}, u32[]{:S(2)}) %copy-start.5) | copy-done | bytes 655384
  70.5 2.1 %copy-done.6 = bf16[768,2560]{1,0:T(8,128)(2,1)S(1)} copy-done((bf16[768,2560]{1,0:T(8,128)(2,1)S(1)}, bf16[768,2560]{1,0:T(8,128)(2,1)}, u32[]{:S(2)}) %copy-start.6) | copy-done | bytes 3932184
  72.6 2.7 %source_rows.1 = bf16[256,768]{1,0:T(8,128)(2,1)} custom-call(s32[2]{0:T(128)S(1)} %pad_add_fusion.place_ref, bf16[256,1280]{1,0:T(8,128)(2,1)S(1)} %copy-done.3, bf16[256,1280]{1,0:T(8,128)(2,1)S(1)} %copy-done.5, bf16[768,2560]{1,0:T(8,128)(2,1)S(1)} %copy-done.6), custom_call_target="tpu_custom_call" | custom-call | flops 1000000000 | bytes 6291456 | tf_op jit(solution)/shard_map/source_rows/pallas_call | solution.py:369
  75.3 22.8 %all-to-all-done.got_ref = bf16[64,120,128]{2,1,0:T(8,128)(2,1)S(1)} async-done(((bf16[64,120,128]{2,1,0:T(8,128)(2,1)}), bf16[64,120,128]{2,1,0:T(8,128)(2,1)S(1)}, u32[]{:S(2)}, u32[]{:S(2)}) %all-to-all-start) | async-done | bytes 1966112 | tf_op jit(solution)/shard_map/all_to_all | solution.py:490
  98.1 1.0 %sum_chunks.1 = f32[6,2560]{1,0:T(8,128)} custom-call(bf16[64,120,128]{2,1,0:T(8,128)(2,1)S(1)} %all-to-all-done.got_ref), custom_call_target="tpu_custom_call" | custom-call | flops 1048576 | bytes 2097152 | tf_op jit(solution)/shard_map/sum_chunks/pallas_call | solution.py:435
  (40 shorter events, 1.5 us)
Async XLA Ops:
  0.6 51.0 %copy-start = (bf16[256,768]{1,0:T(8,128)(2,1)S(1)}, bf16[256,768]{1,0:T(8,128)(2,1)}, u32[]{:S(2)}) copy-start(bf16[256,768]{1,0:T(8,128)(2,1)} %param.8) | copy-start | bytes 1179652
  7.6 11.6 %collective-permute-start.3 = (s32[65,8,128]{2,1,0:T(8,128)}, s32[65,8,128]{2,1,0:T(8,128)S(1)}, u32[]{:S(2)}, u32[]{:S(2)}) collective-permute-start(s32[65,8,128]{2,1,0:T(8,128)} %get-tuple-element.11.edge_ref), channel_id=1, source_target_pairs={{0,2},{1,3},{2,4},{3,5},{4,6},{5,7},{6,0},{7,1},{8,10},{9,11},{10,... | collective-permute-start | bytes 798728 | tf_op jit(solution)/shard_map/ppermute | solution.py:453
  9.6 13.9 %collective-permute-start.5 = (s32[65,8,128]{2,1,0:T(8,128)}, s32[65,8,128]{2,1,0:T(8,128)S(1)}, u32[]{:S(2)}, u32[]{:S(2)}) collective-permute-start(s32[65,8,128]{2,1,0:T(8,128)} %get-tuple-element.11.edge_ref), channel_id=1, source_target_pairs={{0,6},{1,7},{2,0},{3,1},{4,2},{5,3},{6,4},{7,5},{8,14},{9,15},{10,... | collective-permute-start | bytes 798728 | tf_op jit(solution)/shard_map/ppermute | solution.py:453
  11.8 11.8 %collective-permute-start.7 = (s32[65,8,128]{2,1,0:T(8,128)}, s32[65,8,128]{2,1,0:T(8,128)S(1)}, u32[]{:S(2)}, u32[]{:S(2)}) collective-permute-start(s32[65,8,128]{2,1,0:T(8,128)} %get-tuple-element.11.edge_ref), channel_id=1, source_target_pairs={{0,1},{1,0},{2,3},{3,2},{4,5},{5,4},{6,7},{7,6},{8,9},{9,8},{10,11... | collective-permute-start | bytes 798728 | tf_op jit(solution)/shard_map/ppermute | solution.py:456
  11.8 25.6 %collective-permute-start = (s32[65,8,128]{2,1,0:T(8,128)}, s32[65,8,128]{2,1,0:T(8,128)S(1)}, u32[]{:S(2)}, u32[]{:S(2)}) collective-permute-start(s32[65,8,128]{2,1,0:T(8,128)} %get-tuple-element.11.edge_ref), channel_id=1, source_target_pairs={{0,4},{1,5},{2,6},{3,7},{4,0},{5,1},{6,2},{7,3},{8,12},{9,13},{10,... | collective-permute-start | bytes 798728 | tf_op jit(solution)/shard_map/ppermute | solution.py:453
  13.6 23.8 %collective-permute-start.1 = (bf16[64,1024]{1,0:T(8,128)(2,1)}, bf16[64,1024]{1,0:T(8,128)(2,1)S(1)}, u32[]{:S(2)}, u32[]{:S(2)}) collective-permute-start(bf16[64,1024]{1,0:T(8,128)(2,1)} %get-tuple-element.10.refs_0_), channel_id=1, source_target_pairs={{0,2},{1,3},{2,4},{3,5},{4,6},{5,7},{6,0},{7,1},{8,10},{9,11},{10,... | collective-permute-start | bytes 393224 | tf_op jit(solution)/shard_map/ppermute | solution.py:453
  19.2 15.0 %collective-permute-start.4 = (s32[65,8,128]{2,1,0:T(8,128)S(1)}, s32[65,8,128]{2,1,0:T(8,128)S(1)}, u32[]{:S(2)}, u32[]{:S(2)}) collective-permute-start(s32[65,8,128]{2,1,0:T(8,128)S(1)} %collective-permute-done.3.refs_1_), channel_id=1, source_target_pairs={{0,1},{1,0},{2,3},{3,2},{4,5},{5,4},{6,7},{7,6},{8,9},{9,8},{10,11... | collective-permute-start | bytes 798728 | tf_op jit(solution)/shard_map/ppermute | solution.py:456
  23.5 10.6 %collective-permute-start.6 = (s32[65,8,128]{2,1,0:T(8,128)S(1)}, s32[65,8,128]{2,1,0:T(8,128)S(1)}, u32[]{:S(2)}, u32[]{:S(2)}) collective-permute-start(s32[65,8,128]{2,1,0:T(8,128)S(1)} %collective-permute-done.5.refs_2_), channel_id=1, source_target_pairs={{0,1},{1,0},{2,3},{3,2},{4,5},{5,4},{6,7},{7,6},{8,9},{9,8},{10,11... | collective-permute-start | bytes 798728 | tf_op jit(solution)/shard_map/ppermute | solution.py:456
  23.6 13.8 %collective-permute-start.2 = (bf16[64,1024]{1,0:T(8,128)(2,1)}, bf16[64,1024]{1,0:T(8,128)(2,1)S(1)}, u32[]{:S(2)}, u32[]{:S(2)}) collective-permute-start(bf16[64,1024]{1,0:T(8,128)(2,1)} %get-tuple-element.10.refs_0_), channel_id=1, source_target_pairs={{0,6},{1,7},{2,0},{3,1},{4,2},{5,3},{6,4},{7,5},{8,14},{9,15},{10,... | collective-permute-start | bytes 393224 | tf_op jit(solution)/shard_map/ppermute | solution.py:453
  27.2 1.0 copy-start.8
  37.4 0.9 copy-start.7
  37.4 3.9 %collective-permute-start.9 = (s32[65,8,128]{2,1,0:T(8,128)S(1)}, s32[65,8,128]{2,1,0:T(8,128)S(1)}, u32[]{:S(2)}, u32[]{:S(2)}) collective-permute-start(s32[65,8,128]{2,1,0:T(8,128)S(1)} %get-tuple-element.14.refs_0_), channel_id=1, source_target_pairs={{0,1},{1,0},{2,3},{3,2},{4,5},{5,4},{6,7},{7,6},{8,9},{9,8},{10,11... | collective-permute-start | bytes 798728 | tf_op jit(solution)/shard_map/ppermute | solution.py:456
  38.3 7.1 %collective-permute-start.8 = (bf16[64,1024]{1,0:T(8,128)(2,1)S(1)}, bf16[64,1024]{1,0:T(8,128)(2,1)S(1)}, u32[]{:S(2)}, u32[]{:S(2)}) collective-permute-start(bf16[64,1024]{1,0:T(8,128)(2,1)S(1)} %copy-done.7), channel_id=1, source_target_pairs={{0,4},{1,5},{2,6},{3,7},{4,0},{5,1},{6,2},{7,3},{8,12},{9,13},{10,... | collective-permute-start | bytes 393224 | tf_op jit(solution)/shard_map/ppermute | solution.py:453
  38.9 9.8 %collective-permute-start.10 = (bf16[64,1024]{1,0:T(8,128)(2,1)S(1)}, bf16[64,1024]{1,0:T(8,128)(2,1)}, u32[]{:S(2)}, u32[]{:S(2)}) collective-permute-start(bf16[64,1024]{1,0:T(8,128)(2,1)S(1)} %copy-done.7), channel_id=1, source_target_pairs={{0,1},{1,0},{2,3},{3,2},{4,5},{5,4},{6,7},{7,6},{8,9},{9,8},{10,11... | collective-permute-start | bytes 393224 | tf_op jit(solution)/shard_map/ppermute | solution.py:456
  45.4 3.3 %collective-permute-start.11 = (bf16[64,1024]{1,0:T(8,128)(2,1)S(1)}, bf16[64,1024]{1,0:T(8,128)(2,1)}, u32[]{:S(2)}, u32[]{:S(2)}) collective-permute-start(bf16[64,1024]{1,0:T(8,128)(2,1)S(1)} %get-tuple-element.15.refs_1_), channel_id=1, source_target_pairs={{0,1},{1,0},{2,3},{3,2},{4,5},{5,4},{6,7},{7,6},{8,9},{9,8},{10,11... | collective-permute-start | bytes 393224 | tf_op jit(solution)/shard_map/ppermute | solution.py:456
  45.6 3.1 %collective-permute-start.12 = (bf16[64,1024]{1,0:T(8,128)(2,1)S(1)}, bf16[64,1024]{1,0:T(8,128)(2,1)}, u32[]{:S(2)}, u32[]{:S(2)}) collective-permute-start(bf16[64,1024]{1,0:T(8,128)(2,1)S(1)} %get-tuple-element.16.refs_2_), channel_id=1, source_target_pairs={{0,1},{1,0},{2,3},{3,2},{4,5},{5,4},{6,7},{7,6},{8,9},{9,8},{10,11... | collective-permute-start | bytes 393224 | tf_op jit(solution)/shard_map/ppermute | solution.py:456
  45.9 2.8 %collective-permute-start.13 = (bf16[64,1024]{1,0:T(8,128)(2,1)S(1)}, bf16[64,1024]{1,0:T(8,128)(2,1)}, u32[]{:S(2)}, u32[]{:S(2)}) collective-permute-start(bf16[64,1024]{1,0:T(8,128)(2,1)S(1)} %get-tuple-element.17.refs_3_), channel_id=1, source_target_pairs={{0,1},{1,0},{2,3},{3,2},{4,5},{5,4},{6,7},{7,6},{8,9},{9,8},{10,11... | collective-permute-start | bytes 393224 | tf_op jit(solution)/shard_map/ppermute | solution.py:456
  48.3 5.4 %copy-start.2 = (bf16[256,1280]{1,0:T(8,128)(2,1)}, bf16[256,1280]{1,0:T(8,128)(2,1)S(1)}, u32[]{:S(2)}) copy-start(bf16[256,1280]{1,0:T(8,128)(2,1)S(1)} %hidden_half.2.mine_ref) | copy-start | bytes 1966084
  48.3 5.4 %collective-permute-start.14 = (bf16[256,1280]{1,0:T(8,128)(2,1)S(1)}, bf16[256,1280]{1,0:T(8,128)(2,1)S(1)}, u32[]{:S(2)}, u32[]{:S(2)}) collective-permute-start(bf16[256,1280]{1,0:T(8,128)(2,1)S(1)} %hidden_half.2.mine_ref), channel_id=1, source_target_pairs={{0,1},{1,0},{2,3},{3,2},{4,5},{5,4},{6,7},{7,6},{8,9},{9,8},{10,11... | collective-permute-start | bytes 1966088 | tf_op jit(solution)/shard_map/ppermute | solution.py:456
  51.3 2.5 %copy-start.4 = (bf16[256,1280]{1,0:T(8,128)(2,1)}, bf16[256,1280]{1,0:T(8,128)(2,1)S(1)}, u32[]{:S(2)}) copy-start(bf16[256,1280]{1,0:T(8,128)(2,1)S(1)} %hidden_half.3.far_ref) | copy-start | bytes 1966084
  51.3 2.5 %collective-permute-start.15 = (bf16[256,1280]{1,0:T(8,128)(2,1)S(1)}, bf16[256,1280]{1,0:T(8,128)(2,1)S(1)}, u32[]{:S(2)}, u32[]{:S(2)}) collective-permute-start(bf16[256,1280]{1,0:T(8,128)(2,1)S(1)} %hidden_half.3.far_ref), channel_id=1, source_target_pairs={{0,1},{1,0},{2,3},{3,2},{4,5},{5,4},{6,7},{7,6},{8,9},{9,8},{10,11... | collective-permute-start | bytes 1966088 | tf_op jit(solution)/shard_map/ppermute | solution.py:456
  52.0 1.8 %collective-permute-start.16 = (bf16[384,256]{1,0:T(8,128)(2,1)S(1)}, bf16[384,256]{1,0:T(8,128)(2,1)S(1)}, u32[]{:S(2)}, u32[]{:S(2)}) collective-permute-start(bf16[384,256]{1,0:T(8,128)(2,1)S(1)} %convolution_convert_fusion), channel_id=1, source_target_pairs={{0,1},{1,0},{2,3},{3,2},{4,5},{5,4},{6,7},{7,6},{8,9},{9,8},{10,11... | collective-permute-start | bytes 589832 | tf_op jit(solution)/shard_map/ppermute | solution.py:456
  57.4 1.3 %copy-start.1 = (bf16[64,120,128]{2,1,0:T(8,128)(2,1)}, bf16[64,120,128]{2,1,0:T(8,128)(2,1)S(1)}, u32[]{:S(2)}) copy-start(bf16[64,120,128]{2,1,0:T(8,128)(2,1)S(1)} %products.1) | copy-start | bytes 5898244
  58.7 10.7 %copy-start.3 = (bf16[256,1280]{1,0:T(8,128)(2,1)S(1)}, bf16[256,1280]{1,0:T(8,128)(2,1)}, u32[]{:S(2)}) copy-start(bf16[256,1280]{1,0:T(8,128)(2,1)} %copy-done.2) | copy-start | bytes 1966084
  58.7 39.4 %all-to-all-start = ((bf16[64,120,128]{2,1,0:T(8,128)(2,1)}), bf16[64,120,128]{2,1,0:T(8,128)(2,1)S(1)}, u32[]{:S(2)}, u32[]{:S(2)}) async-start(bf16[64,120,128]{2,1,0:T(8,128)(2,1)} %copy-done.1), calls=%async_computation | async-start | bytes 3932160 | tf_op jit(solution)/shard_map/all_to_all | solution.py:490
  69.4 1.1 %copy-start.5 = (bf16[256,1280]{1,0:T(8,128)(2,1)S(1)}, bf16[256,1280]{1,0:T(8,128)(2,1)}, u32[]{:S(2)}) copy-start(bf16[256,1280]{1,0:T(8,128)(2,1)} %copy-done.4) | copy-start | bytes 1966084
  70.5 2.1 %copy-start.6 = (bf16[768,2560]{1,0:T(8,128)(2,1)S(1)}, bf16[768,2560]{1,0:T(8,128)(2,1)}, u32[]{:S(2)}) copy-start(bf16[768,2560]{1,0:T(8,128)(2,1)} %weight_ref.1) | copy-start | bytes 11796484

commit v6 on v4

--- a/solution.py
+++ b/solution.py
@@ -26,7 +26,6 @@
 LANES = 128
 CHUNK = 120
 PEERS = 64
-PRODUCT_VMEM = 24
 TILES = TGT // LANES
 STEP = 2
 PIECE = HID // 8
@@ -201,40 +200,29 @@
     count_all(place_ref[0], loads, words, meta, keys, planes_ref)
 
 
-def first_kernel(place_ref, edge_ref, *refs):
-    grads = refs[:4]
-    planes_ref, half_ref, words, keys, meta, word_sems, meta_sems, grad_sems = refs[4:]
-    loads = start_loads([edge_ref], words, meta, word_sems, meta_sems)
-    copies = []
-    for k in range(4):
-        z = (place_ref[0] // 2 - k) & 3
-        rows = pl.ds(pl.multiple_of(z * PIECE, PIECE), PIECE)
-        copies.append(pltpu.make_async_copy(grads[k], half_ref.at[rows], grad_sems.at[k]))
-        copies[k].start()
+def first_kernel(n, place_ref, *refs):
+    edges = refs[:n]
+    planes_ref, words, keys, meta, word_sems, meta_sems = refs[n:]
+    loads = start_loads(edges, words, meta, word_sems, meta_sems)
     planes_ref[...] = jnp.zeros_like(planes_ref)
     count_all(place_ref[0], loads, words, meta, keys, planes_ref)
-    for copy in copies:
-        copy.wait()
-
-
-def count_first(place, edge, grads):
-    vmem = pl.BlockSpec(memory_space=pltpu.VMEM)
-    return pl.pallas_call(
-        first_kernel,
-        out_shape=[
-            jax.ShapeDtypeStruct(PLANE_SHAPE, I32),
-            jax.ShapeDtypeStruct((HID // 2, TGT), BF16),
-        ],
+
+
+def count_first(place, edges):
+    n = len(edges)
+    return pl.pallas_call(
+        functools.partial(first_kernel, n),
+        out_shape=jax.ShapeDtypeStruct(PLANE_SHAPE, I32),
         in_specs=[pl.BlockSpec(memory_space=pltpu.SMEM)]
-        + [pl.BlockSpec(memory_space=pl.ANY)] * 5,
-        out_specs=[vmem] * 2,
-        scratch_shapes=count_scratch(1) + [pltpu.SemaphoreType.DMA((4,))],
+        + [pl.BlockSpec(memory_space=pl.ANY)] * n,
+        out_specs=pl.BlockSpec(memory_space=pltpu.VMEM),
+        scratch_shapes=count_scratch(n),
         compiler_params=pltpu.CompilerParams(vmem_limit_bytes=14 << 20),
         cost_estimate=pl.CostEstimate(
             flops=2_000_000_000, bytes_accessed=1 << 20, transcendentals=0
         ),
         name="count_first",
-    )(place, edge, *grads)
+    )(place, *edges)
 
 
 def count_edges(place, edges, planes):
@@ -256,66 +244,80 @@
     )(place, *edges, planes)
 
 
-def after_kernel(value_ref, earlier_ref, out_ref):
-    pass
-
-
-def after(value, earlier):
-    anywhere = pl.BlockSpec(memory_space=pl.ANY)
-    return pl.pallas_call(
-        after_kernel,
-        out_shape=jax.ShapeDtypeStruct(value.shape, value.dtype),
-        in_specs=[anywhere] * 2,
-        out_specs=anywhere,
-        input_output_aliases={0: 0},
-        compiler_params=pltpu.CompilerParams(vmem_limit_bytes=1 << 20),
-        name="after",
-    )(value, earlier)
-
-
-def hidden_kernel(place_ref, mine_ref, far_ref, planes_ref, out_ref, adj, grads_vmem, sems):
+def last_kernel(n, place_ref, *refs):
+    edges = refs[:n]
+    start_ref, adj_ref, words, keys, meta, word_sems, meta_sems, planes_ref = refs[n:]
+    loads = start_loads(edges, words, meta, word_sems, meta_sems)
+    planes_ref[...] = start_ref[...]
+    count_all(place_ref[0], loads, words, meta, keys, planes_ref)
+    for r in range(RELS):
+        for t in range(TILES):
+            adj_ref[r * OWN : (r + 1) * OWN, t * LANES : (t + 1) * LANES] = counts(
+                [planes_ref[r, p, t] for p in range(PLANES)]
+            )
+
+
+def count_last(place, edges, planes):
+    n = len(edges)
+    vmem = pl.BlockSpec(memory_space=pltpu.VMEM)
+    return pl.pallas_call(
+        functools.partial(last_kernel, n),
+        out_shape=jax.ShapeDtypeStruct((RELS * OWN, TGT), BF16),
+        in_specs=[pl.BlockSpec(memory_space=pltpu.SMEM)]
+        + [pl.BlockSpec(memory_space=pl.ANY)] * n
+        + [vmem],
+        out_specs=vmem,
+        scratch_shapes=count_scratch(n) + [pltpu.VMEM(PLANE_SHAPE, I32)],
+        compiler_params=pltpu.CompilerParams(vmem_limit_bytes=14 << 20),
+        cost_estimate=pl.CostEstimate(
+            flops=6_000_000_000, bytes_accessed=4 << 20, transcendentals=0
+        ),
+        name="count_last",
+    )(place, *edges, planes)
+
+
+def hidden_kernel(place_ref, *refs):
+    grads = refs[:8]
+    adj_ref, out_ref, grads_vmem, sems = refs[8:]
     copies = []
     for i in range(8):
+        z = (place_ref[0] // 2 - i % 4) & 3
         core = place_ref[1] if i < 4 else 1 - place_ref[1]
-        half = mine_ref if i < 4 else far_ref
-        rows = pl.ds(pl.multiple_of((i % 4 * 2 + core) * PIECE, PIECE), PIECE)
-        piece = half.at[pl.ds(i % 4 * PIECE, PIECE)]
-        copies.append(pltpu.make_async_copy(piece, grads_vmem.at[rows], sems.at[i]))
+        rows = pl.ds(pl.multiple_of((z * 2 + core) * PIECE, PIECE), PIECE)
+        copies.append(pltpu.make_async_copy(grads[i], grads_vmem.at[rows], sems.at[i]))
         copies[i].start()
-    for r in range(RELS):
-        for t in range(TILES):
-            adj[r % 2, :, t * LANES : (t + 1) * LANES] = counts(
-                [planes_ref[r, p, t] for p in range(PLANES)]
-            )
-        if r == 0:
-            for copy in copies:
-                copy.wait()
+    for copy in copies:
+        copy.wait()
+    wide = 2 * LANES
+    for b in range(HID // wide):
         h = lax.dot_general(
-            adj[r % 2], grads_vmem[...], (((1,), (1,)), ((), ())), preferred_element_type=F32
+            adj_ref[...],
+            grads_vmem[b * wide : (b + 1) * wide, :],
+            (((1,), (1,)), ((), ())),
+            preferred_element_type=F32,
         )
-        out_ref[:, r * HID : (r + 1) * HID] = (h * (1.0 / FANOUT)).astype(BF16)
-
-
-def hidden_rows(place, mine, far, planes):
+        h = (h * (1.0 / FANOUT)).astype(BF16)
+        for r in range(RELS):
+            to = r * HID + b * wide
+            out_ref[:, to : to + wide] = h[r * OWN : (r + 1) * OWN, :]
+
+
+def hidden_rows(place, grads, adj):
     vmem = pl.BlockSpec(memory_space=pltpu.VMEM)
     return pl.pallas_call(
         hidden_kernel,
         out_shape=jax.ShapeDtypeStruct((OWN, COLS), BF16),
         in_specs=[pl.BlockSpec(memory_space=pltpu.SMEM)]
-        + [pl.BlockSpec(memory_space=pl.ANY)] * 2
+        + [pl.BlockSpec(memory_space=pl.ANY)] * 8
         + [vmem],
         out_specs=vmem,
-        scratch_shapes=[
-            pltpu.VMEM((2, OWN, TGT), BF16),
-            pltpu.VMEM((HID, TGT), BF16),
-            pltpu.SemaphoreType.DMA((8,)),
-        ],
+        scratch_shapes=[pltpu.VMEM((HID, TGT), BF16), pltpu.SemaphoreType.DMA((8,))],
         compiler_params=pltpu.CompilerParams(vmem_limit_bytes=14 << 20),
         cost_estimate=pl.CostEstimate(
-            flops=3_000_000_000, bytes_accessed=4 << 20, transcendentals=0
+            flops=2_000_000_000, bytes_accessed=4 << 20, transcendentals=0
         ),
         name="hidden_rows",
-    )(place, mine, far, planes)
+    )(place, *grads, adj)
 
 
 def source_kernel(hidden_ref, weight_ref, out_ref):
@@ -339,14 +341,26 @@
     )(hidden, weight)
 
 
+def chunk_row(r, tile):
+    return tile // 4 * 24 + tile // 2 % 2 * 12 + r * 2 + tile % 2
+
+
 def product_kernel(h0_ref, h1_ref, f0_ref, f1_ref, out_ref, chunks):
-    tiles = COLS // LANES
-    for r in range(ROWS_OUT):
-        rows = slice(r * PEERS, (r + 1) * PEERS)
-        p = jnp.dot(f0_ref[rows, :], h0_ref[...], preferred_element_type=F32)
-        p += jnp.dot(f1_ref[rows, :], h1_ref[...], preferred_element_type=F32)
-        for c in range(tiles):
-            chunks[:, r * tiles + c, :] = p[:, c * LANES : (c + 1) * LANES]
+    wide = 2 * LANES
+    for pair in range(COLS // (2 * wide)):
+        parts = []
+        for b in (2 * pair, 2 * pair + 1):
+            cols = slice(b * wide, (b + 1) * wide)
+            p = jnp.dot(f0_ref[...], h0_ref[:, cols], preferred_element_type=F32)
+            p += jnp.dot(f1_ref[...], h1_ref[:, cols], preferred_element_type=F32)
+            for r in range(ROWS_OUT):
+                rows = p[r * PEERS : (r + 1) * PEERS]
+                parts += [rows[:, c * LANES : (c + 1) * LANES] for c in range(2)]
+        for g in range(3):
+            at = pair * 24 + g * 8
+            for d in range(0, PEERS, 8):
+                block = jnp.stack([part[d : d + 8] for part in parts[g * 8 : (g + 1) * 8]], axis=0)
+                chunks[d : d + 8, at : at + 8, :] = jnp.swapaxes(block, 0, 1)
     out_ref[...] = chunks[...].astype(BF16)
 
 
@@ -358,7 +372,7 @@
         in_specs=[vmem] * 4,
         out_specs=vmem,
         scratch_shapes=[pltpu.VMEM((PEERS, CHUNK, LANES), F32)],
-        compiler_params=pltpu.CompilerParams(vmem_limit_bytes=PRODUCT_VMEM << 20),
+        compiler_params=pltpu.CompilerParams(vmem_limit_bytes=20 << 20),
         cost_estimate=pl.CostEstimate(
             flops=1_000_000_000, bytes_accessed=5 << 20, transcendentals=0
         ),
@@ -374,7 +388,7 @@
     sums[...] = total * scale
     for r in range(ROWS_OUT):
         for i in range(tiles):
-            at = r * tiles + i
+            at = chunk_row(r, i)
             out_ref[r : r + 1, i * LANES : (i + 1) * LANES] = sums[at : at + 1, :]
 
 
@@ -408,12 +422,11 @@
     grads = {0: grad_out.T}
     for k in (1, 3, 2):
         grads[k] = along_z(grads[0], k)
-    planes, mine = count_first(place, codes, [grads[k] for k in range(4)])
-    planes = count_edges(place, [other_core(codes), far[1], far[3]], planes)
-    planes = count_edges(place, [other_core(far[1]), other_core(far[3])], planes)
-    last = after(far[2], planes)
-    planes = count_edges(place, [last], planes)
-    planes = count_edges(place, [other_core(last)], planes)
+    pieces = [grads[k] for k in range(4)]
+    pieces += [other_core(v) for v in pieces]
+    planes = count_first(place, [codes, other_core(codes)])
+    planes = count_edges(place, [far[k] for k in (1, 3, 2)], planes)
+    adj = count_last(place, [other_core(far[k]) for k in (1, 3, 2)], planes)
 
     old = jnp.arange(D_IN, dtype=I32)[:, None]
     new = jnp.arange(D_IN // 2, dtype=I32)[None, :]
@@ -428,7 +441,7 @@
     feats = half_feats(core)
     feats_other = other_core(half_feats(1 - core))
 
-    hidden = hidden_rows(place, mine, other_core(mine), planes)
+    hidden = hidden_rows(place, pieces, adj)
     got = other_core(hidden)
     source_grad = source_rows(hidden, weight)
     chunks = products(hidden, got, feats, feats_other)

time: 90.9 us -> 86.6 us (0.953)
  Pallas kernels: 28.9 us -> 23.7 us
  local copies, waits for them, and re-layouts: 6.59 us -> 5.67 us
    pallas_call x4 -> x1, Pallas kernels: 11.8 us -> 4.07 us  [count_edges(): pl.pallas_call(functools.partial(count_kernel, n), out_shape=jax.ShapeDty...]
    pallas_call x2, Pallas kernels: 2.35 us -> 8.91 us  [the longest x1 5.66 us: count_last(): pl.pallas_call(functools.partial(last_kernel, n), out_shape=jax.ShapeDtyp...]
    pallas_call x1, Pallas kernels: 4.22 us -> 1.36 us  [products(): pl.pallas_call(product_kernel, out_shape=jax.ShapeDtypeStruct((PEERS, CHU...]
    pallas_call x1, Pallas kernels: 4.84 us -> 3.63 us  [hidden_rows(): pl.pallas_call(hidden_kernel, out_shape=jax.ShapeDtypeStruct((OWN, COLS),...]
    all_to_all x1, starting transfers between devices: 9.82 us -> 10.9 us  [on_device(): lax.all_to_all(chunks, ('dp', 'rel'), 0, 0, tiled=True, axis_index_groups...]
    unnamed x14, local copies, waits for them, and re-layouts: 6.59 us -> 5.67 us
    ppermute x7 -> x10, starting transfers between devices: 2.12 us -> 2.46 us  [other_core(): return lax.ppermute(v, 'rel', [(i, i ^ 1) for i in range(8)])]
    ppermute x7 -> x10, waiting for transfers between devices: 1.89 us -> 1.97 us  [other_core(): return lax.ppermute(v, 'rel', [(i, i ^ 1) for i in range(8)])]
  transfers between devices with their start and end apart: 14 -> 17, of which waited for: 3 -> 3; matrix products, arithmetic and copies ran while one was open for 1% -> 1% of each run, Pallas kernels for 21% -> 17%
where the time goes in v6:
time: 86.6 us; the launch traced here: 86.1 us
  waiting for transfers between devices  32.3 us (37%)
  Pallas kernels  23.7 us (27%)
  starting transfers between devices  22.7 us (26%)
  local copies, waits for them, and re-layouts  5.67 us (7%)
    all_to_all x1, waiting for transfers between devices, on_device(): lax.all_to_all(chunks, ('dp', 'rel'), 0, 0, tiled=True, axis_index_groups...  23.4 us
    all_to_all x1, starting transfers between devices, on_device(): lax.all_to_all(chunks, ('dp', 'rel'), 0, 0, tiled=True, axis_index_groups...  10.9 us
    ppermute x6, starting transfers between devices, along_z(): return lax.ppermute(v, 'rel', [(i, (i + 2 * k) % 8) for i in range(8)])  9.33 us
    ppermute x6, waiting for transfers between devices, along_z(): return lax.ppermute(v, 'rel', [(i, (i + 2 * k) % 8) for i in range(8)])  6.93 us
    unnamed x14, local copies, waits for them, and re-layouts  5.67 us
    pallas_call x1, Pallas kernels, count_last(): pl.pallas_call(functools.partial(last_kernel, n), out_shape=jax.ShapeDtyp...  5.66 us
    pallas_call x1, Pallas kernels, count_edges(): pl.pallas_call(functools.partial(count_kernel, n), out_shape=jax.ShapeDty...  4.07 us
    pallas_call x1, Pallas kernels, hidden_rows(): pl.pallas_call(hidden_kernel, out_shape=jax.ShapeDtypeStruct((OWN, COLS),...  3.63 us
  transfers between devices with their start and end apart: 17, of which 3 were waited for; matrix products, arithmetic and copies ran while one was open for 1% of the time, Pallas kernels for 17%

profile of v6, /device:TPU:0, one launch (start us, length us, event | category | flops | bytes accessed | tf_op | source)
XLA Modules:
  0.0 86.1 jit_solution(561177267437609306)
XLA Ops:
  0.6 2.8 %edge_codes.1.refs_0_ = s32[65,8,128]{2,1,0:T(8,128)} custom-call(s32[1,8]{1,0:T(1,128)} %valid_ref.1, s32[8]{0:T(128)} %rel_ref.1, s32[8,512]{1,0:T(8,128)} %bitcast.13, s32[8,16,1024]{2,1,0:T(8,128)} %bitcast.12), custom_call_target="tpu_custom_call" | custom-call | bytes 1048576 | tf_op jit(solution)/shard_map/edge_codes/pallas_call | solution.py:72
  3.5 4.0 %collective-permute-start.11 = (s32[65,8,128]{2,1,0:T(8,128)}, s32[65,8,128]{2,1,0:T(8,128)S(1)}, u32[]{:S(2)}, u32[]{:S(2)}) collective-permute-start(s32[65,8,128]{2,1,0:T(8,128)} %edge_codes.1.refs_0_), channel_id=1, source_target_pairs={{0,4},{1,5},{2,6},{3,7},{4,0},{5,1},{6,2},{7,3},{8,12},{9,13},{10,... | collective-permute-start | bytes 798728 | tf_op jit(solution)/shard_map/ppermute | solution.py:415
  7.4 1.0 %collective-permute-start.7 = (s32[65,8,128]{2,1,0:T(8,128)}, s32[65,8,128]{2,1,0:T(8,128)S(1)}, u32[]{:S(2)}, u32[]{:S(2)}) collective-permute-start(s32[65,8,128]{2,1,0:T(8,128)} %edge_codes.1.refs_0_), channel_id=1, source_target_pairs={{0,2},{1,3},{2,4},{3,5},{4,6},{5,7},{6,0},{7,1},{8,10},{9,11},{10,... | collective-permute-start | bytes 798728 | tf_op jit(solution)/shard_map/ppermute | solution.py:415
  8.5 2.2 %collective-permute-start.9 = (s32[65,8,128]{2,1,0:T(8,128)}, s32[65,8,128]{2,1,0:T(8,128)S(1)}, u32[]{:S(2)}, u32[]{:S(2)}) collective-permute-start(s32[65,8,128]{2,1,0:T(8,128)} %edge_codes.1.refs_0_), channel_id=1, source_target_pairs={{0,6},{1,7},{2,0},{3,1},{4,2},{5,3},{6,4},{7,5},{8,14},{9,15},{10,... | collective-permute-start | bytes 798728 | tf_op jit(solution)/shard_map/ppermute | solution.py:415
  10.7 0.1 pad_add_fusion.place_ref
  10.8 1.5 %collective-permute-start.1 = (bf16[64,1024]{1,0:T(8,128)(2,1)}, bf16[64,1024]{1,0:T(8,128)(2,1)S(1)}, u32[]{:S(2)}, u32[]{:S(2)}) collective-permute-start(bf16[64,1024]{1,0:T(8,128)(2,1)} %bitcast.8), channel_id=1, source_target_pairs={{0,4},{1,5},{2,6},{3,7},{4,0},{5,1},{6,2},{7,3},{8,12},{9,13},{10,... | collective-permute-start | bytes 393224 | tf_op jit(solution)/shard_map/ppermute | solution.py:415
  12.2 0.9 %copy-done.5 = s32[65,8,128]{2,1,0:T(8,128)S(1)} copy-done((s32[65,8,128]{2,1,0:T(8,128)S(1)}, s32[65,8,128]{2,1,0:T(8,128)}, u32[]{:S(2)}) %copy-start.5) | copy-done | bytes 266264
  13.2 3.3 %count_first.1.refs_3_ = s32[5,10,8,8,128]{4,3,2,1,0:T(8,128)S(1)} custom-call(s32[2]{0:T(128)S(1)} %pad_add_fusion.place_ref, s32[65,8,128]{2,1,0:T(8,128)S(1)} %copy-done.5, s32[65,8,128]{2,1,0:T(8,128)S(1)} %collective-permute-done.13.refs_1_), custom_call_target="tpu_custom_call" | custom-call | flops 2000000000 | bytes 1048576 | tf_op jit(solution)/shard_map/count_first/pallas_call | solution.py:213
  16.5 6.9 %collective-permute-done.refs_1_ = bf16[64,1024]{1,0:T(8,128)(2,1)S(1)} collective-permute-done((bf16[64,1024]{1,0:T(8,128)(2,1)}, bf16[64,1024]{1,0:T(8,128)(2,1)S(1)}, u32[]{:S(2)}, u32[]{:S(2)}) %collective-permute-start) | collective-permute-done | bytes 131104 | tf_op jit(solution)/shard_map/ppermute | solution.py:415
  23.4 0.7 collective-permute-start.2
  24.0 0.5 collective-permute-start.12
  24.6 0.1 collective-permute-start.8
  24.6 4.1 %count_edges.1.refs_3_ = s32[5,10,8,8,128]{4,3,2,1,0:T(8,128)S(1)} custom-call(s32[2]{0:T(128)S(1)} %pad_add_fusion.place_ref, s32[65,8,128]{2,1,0:T(8,128)S(1)} %collective-permute-done.7.refs_0_, s32[65,8,128]{2,1,0:T(8,128)S(1)} %collective-permute-done.9.refs_1_, s32[65,8,128]{2,1,0:T(8,128)S(1)} %collective-permute-done.11.refs_2_, ...), custom_call_target="tpu_custom_call" | custom-call | flops 4499999744 | bytes 1572864 | tf_op jit(solution)/shard_map/count_edges/pallas_call | solution.py:231
  28.7 0.6 collective-permute-start.3
  29.3 0.1 collective-permute-start.4
  29.4 0.4 collective-permute-start.5
  29.8 0.1 collective-permute-start.6
  29.9 5.7 %count_last.1.refs_8_ = bf16[1280,1024]{1,0:T(8,128)(2,1)S(1)} custom-call(s32[2]{0:T(128)S(1)} %pad_add_fusion.place_ref, s32[65,8,128]{2,1,0:T(8,128)S(1)} %collective-permute-done.8.refs_0_, s32[65,8,128]{2,1,0:T(8,128)S(1)} %collective-permute-done.10.refs_1_, s32[65,8,128]{2,1,0:T(8,128)S(1)} %collective-permute-done.12.refs_2_, ...), custom_call_target="tpu_custom_call" | custom-call | flops 6000000000 | bytes 4194304 | tf_op jit(solution)/shard_map/count_last/pallas_call | solution.py:263
  35.7 3.6 %hidden_rows.1.hidden_ref.h0_ref = bf16[256,2560]{1,0:T(8,128)(2,1)S(1)} custom-call(s32[2]{0:T(128)S(1)} %pad_add_fusion.place_ref, bf16[64,1024]{1,0:T(8,128)(2,1)S(1)} %bitcast.11, bf16[64,1024]{1,0:T(8,128)(2,1)S(1)} %collective-permute-done.refs_1_, bf16[64,1024]{1,0:T(8,128)(2,1)S(1)} %collective-permute-done.1.refs_2_, ...), custom_call_target="tpu_custom_call" | custom-call | flops 2000000000 | bytes 4194304 | tf_op jit(solution)/shard_map/hidden_rows/pallas_call | solution.py:307
  39.3 0.4 collective-permute-start.14
  39.7 0.4 convolution_convert_fusion
  40.1 0.3 collective-permute-start.15
  40.4 0.4 convolution_convert_fusion.1.f0_ref
  40.7 1.9 %collective-permute-done.15.f1_ref = bf16[384,256]{1,0:T(8,128)(2,1)S(1)} collective-permute-done((bf16[384,256]{1,0:T(8,128)(2,1)S(1)}, bf16[384,256]{1,0:T(8,128)(2,1)S(1)}, u32[]{:S(2)}, u32[]{:S(2)}) %collective-permute-start.15) | collective-permute-done | bytes 196640 | tf_op jit(solution)/shard_map/ppermute | solution.py:418
  42.7 1.4 %products.1 = bf16[64,120,128]{2,1,0:T(8,128)(2,1)S(1)} custom-call(bf16[256,2560]{1,0:T(8,128)(2,1)S(1)} %hidden_rows.1.hidden_ref.h0_ref, bf16[256,2560]{1,0:T(8,128)(2,1)S(1)} %collective-permute-done.14.h1_ref, bf16[384,256]{1,0:T(8,128)(2,1)S(1)} %convolution_convert_fusion.1.f0_ref, bf16[384,256]{1,0:T(8,128)(2,1)S(1)} %collective-permute-done.15.f1_ref), custom_call_target="tpu_custom_call" | custom-call | flops 1000000000 | bytes 5242880 | tf_op jit(solution)/shard_map/products/pallas_call | solution.py:369
  44.1 1.3 %copy-done.1 = bf16[64,120,128]{2,1,0:T(8,128)(2,1)} copy-done((bf16[64,120,128]{2,1,0:T(8,128)(2,1)}, bf16[64,120,128]{2,1,0:T(8,128)(2,1)S(1)}, u32[]{:S(2)}) %copy-start.1) | copy-done | bytes 1966104
  45.4 10.9 %all-to-all-start = ((bf16[64,120,128]{2,1,0:T(8,128)(2,1)}), bf16[64,120,128]{2,1,0:T(8,128)(2,1)S(1)}, u32[]{:S(2)}, u32[]{:S(2)}) async-start(bf16[64,120,128]{2,1,0:T(8,128)(2,1)} %copy-done.1), calls=%async_computation | async-start | bytes 3932160 | tf_op jit(solution)/shard_map/all_to_all | solution.py:449
  56.3 1.3 %copy-done.3 = bf16[256,2560]{1,0:T(8,128)(2,1)S(1)} copy-done((bf16[256,2560]{1,0:T(8,128)(2,1)S(1)}, bf16[256,2560]{1,0:T(8,128)(2,1)}, u32[]{:S(2)}) %copy-start.3) | copy-done | bytes 1310744
  57.6 2.1 %copy-done.4 = bf16[768,2560]{1,0:T(8,128)(2,1)S(1)} copy-done((bf16[768,2560]{1,0:T(8,128)(2,1)S(1)}, bf16[768,2560]{1,0:T(8,128)(2,1)}, u32[]{:S(2)}) %copy-start.4) | copy-done | bytes 3932184
  59.7 2.0 %source_rows.1 = bf16[256,768]{1,0:T(8,128)(2,1)} custom-call(bf16[256,2560]{1,0:T(8,128)(2,1)S(1)} %copy-done.3, bf16[768,2560]{1,0:T(8,128)(2,1)S(1)} %copy-done.4), custom_call_target="tpu_custom_call" | custom-call | flops 1000000000 | bytes 6291456 | tf_op jit(solution)/shard_map/source_rows/pallas_call | solution.py:331
  61.7 23.4 %all-to-all-done.got_ref = bf16[64,120,128]{2,1,0:T(8,128)(2,1)S(1)} async-done(((bf16[64,120,128]{2,1,0:T(8,128)(2,1)}), bf16[64,120,128]{2,1,0:T(8,128)(2,1)S(1)}, u32[]{:S(2)}, u32[]{:S(2)}) %all-to-all-start) | async-done | bytes 1966112 | tf_op jit(solution)/shard_map/all_to_all | solution.py:449
  85.1 0.9 %sum_chunks.1 = f32[6,2560]{1,0:T(8,128)} custom-call(bf16[64,120,128]{2,1,0:T(8,128)(2,1)S(1)} %all-to-all-done.got_ref), custom_call_target="tpu_custom_call" | custom-call | flops 1048576 | bytes 2097152 | tf_op jit(solution)/shard_map/sum_chunks/pallas_call | solution.py:397
  (29 shorter events, 0.1 us)
Async XLA Ops:
  0.6 39.1 %copy-start = (bf16[256,768]{1,0:T(8,128)(2,1)S(1)}, bf16[256,768]{1,0:T(8,128)(2,1)}, u32[]{:S(2)}) copy-start(bf16[256,768]{1,0:T(8,128)(2,1)} %param.8) | copy-start | bytes 1179652
  3.5 7.3 %collective-permute-start.13 = (s32[65,8,128]{2,1,0:T(8,128)}, s32[65,8,128]{2,1,0:T(8,128)S(1)}, u32[]{:S(2)}, u32[]{:S(2)}) collective-permute-start(s32[65,8,128]{2,1,0:T(8,128)} %edge_codes.1.refs_0_), channel_id=1, source_target_pairs={{0,1},{1,0},{2,3},{3,2},{4,5},{5,4},{6,7},{7,6},{8,9},{9,8},{10,11... | collective-permute-start | bytes 798728 | tf_op jit(solution)/shard_map/ppermute | solution.py:418
  3.5 20.5 %collective-permute-start.11 = (s32[65,8,128]{2,1,0:T(8,128)}, s32[65,8,128]{2,1,0:T(8,128)S(1)}, u32[]{:S(2)}, u32[]{:S(2)}) collective-permute-start(s32[65,8,128]{2,1,0:T(8,128)} %edge_codes.1.refs_0_), channel_id=1, source_target_pairs={{0,4},{1,5},{2,6},{3,7},{4,0},{5,1},{6,2},{7,3},{8,12},{9,13},{10,... | collective-permute-start | bytes 798728 | tf_op jit(solution)/shard_map/ppermute | solution.py:415
  7.4 17.1 %collective-permute-start.7 = (s32[65,8,128]{2,1,0:T(8,128)}, s32[65,8,128]{2,1,0:T(8,128)S(1)}, u32[]{:S(2)}, u32[]{:S(2)}) collective-permute-start(s32[65,8,128]{2,1,0:T(8,128)} %edge_codes.1.refs_0_), channel_id=1, source_target_pairs={{0,2},{1,3},{2,4},{3,5},{4,6},{5,7},{6,0},{7,1},{8,10},{9,11},{10,... | collective-permute-start | bytes 798728 | tf_op jit(solution)/shard_map/ppermute | solution.py:415
  8.5 15.6 %collective-permute-start.9 = (s32[65,8,128]{2,1,0:T(8,128)}, s32[65,8,128]{2,1,0:T(8,128)S(1)}, u32[]{:S(2)}, u32[]{:S(2)}) collective-permute-start(s32[65,8,128]{2,1,0:T(8,128)} %edge_codes.1.refs_0_), channel_id=1, source_target_pairs={{0,6},{1,7},{2,0},{3,1},{4,2},{5,3},{6,4},{7,5},{8,14},{9,15},{10,... | collective-permute-start | bytes 798728 | tf_op jit(solution)/shard_map/ppermute | solution.py:415
  10.7 12.7 %collective-permute-start = (bf16[64,1024]{1,0:T(8,128)(2,1)}, bf16[64,1024]{1,0:T(8,128)(2,1)S(1)}, u32[]{:S(2)}, u32[]{:S(2)}) collective-permute-start(bf16[64,1024]{1,0:T(8,128)(2,1)} %bitcast.7), channel_id=1, source_target_pairs={{0,2},{1,3},{2,4},{3,5},{4,6},{5,7},{6,0},{7,1},{8,10},{9,11},{10,... | collective-permute-start | bytes 393224 | tf_op jit(solution)/shard_map/ppermute | solution.py:415
  10.8 18.0 %collective-permute-start.1 = (bf16[64,1024]{1,0:T(8,128)(2,1)}, bf16[64,1024]{1,0:T(8,128)(2,1)S(1)}, u32[]{:S(2)}, u32[]{:S(2)}) collective-permute-start(bf16[64,1024]{1,0:T(8,128)(2,1)} %bitcast.8), channel_id=1, source_target_pairs={{0,4},{1,5},{2,6},{3,7},{4,0},{5,1},{6,2},{7,3},{8,12},{9,13},{10,... | collective-permute-start | bytes 393224 | tf_op jit(solution)/shard_map/ppermute | solution.py:415
  12.2 1.0 %copy-start.5 = (s32[65,8,128]{2,1,0:T(8,128)S(1)}, s32[65,8,128]{2,1,0:T(8,128)}, u32[]{:S(2)}) copy-start(s32[65,8,128]{2,1,0:T(8,128)} %edge_codes.1.refs_0_) | copy-start | bytes 798724
  13.2 10.2 %copy-start.6 = (bf16[1024,64]{0,1:T(8,128)(2,1)S(1)}, bf16[1024,64]{0,1:T(8,128)(2,1)}, u32[]{:S(2)}) copy-start(bf16[1024,64]{0,1:T(8,128)(2,1)} %param.7) | copy-start | bytes 393220
  23.4 5.9 %collective-permute-start.2 = (bf16[64,1024]{1,0:T(8,128)(2,1)S(1)}, bf16[64,1024]{1,0:T(8,128)(2,1)S(1)}, u32[]{:S(2)}, u32[]{:S(2)}) collective-permute-start(bf16[64,1024]{1,0:T(8,128)(2,1)S(1)} %bitcast.9), channel_id=1, source_target_pairs={{0,6},{1,7},{2,0},{3,1},{4,2},{5,3},{6,4},{7,5},{8,14},{9,15},{10,... | collective-permute-start | bytes 393224 | tf_op jit(solution)/shard_map/ppermute | solution.py:415
  24.0 5.4 %collective-permute-start.10 = (s32[65,8,128]{2,1,0:T(8,128)S(1)}, s32[65,8,128]{2,1,0:T(8,128)S(1)}, u32[]{:S(2)}, u32[]{:S(2)}) collective-permute-start(s32[65,8,128]{2,1,0:T(8,128)S(1)} %collective-permute-done.9.refs_1_), channel_id=1, source_target_pairs={{0,1},{1,0},{2,3},{3,2},{4,5},{5,4},{6,7},{7,6},{8,9},{9,8},{10,11... | collective-permute-start | bytes 798728 | tf_op jit(solution)/shard_map/ppermute | solution.py:418
  24.0 5.8 %collective-permute-start.12 = (s32[65,8,128]{2,1,0:T(8,128)S(1)}, s32[65,8,128]{2,1,0:T(8,128)S(1)}, u32[]{:S(2)}, u32[]{:S(2)}) collective-permute-start(s32[65,8,128]{2,1,0:T(8,128)S(1)} %collective-permute-done.11.refs_2_), channel_id=1, source_target_pairs={{0,1},{1,0},{2,3},{3,2},{4,5},{5,4},{6,7},{7,6},{8,9},{9,8},{10,11... | collective-permute-start | bytes 798728 | tf_op jit(solution)/shard_map/ppermute | solution.py:418
  24.6 5.4 %collective-permute-start.8 = (s32[65,8,128]{2,1,0:T(8,128)S(1)}, s32[65,8,128]{2,1,0:T(8,128)S(1)}, u32[]{:S(2)}, u32[]{:S(2)}) collective-permute-start(s32[65,8,128]{2,1,0:T(8,128)S(1)} %collective-permute-done.7.refs_0_), channel_id=1, source_target_pairs={{0,1},{1,0},{2,3},{3,2},{4,5},{5,4},{6,7},{7,6},{8,9},{9,8},{10,11... | collective-permute-start | bytes 798728 | tf_op jit(solution)/shard_map/ppermute | solution.py:418
  28.7 6.9 %collective-permute-start.3 = (bf16[64,1024]{1,0:T(8,128)(2,1)S(1)}, bf16[64,1024]{1,0:T(8,128)(2,1)S(1)}, u32[]{:S(2)}, u32[]{:S(2)}) collective-permute-start(bf16[64,1024]{1,0:T(8,128)(2,1)S(1)} %bitcast.10), channel_id=1, source_target_pairs={{0,1},{1,0},{2,3},{3,2},{4,5},{5,4},{6,7},{7,6},{8,9},{9,8},{10,11... | collective-permute-start | bytes 393224 | tf_op jit(solution)/shard_map/ppermute | solution.py:418
  29.3 6.3 %collective-permute-start.4 = (bf16[64,1024]{1,0:T(8,128)(2,1)S(1)}, bf16[64,1024]{1,0:T(8,128)(2,1)S(1)}, u32[]{:S(2)}, u32[]{:S(2)}) collective-permute-start(bf16[64,1024]{1,0:T(8,128)(2,1)S(1)} %collective-permute-done.refs_1_), channel_id=1, source_target_pairs={{0,1},{1,0},{2,3},{3,2},{4,5},{5,4},{6,7},{7,6},{8,9},{9,8},{10,11... | collective-permute-start | bytes 393224 | tf_op jit(solution)/shard_map/ppermute | solution.py:418
  29.4 6.2 %collective-permute-start.5 = (bf16[64,1024]{1,0:T(8,128)(2,1)S(1)}, bf16[64,1024]{1,0:T(8,128)(2,1)S(1)}, u32[]{:S(2)}, u32[]{:S(2)}) collective-permute-start(bf16[64,1024]{1,0:T(8,128)(2,1)S(1)} %collective-permute-done.1.refs_2_), channel_id=1, source_target_pairs={{0,1},{1,0},{2,3},{3,2},{4,5},{5,4},{6,7},{7,6},{8,9},{9,8},{10,11... | collective-permute-start | bytes 393224 | tf_op jit(solution)/shard_map/ppermute | solution.py:418
  29.8 5.8 %collective-permute-start.6 = (bf16[64,1024]{1,0:T(8,128)(2,1)S(1)}, bf16[64,1024]{1,0:T(8,128)(2,1)S(1)}, u32[]{:S(2)}, u32[]{:S(2)}) collective-permute-start(bf16[64,1024]{1,0:T(8,128)(2,1)S(1)} %collective-permute-done.2.refs_3_), channel_id=1, source_target_pairs={{0,1},{1,0},{2,3},{3,2},{4,5},{5,4},{6,7},{7,6},{8,9},{9,8},{10,11... | collective-permute-start | bytes 393224 | tf_op jit(solution)/shard_map/ppermute | solution.py:418
  39.3 4.8 %copy-start.2 = (bf16[256,2560]{1,0:T(8,128)(2,1)}, bf16[256,2560]{1,0:T(8,128)(2,1)S(1)}, u32[]{:S(2)}) copy-start(bf16[256,2560]{1,0:T(8,128)(2,1)S(1)} %hidden_rows.1.hidden_ref.h0_ref) | copy-start | bytes 3932164
  39.3 3.4 %collective-permute-start.14 = (bf16[256,2560]{1,0:T(8,128)(2,1)S(1)}, bf16[256,2560]{1,0:T(8,128)(2,1)S(1)}, u32[]{:S(2)}, u32[]{:S(2)}) collective-permute-start(bf16[256,2560]{1,0:T(8,128)(2,1)S(1)} %hidden_rows.1.hidden_ref.h0_ref), channel_id=1, source_target_pairs={{0,1},{1,0},{2,3},{3,2},{4,5},{5,4},{6,7},{7,6},{8,9},{9,8},{10,11... | collective-permute-start | bytes 3932168 | tf_op jit(solution)/shard_map/ppermute | solution.py:418
  40.1 2.6 %collective-permute-start.15 = (bf16[384,256]{1,0:T(8,128)(2,1)S(1)}, bf16[384,256]{1,0:T(8,128)(2,1)S(1)}, u32[]{:S(2)}, u32[]{:S(2)}) collective-permute-start(bf16[384,256]{1,0:T(8,128)(2,1)S(1)} %convolution_convert_fusion), channel_id=1, source_target_pairs={{0,1},{1,0},{2,3},{3,2},{4,5},{5,4},{6,7},{7,6},{8,9},{9,8},{10,11... | collective-permute-start | bytes 589832 | tf_op jit(solution)/shard_map/ppermute | solution.py:418
  44.1 1.3 %copy-start.1 = (bf16[64,120,128]{2,1,0:T(8,128)(2,1)}, bf16[64,120,128]{2,1,0:T(8,128)(2,1)S(1)}, u32[]{:S(2)}) copy-start(bf16[64,120,128]{2,1,0:T(8,128)(2,1)S(1)} %products.1) | copy-start | bytes 5898244
  45.4 39.7 %all-to-all-start = ((bf16[64,120,128]{2,1,0:T(8,128)(2,1)}), bf16[64,120,128]{2,1,0:T(8,128)(2,1)S(1)}, u32[]{:S(2)}, u32[]{:S(2)}) async-start(bf16[64,120,128]{2,1,0:T(8,128)(2,1)} %copy-done.1), calls=%async_computation | async-start | bytes 3932160 | tf_op jit(solution)/shard_map/all_to_all | solution.py:449
  56.3 1.3 %copy-start.3 = (bf16[256,2560]{1,0:T(8,128)(2,1)S(1)}, bf16[256,2560]{1,0:T(8,128)(2,1)}, u32[]{:S(2)}) copy-start(bf16[256,2560]{1,0:T(8,128)(2,1)} %copy-done.2) | copy-start | bytes 3932164
  57.6 2.1 %copy-start.4 = (bf16[768,2560]{1,0:T(8,128)(2,1)S(1)}, bf16[768,2560]{1,0:T(8,128)(2,1)}, u32[]{:S(2)}) copy-start(bf16[768,2560]{1,0:T(8,128)(2,1)} %weight_ref.1) | copy-start | bytes 11796484

commit v7 on v6

--- a/solution.py
+++ b/solution.py
@@ -244,54 +244,31 @@
     )(place, *edges, planes)
 
 
-def last_kernel(n, place_ref, *refs):
-    edges = refs[:n]
-    start_ref, adj_ref, words, keys, meta, word_sems, meta_sems, planes_ref = refs[n:]
+def hidden_kernel(n, place_ref, *refs):
+    edges, pieces = refs[:n], refs[n : n + 8]
+    start_ref, out_ref, words, keys, meta, word_sems, meta_sems = refs[n + 8 : n + 15]
+    planes_ref, adj, grads_vmem, sems = refs[n + 15 :]
     loads = start_loads(edges, words, meta, word_sems, meta_sems)
-    planes_ref[...] = start_ref[...]
-    count_all(place_ref[0], loads, words, meta, keys, planes_ref)
-    for r in range(RELS):
-        for t in range(TILES):
-            adj_ref[r * OWN : (r + 1) * OWN, t * LANES : (t + 1) * LANES] = counts(
-                [planes_ref[r, p, t] for p in range(PLANES)]
-            )
-
-
-def count_last(place, edges, planes):
-    n = len(edges)
-    vmem = pl.BlockSpec(memory_space=pltpu.VMEM)
-    return pl.pallas_call(
-        functools.partial(last_kernel, n),
-        out_shape=jax.ShapeDtypeStruct((RELS * OWN, TGT), BF16),
-        in_specs=[pl.BlockSpec(memory_space=pltpu.SMEM)]
-        + [pl.BlockSpec(memory_space=pl.ANY)] * n
-        + [vmem],
-        out_specs=vmem,
-        scratch_shapes=count_scratch(n) + [pltpu.VMEM(PLANE_SHAPE, I32)],
-        compiler_params=pltpu.CompilerParams(vmem_limit_bytes=14 << 20),
-        cost_estimate=pl.CostEstimate(
-            flops=6_000_000_000, bytes_accessed=4 << 20, transcendentals=0
-        ),
-        name="count_last",
-    )(place, *edges, planes)
-
-
-def hidden_kernel(place_ref, *refs):
-    grads = refs[:8]
-    adj_ref, out_ref, grads_vmem, sems = refs[8:]
     copies = []
     for i in range(8):
         z = (place_ref[0] // 2 - i % 4) & 3
         core = place_ref[1] if i < 4 else 1 - place_ref[1]
         rows = pl.ds(pl.multiple_of((z * 2 + core) * PIECE, PIECE), PIECE)
-        copies.append(pltpu.make_async_copy(grads[i], grads_vmem.at[rows], sems.at[i]))
+        copies.append(pltpu.make_async_copy(pieces[i], grads_vmem.at[rows], sems.at[i]))
         copies[i].start()
+    planes_ref[...] = start_ref[...]
+    count_all(place_ref[0], loads, words, meta, keys, planes_ref)
+    for r in range(RELS):
+        for t in range(TILES):
+            adj[r * OWN : (r + 1) * OWN, t * LANES : (t + 1) * LANES] = counts(
+                [planes_ref[r, p, t] for p in range(PLANES)]
+            )
     for copy in copies:
         copy.wait()
     wide = 2 * LANES
     for b in range(HID // wide):
         h = lax.dot_general(
-            adj_ref[...],
+            adj[...],
             grads_vmem[b * wide : (b + 1) * wide, :],
             (((1,), (1,)), ((), ())),
             preferred_element_type=F32,
@@ -302,22 +279,48 @@
             out_ref[:, to : to + wide] = h[r * OWN : (r + 1) * OWN, :]
 
 
-def hidden_rows(place, grads, adj):
+def hidden_rows(place, edges, pieces, planes):
+    n = len(edges)
     vmem = pl.BlockSpec(memory_space=pltpu.VMEM)
     return pl.pallas_call(
-        hidden_kernel,
+        functools.partial(hidden_kernel, n),
         out_shape=jax.ShapeDtypeStruct((OWN, COLS), BF16),
         in_specs=[pl.BlockSpec(memory_space=pltpu.SMEM)]
-        + [pl.BlockSpec(memory_space=pl.ANY)] * 8
+        + [pl.BlockSpec(memory_space=pl.ANY)] * (n + 8)
         + [vmem],
         out_specs=vmem,
-        scratch_shapes=[pltpu.VMEM((HID, TGT), BF16), pltpu.SemaphoreType.DMA((8,))],
-        compiler_params=pltpu.CompilerParams(vmem_limit_bytes=14 << 20),
+        scratch_shapes=count_scratch(n)
+        + [
+            pltpu.VMEM(PLANE_SHAPE, I32),
+            pltpu.VMEM((RELS * OWN, TGT), BF16),
+            pltpu.VMEM((HID, TGT), BF16),
+            pltpu.SemaphoreType.DMA((8,)),
+        ],
+        compiler_params=pltpu.CompilerParams(vmem_limit_bytes=20 << 20),
         cost_estimate=pl.CostEstimate(
-            flops=2_000_000_000, bytes_accessed=4 << 20, transcendentals=0
+            flops=6_000_000_000, bytes_accessed=4 << 20, transcendentals=0
         ),
         name="hidden_rows",
-    )(place, *grads, adj)
+    )(place, *edges, *pieces, planes)
+
+
+def after_kernel(*refs):
+    pass
+
+
+def after(values, earlier):
+    n = len(values)
+    anywhere = pl.BlockSpec(memory_space=pl.ANY)
+    return pl.pallas_call(
+        after_kernel,
+        out_shape=[jax.ShapeDtypeStruct(v.shape, v.dtype) for v in values],
+        in_specs=[anywhere] * (n + 1),
+        out_specs=[anywhere] * n,
+        input_output_aliases={i: i for i in range(n)},
+        compiler_params=pltpu.CompilerParams(vmem_limit_bytes=1 << 20),
+        cost_estimate=pl.CostEstimate(flops=1000, bytes_accessed=1 << 10, transcendentals=0),
+        name="after",
+    )(*values, earlier)
 
 
 def source_kernel(hidden_ref, weight_ref, out_ref):
@@ -418,15 +421,17 @@
         return lax.ppermute(v, "rel", [(i, i ^ 1) for i in range(8)])
 
     codes = edge_codes(valid_rows, block_rel, src_ids[0], nbr_slot.transpose(1, 2, 0))
-    far = {k: along_z(codes, k) for k in (1, 3, 2)}
-    grads = {0: grad_out.T}
-    for k in (1, 3, 2):
-        grads[k] = along_z(grads[0], k)
-    pieces = [grads[k] for k in range(4)]
+    far = {k: along_z(codes, k) for k in (1, 3)}
+    own_grads = grad_out.T
+    up, down = along_z(own_grads, 1), along_z(own_grads, 3)
+    planes = count_first(place, [codes, other_core(codes)])
+    far[1], down = after([far[1], down], planes)
+    far[2], twice_down = along_z(far[1], 1), along_z(down, 3)
+    planes = count_edges(place, [far[1], far[3]], planes)
+    planes = count_edges(place, [other_core(far[1]), other_core(far[3])], planes)
+    far[2], *pieces = after([far[2], up, twice_down, down], planes)
+    pieces = [own_grads] + pieces
     pieces += [other_core(v) for v in pieces]
-    planes = count_first(place, [codes, other_core(codes)])
-    planes = count_edges(place, [far[k] for k in (1, 3, 2)], planes)
-    adj = count_last(place, [other_core(far[k]) for k in (1, 3, 2)], planes)
 
     old = jnp.arange(D_IN, dtype=I32)[:, None]
     new = jnp.arange(D_IN // 2, dtype=I32)[None, :]
@@ -441,7 +446,7 @@
     feats = half_feats(core)
     feats_other = other_core(half_feats(1 - core))
 
-    hidden = hidden_rows(place, pieces, adj)
+    hidden = hidden_rows(place, [far[2], other_core(far[2])], pieces, planes)
     got = other_core(hidden)
     source_grad = source_rows(hidden, weight)
     chunks = products(hidden, got, feats, feats_other)

time: 86.6 us -> 83.4 us (0.963)
  waiting for transfers between devices: 32.3 us -> 30.4 us
  starting transfers between devices: 22.7 us -> 21.1 us
    ppermute x6, waiting for transfers between devices: 6.93 us -> 3.86 us  [along_z(): return lax.ppermute(v, 'rel', [(i, (i + 2 * k) % 8) for i in range(8)])]
    pallas_call x1 -> x2, Pallas kernels: 4.07 us -> 6.37 us  [count_edges(): pl.pallas_call(functools.partial(count_kernel, n), out_shape=jax.ShapeDty...]
    pallas_call x2 -> x3, Pallas kernels: 9.29 us -> 7.53 us  [the longest x1 7.53 us: hidden_rows(): pl.pallas_call(functools.partial(hidden_kernel, n), out_shape=jax.ShapeDt...]
    all_to_all x1, starting transfers between devices: 10.9 us -> 9.37 us  [on_device(): lax.all_to_all(chunks, ('dp', 'rel'), 0, 0, tiled=True, axis_index_groups...]
    ppermute x10, waiting for transfers between devices: 1.97 us -> 3.24 us  [other_core(): return lax.ppermute(v, 'rel', [(i, i ^ 1) for i in range(8)])]
  transfers between devices with their start and end apart: 17 -> 17, of which waited for: 3 -> 8; matrix products, arithmetic and copies ran while one was open for 1% -> 1% of each run, Pallas kernels for 17% -> 14%
where the time goes in v7:
time: 83.4 us; the launch traced here: 83.1 us
  waiting for transfers between devices  30.4 us (36%)
  Pallas kernels  24 us (29%)
  starting transfers between devices  21.1 us (25%)
  local copies, waits for them, and re-layouts  6.02 us (7%)
    all_to_all x1, waiting for transfers between devices, on_device(): lax.all_to_all(chunks, ('dp', 'rel'), 0, 0, tiled=True, axis_index_groups...  23.3 us
    ppermute x6, starting transfers between devices, along_z(): return lax.ppermute(v, 'rel', [(i, (i + 2 * k) % 8) for i in range(8)])  9.79 us
    all_to_all x1, starting transfers between devices, on_device(): lax.all_to_all(chunks, ('dp', 'rel'), 0, 0, tiled=True, axis_index_groups...  9.37 us
    pallas_call x1, Pallas kernels, hidden_rows(): pl.pallas_call(functools.partial(hidden_kernel, n), out_shape=jax.ShapeDt...  7.53 us
    pallas_call x2, Pallas kernels, count_edges(): pl.pallas_call(functools.partial(count_kernel, n), out_shape=jax.ShapeDty...  6.37 us
    unnamed x14, local copies, waits for them, and re-layouts  6.02 us
    ppermute x6, waiting for transfers between devices, along_z(): return lax.ppermute(v, 'rel', [(i, (i + 2 * k) % 8) for i in range(8)])  3.86 us
    ppermute x10, waiting for transfers between devices, other_core(): return lax.ppermute(v, 'rel', [(i, i ^ 1) for i in range(8)])  3.24 us
  transfers between devices with their start and end apart: 17, of which 8 were waited for; matrix products, arithmetic and copies ran while one was open for 1% of the time, Pallas kernels for 14%

profile of v7, /device:TPU:0, one launch (start us, length us, event | category | flops | bytes accessed | tf_op | source)
XLA Modules:
  0.0 83.1 jit_solution(8965660177120605786)
XLA Ops:
  0.6 2.8 %edge_codes.1.refs_0_ = s32[65,8,128]{2,1,0:T(8,128)} custom-call(s32[1,8]{1,0:T(1,128)} %valid_ref.1, s32[8]{0:T(128)} %rel_ref.1, s32[8,512]{1,0:T(8,128)} %bitcast.12, s32[8,16,1024]{2,1,0:T(8,128)} %bitcast.11), custom_call_target="tpu_custom_call" | custom-call | bytes 1048576 | tf_op jit(solution)/shard_map/edge_codes/pallas_call | solution.py:72
  3.5 2.0 %collective-permute-start = (s32[65,8,128]{2,1,0:T(8,128)}, s32[65,8,128]{2,1,0:T(8,128)S(1)}, u32[]{:S(2)}, u32[]{:S(2)}) collective-permute-start(s32[65,8,128]{2,1,0:T(8,128)} %edge_codes.1.refs_0_), channel_id=1, source_target_pairs={{0,2},{1,3},{2,4},{3,5},{4,6},{5,7},{6,0},{7,1},{8,10},{9,11},{10,... | collective-permute-start | bytes 798728 | tf_op jit(solution)/shard_map/ppermute | solution.py:418
  5.5 2.2 %collective-permute-start.7 = (s32[65,8,128]{2,1,0:T(8,128)}, s32[65,8,128]{2,1,0:T(8,128)S(1)}, u32[]{:S(2)}, u32[]{:S(2)}) collective-permute-start(s32[65,8,128]{2,1,0:T(8,128)} %edge_codes.1.refs_0_), channel_id=1, source_target_pairs={{0,6},{1,7},{2,0},{3,1},{4,2},{5,3},{6,4},{7,5},{8,14},{9,15},{10,... | collective-permute-start | bytes 798728 | tf_op jit(solution)/shard_map/ppermute | solution.py:418
  7.7 2.0 %collective-permute-start.1 = (bf16[64,1024]{1,0:T(8,128)(2,1)}, bf16[64,1024]{1,0:T(8,128)(2,1)S(1)}, u32[]{:S(2)}, u32[]{:S(2)}) collective-permute-start(bf16[64,1024]{1,0:T(8,128)(2,1)} %bitcast.7), channel_id=1, source_target_pairs={{0,6},{1,7},{2,0},{3,1},{4,2},{5,3},{6,4},{7,5},{8,14},{9,15},{10,... | collective-permute-start | bytes 393224 | tf_op jit(solution)/shard_map/ppermute | solution.py:418
  9.8 1.0 %copy-done.5 = s32[65,8,128]{2,1,0:T(8,128)S(1)} copy-done((s32[65,8,128]{2,1,0:T(8,128)S(1)}, s32[65,8,128]{2,1,0:T(8,128)}, u32[]{:S(2)}) %copy-start.5) | copy-done | bytes 266264
  10.7 3.0 %count_first.1.refs_2_ = s32[5,10,8,8,128]{4,3,2,1,0:T(8,128)S(1)} custom-call(s32[2]{0:T(128)S(1)} %pad_add_fusion.place_ref, s32[65,8,128]{2,1,0:T(8,128)S(1)} %copy-done.5, s32[65,8,128]{2,1,0:T(8,128)S(1)} %collective-permute-done.2.refs_1_), custom_call_target="tpu_custom_call" | custom-call | flops 2000000000 | bytes 1048576 | tf_op jit(solution)/shard_map/count_first/pallas_call | solution.py:213
  13.8 3.5 %collective-permute-done.1.refs_1_ = bf16[64,1024]{1,0:T(8,128)(2,1)S(1)} collective-permute-done((bf16[64,1024]{1,0:T(8,128)(2,1)}, bf16[64,1024]{1,0:T(8,128)(2,1)S(1)}, u32[]{:S(2)}, u32[]{:S(2)}) %collective-permute-start.1) | collective-permute-done | bytes 131104 | tf_op jit(solution)/shard_map/ppermute | solution.py:418
  17.3 1.8 %collective-permute-start.3 = (s32[65,8,128]{2,1,0:T(8,128)S(1)}, s32[65,8,128]{2,1,0:T(8,128)S(1)}, u32[]{:S(2)}, u32[]{:S(2)}) collective-permute-start(s32[65,8,128]{2,1,0:T(8,128)S(1)} %get-tuple-element.8.refs_0_), channel_id=1, source_target_pairs={{0,2},{1,3},{2,4},{3,5},{4,6},{5,7},{6,0},{7,1},{8,10},{9,11},{10,... | collective-permute-start | bytes 798728 | tf_op jit(solution)/shard_map/ppermute | solution.py:418
  19.0 1.8 %collective-permute-start.5 = (bf16[64,1024]{1,0:T(8,128)(2,1)S(1)}, bf16[64,1024]{1,0:T(8,128)(2,1)S(1)}, u32[]{:S(2)}, u32[]{:S(2)}) collective-permute-start(bf16[64,1024]{1,0:T(8,128)(2,1)S(1)} %get-tuple-element.9.refs_3_), channel_id=1, source_target_pairs={{0,6},{1,7},{2,0},{3,1},{4,2},{5,3},{6,4},{7,5},{8,14},{9,15},{10,... | collective-permute-start | bytes 393224 | tf_op jit(solution)/shard_map/ppermute | solution.py:418
  20.9 3.2 %count_edges.2.refs_2_ = s32[5,10,8,8,128]{4,3,2,1,0:T(8,128)S(1)} custom-call(s32[2]{0:T(128)S(1)} %pad_add_fusion.place_ref, s32[65,8,128]{2,1,0:T(8,128)S(1)} %get-tuple-element.8.refs_0_, s32[65,8,128]{2,1,0:T(8,128)S(1)} %collective-permute-done.7.refs_1_, s32[5,10,8,8,128]{4,3,2,1,0:T(8,128)S(1)} %count_first.1.refs_2_), custom_call_target="tpu_custom_call" | custom-call | flops 3000000000 | bytes 1048576 | tf_op jit(solution)/shard_map/count_edges/pallas_call | solution.py:231
  24.1 3.2 %count_edges.3.refs_4_.refs_10_ = s32[5,10,8,8,128]{4,3,2,1,0:T(8,128)S(1)} custom-call(s32[2]{0:T(128)S(1)} %pad_add_fusion.place_ref, s32[65,8,128]{2,1,0:T(8,128)S(1)} %collective-permute-done.6.refs_0_, s32[65,8,128]{2,1,0:T(8,128)S(1)} %collective-permute-done.8.refs_1_, s32[5,10,8,8,128]{4,3,2,1,0:T(8,128)S(1)} %count_edges.2.refs_2_), custom_call_target="tpu_custom_call" | custom-call | flops 3000000000 | bytes 1048576 | tf_op jit(solution)/shard_map/count_edges/pallas_call | solution.py:231
  27.3 0.4 collective-permute-done.3.refs_0_
  27.9 0.3 copy-done.6
  28.2 0.4 collective-permute-start.10
  28.7 0.4 collective-permute-start.12
  29.2 0.4 collective-permute-done.10.refs_6_
  29.6 0.4 collective-permute-done.11.refs_7_
  30.2 0.3 collective-permute-done.13.refs_9_
  30.5 7.5 %hidden_rows.1.hidden_ref.h0_ref = bf16[256,2560]{1,0:T(8,128)(2,1)S(1)} custom-call(s32[2]{0:T(128)S(1)} %pad_add_fusion.place_ref, s32[65,8,128]{2,1,0:T(8,128)S(1)} %get-tuple-element.10.refs_0_, s32[65,8,128]{2,1,0:T(8,128)S(1)} %collective-permute-done.9.refs_1_, bf16[64,1024]{1,0:T(8,128)(2,1)S(1)} %bitcast.10, ...), custom_call_target="tpu_custom_call" | custom-call | flops 6000000000 | bytes 4194304 | tf_op jit(solution)/shard_map/hidden_rows/pallas_call | solution.py:285
  38.1 0.3 collective-permute-start.14
  38.3 0.4 convolution_convert_fusion
  38.7 0.4 collective-permute-start.15
  39.1 0.4 convolution_convert_fusion.1.f0_ref
  39.5 2.0 %collective-permute-done.15.f1_ref = bf16[384,256]{1,0:T(8,128)(2,1)S(1)} collective-permute-done((bf16[384,256]{1,0:T(8,128)(2,1)S(1)}, bf16[384,256]{1,0:T(8,128)(2,1)S(1)}, u32[]{:S(2)}, u32[]{:S(2)}) %collective-permute-start.15) | collective-permute-done | bytes 196640 | tf_op jit(solution)/shard_map/ppermute | solution.py:421
  41.5 1.4 %products.1 = bf16[64,120,128]{2,1,0:T(8,128)(2,1)S(1)} custom-call(bf16[256,2560]{1,0:T(8,128)(2,1)S(1)} %hidden_rows.1.hidden_ref.h0_ref, bf16[256,2560]{1,0:T(8,128)(2,1)S(1)} %collective-permute-done.14.h1_ref, bf16[384,256]{1,0:T(8,128)(2,1)S(1)} %convolution_convert_fusion.1.f0_ref, bf16[384,256]{1,0:T(8,128)(2,1)S(1)} %collective-permute-done.15.f1_ref), custom_call_target="tpu_custom_call" | custom-call | flops 1000000000 | bytes 5242880 | tf_op jit(solution)/shard_map/products/pallas_call | solution.py:372
  42.8 1.3 %copy-done.1 = bf16[64,120,128]{2,1,0:T(8,128)(2,1)} copy-done((bf16[64,120,128]{2,1,0:T(8,128)(2,1)}, bf16[64,120,128]{2,1,0:T(8,128)(2,1)S(1)}, u32[]{:S(2)}) %copy-start.1) | copy-done | bytes 1966104
  44.1 9.4 %all-to-all-start = ((bf16[64,120,128]{2,1,0:T(8,128)(2,1)}), bf16[64,120,128]{2,1,0:T(8,128)(2,1)S(1)}, u32[]{:S(2)}, u32[]{:S(2)}) async-start(bf16[64,120,128]{2,1,0:T(8,128)(2,1)} %copy-done.1), calls=%async_computation | async-start | bytes 3932160 | tf_op jit(solution)/shard_map/all_to_all | solution.py:454
  53.5 1.3 %copy-done.3 = bf16[256,2560]{1,0:T(8,128)(2,1)S(1)} copy-done((bf16[256,2560]{1,0:T(8,128)(2,1)S(1)}, bf16[256,2560]{1,0:T(8,128)(2,1)}, u32[]{:S(2)}) %copy-start.3) | copy-done | bytes 1310744
  54.8 2.1 %copy-done.4 = bf16[768,2560]{1,0:T(8,128)(2,1)S(1)} copy-done((bf16[768,2560]{1,0:T(8,128)(2,1)S(1)}, bf16[768,2560]{1,0:T(8,128)(2,1)}, u32[]{:S(2)}) %copy-start.4) | copy-done | bytes 3932184
  56.9 2.0 %source_rows.1 = bf16[256,768]{1,0:T(8,128)(2,1)} custom-call(bf16[256,2560]{1,0:T(8,128)(2,1)S(1)} %copy-done.3, bf16[768,2560]{1,0:T(8,128)(2,1)S(1)} %copy-done.4), custom_call_target="tpu_custom_call" | custom-call | flops 1000000000 | bytes 6291456 | tf_op jit(solution)/shard_map/source_rows/pallas_call | solution.py:334
  58.9 23.3 %all-to-all-done.got_ref = bf16[64,120,128]{2,1,0:T(8,128)(2,1)S(1)} async-done(((bf16[64,120,128]{2,1,0:T(8,128)(2,1)}), bf16[64,120,128]{2,1,0:T(8,128)(2,1)S(1)}, u32[]{:S(2)}, u32[]{:S(2)}) %all-to-all-start) | async-done | bytes 1966112 | tf_op jit(solution)/shard_map/all_to_all | solution.py:454
  82.2 0.9 %sum_chunks.1 = f32[6,2560]{1,0:T(8,128)} custom-call(bf16[64,120,128]{2,1,0:T(8,128)(2,1)S(1)} %all-to-all-done.got_ref), custom_call_target="tpu_custom_call" | custom-call | flops 1048576 | bytes 2097152 | tf_op jit(solution)/shard_map/sum_chunks/pallas_call | solution.py:400
  (31 shorter events, 0.8 us)
Async XLA Ops:
  0.6 37.7 %copy-start = (bf16[256,768]{1,0:T(8,128)(2,1)S(1)}, bf16[256,768]{1,0:T(8,128)(2,1)}, u32[]{:S(2)}) copy-start(bf16[256,768]{1,0:T(8,128)(2,1)} %param.8) | copy-start | bytes 1179652
  3.5 6.3 %collective-permute-start.2 = (s32[65,8,128]{2,1,0:T(8,128)}, s32[65,8,128]{2,1,0:T(8,128)S(1)}, u32[]{:S(2)}, u32[]{:S(2)}) collective-permute-start(s32[65,8,128]{2,1,0:T(8,128)} %edge_codes.1.refs_0_), channel_id=1, source_target_pairs={{0,1},{1,0},{2,3},{3,2},{4,5},{5,4},{6,7},{7,6},{8,9},{9,8},{10,11... | collective-permute-start | bytes 798728 | tf_op jit(solution)/shard_map/ppermute | solution.py:421
  3.5 13.8 %collective-permute-start = (s32[65,8,128]{2,1,0:T(8,128)}, s32[65,8,128]{2,1,0:T(8,128)S(1)}, u32[]{:S(2)}, u32[]{:S(2)}) collective-permute-start(s32[65,8,128]{2,1,0:T(8,128)} %edge_codes.1.refs_0_), channel_id=1, source_target_pairs={{0,2},{1,3},{2,4},{3,5},{4,6},{5,7},{6,0},{7,1},{8,10},{9,11},{10,... | collective-permute-start | bytes 798728 | tf_op jit(solution)/shard_map/ppermute | solution.py:418
  5.5 15.3 %collective-permute-start.7 = (s32[65,8,128]{2,1,0:T(8,128)}, s32[65,8,128]{2,1,0:T(8,128)S(1)}, u32[]{:S(2)}, u32[]{:S(2)}) collective-permute-start(s32[65,8,128]{2,1,0:T(8,128)} %edge_codes.1.refs_0_), channel_id=1, source_target_pairs={{0,6},{1,7},{2,0},{3,1},{4,2},{5,3},{6,4},{7,5},{8,14},{9,15},{10,... | collective-permute-start | bytes 798728 | tf_op jit(solution)/shard_map/ppermute | solution.py:418
  7.7 9.6 %collective-permute-start.1 = (bf16[64,1024]{1,0:T(8,128)(2,1)}, bf16[64,1024]{1,0:T(8,128)(2,1)S(1)}, u32[]{:S(2)}, u32[]{:S(2)}) collective-permute-start(bf16[64,1024]{1,0:T(8,128)(2,1)} %bitcast.7), channel_id=1, source_target_pairs={{0,6},{1,7},{2,0},{3,1},{4,2},{5,3},{6,4},{7,5},{8,14},{9,15},{10,... | collective-permute-start | bytes 393224 | tf_op jit(solution)/shard_map/ppermute | solution.py:418
  9.6 17.7 %collective-permute-start.4 = (bf16[64,1024]{1,0:T(8,128)(2,1)}, bf16[64,1024]{1,0:T(8,128)(2,1)S(1)}, u32[]{:S(2)}, u32[]{:S(2)}) collective-permute-start(bf16[64,1024]{1,0:T(8,128)(2,1)} %bitcast.8), channel_id=1, source_target_pairs={{0,2},{1,3},{2,4},{3,5},{4,6},{5,7},{6,0},{7,1},{8,10},{9,11},{10,... | collective-permute-start | bytes 393224 | tf_op jit(solution)/shard_map/ppermute | solution.py:418
  9.8 1.0 %copy-start.5 = (s32[65,8,128]{2,1,0:T(8,128)S(1)}, s32[65,8,128]{2,1,0:T(8,128)}, u32[]{:S(2)}) copy-start(s32[65,8,128]{2,1,0:T(8,128)} %edge_codes.1.refs_0_) | copy-start | bytes 798724
  17.2 6.8 %collective-permute-start.6 = (s32[65,8,128]{2,1,0:T(8,128)S(1)}, s32[65,8,128]{2,1,0:T(8,128)S(1)}, u32[]{:S(2)}, u32[]{:S(2)}) collective-permute-start(s32[65,8,128]{2,1,0:T(8,128)S(1)} %get-tuple-element.8.refs_0_), channel_id=1, source_target_pairs={{0,1},{1,0},{2,3},{3,2},{4,5},{5,4},{6,7},{7,6},{8,9},{9,8},{10,11... | collective-permute-start | bytes 798728 | tf_op jit(solution)/shard_map/ppermute | solution.py:421
  17.3 10.5 %collective-permute-start.3 = (s32[65,8,128]{2,1,0:T(8,128)S(1)}, s32[65,8,128]{2,1,0:T(8,128)S(1)}, u32[]{:S(2)}, u32[]{:S(2)}) collective-permute-start(s32[65,8,128]{2,1,0:T(8,128)S(1)} %get-tuple-element.8.refs_0_), channel_id=1, source_target_pairs={{0,2},{1,3},{2,4},{3,5},{4,6},{5,7},{6,0},{7,1},{8,10},{9,11},{10,... | collective-permute-start | bytes 798728 | tf_op jit(solution)/shard_map/ppermute | solution.py:418
  19.0 8.3 %collective-permute-start.5 = (bf16[64,1024]{1,0:T(8,128)(2,1)S(1)}, bf16[64,1024]{1,0:T(8,128)(2,1)S(1)}, u32[]{:S(2)}, u32[]{:S(2)}) collective-permute-start(bf16[64,1024]{1,0:T(8,128)(2,1)S(1)} %get-tuple-element.9.refs_3_), channel_id=1, source_target_pairs={{0,6},{1,7},{2,0},{3,1},{4,2},{5,3},{6,4},{7,5},{8,14},{9,15},{10,... | collective-permute-start | bytes 393224 | tf_op jit(solution)/shard_map/ppermute | solution.py:418
  20.8 3.3 %collective-permute-start.8 = (s32[65,8,128]{2,1,0:T(8,128)S(1)}, s32[65,8,128]{2,1,0:T(8,128)S(1)}, u32[]{:S(2)}, u32[]{:S(2)}) collective-permute-start(s32[65,8,128]{2,1,0:T(8,128)S(1)} %collective-permute-done.7.refs_1_), channel_id=1, source_target_pairs={{0,1},{1,0},{2,3},{3,2},{4,5},{5,4},{6,7},{7,6},{8,9},{9,8},{10,11... | collective-permute-start | bytes 798728 | tf_op jit(solution)/shard_map/ppermute | solution.py:421
  27.3 0.9 %copy-start.6 = (bf16[1024,64]{0,1:T(8,128)(2,1)S(1)}, bf16[1024,64]{0,1:T(8,128)(2,1)}, u32[]{:S(2)}) copy-start(bf16[1024,64]{0,1:T(8,128)(2,1)} %param.7) | copy-start | bytes 393220
  27.7 2.8 %collective-permute-start.9 = (s32[65,8,128]{2,1,0:T(8,128)S(1)}, s32[65,8,128]{2,1,0:T(8,128)S(1)}, u32[]{:S(2)}, u32[]{:S(2)}) collective-permute-start(s32[65,8,128]{2,1,0:T(8,128)S(1)} %get-tuple-element.10.refs_0_), channel_id=1, source_target_pairs={{0,1},{1,0},{2,3},{3,2},{4,5},{5,4},{6,7},{7,6},{8,9},{9,8},{10,11... | collective-permute-start | bytes 798728 | tf_op jit(solution)/shard_map/ppermute | solution.py:421
  28.2 1.4 %collective-permute-start.10 = (bf16[64,1024]{1,0:T(8,128)(2,1)S(1)}, bf16[64,1024]{1,0:T(8,128)(2,1)S(1)}, u32[]{:S(2)}, u32[]{:S(2)}) collective-permute-start(bf16[64,1024]{1,0:T(8,128)(2,1)S(1)} %bitcast.9), channel_id=1, source_target_pairs={{0,1},{1,0},{2,3},{3,2},{4,5},{5,4},{6,7},{7,6},{8,9},{9,8},{10,11... | collective-permute-start | bytes 393224 | tf_op jit(solution)/shard_map/ppermute | solution.py:421
  28.6 1.3 %collective-permute-start.11 = (bf16[64,1024]{1,0:T(8,128)(2,1)S(1)}, bf16[64,1024]{1,0:T(8,128)(2,1)S(1)}, u32[]{:S(2)}, u32[]{:S(2)}) collective-permute-start(bf16[64,1024]{1,0:T(8,128)(2,1)S(1)} %get-tuple-element.11.refs_3_), channel_id=1, source_target_pairs={{0,1},{1,0},{2,3},{3,2},{4,5},{5,4},{6,7},{7,6},{8,9},{9,8},{10,11... | collective-permute-start | bytes 393224 | tf_op jit(solution)/shard_map/ppermute | solution.py:421
  28.7 1.5 %collective-permute-start.12 = (bf16[64,1024]{1,0:T(8,128)(2,1)S(1)}, bf16[64,1024]{1,0:T(8,128)(2,1)S(1)}, u32[]{:S(2)}, u32[]{:S(2)}) collective-permute-start(bf16[64,1024]{1,0:T(8,128)(2,1)S(1)} %get-tuple-element.12.refs_4_), channel_id=1, source_target_pairs={{0,1},{1,0},{2,3},{3,2},{4,5},{5,4},{6,7},{7,6},{8,9},{9,8},{10,11... | collective-permute-start | bytes 393224 | tf_op jit(solution)/shard_map/ppermute | solution.py:421
  29.2 1.3 %collective-permute-start.13 = (bf16[64,1024]{1,0:T(8,128)(2,1)S(1)}, bf16[64,1024]{1,0:T(8,128)(2,1)S(1)}, u32[]{:S(2)}, u32[]{:S(2)}) collective-permute-start(bf16[64,1024]{1,0:T(8,128)(2,1)S(1)} %get-tuple-element.13.refs_5_), channel_id=1, source_target_pairs={{0,1},{1,0},{2,3},{3,2},{4,5},{5,4},{6,7},{7,6},{8,9},{9,8},{10,11... | collective-permute-start | bytes 393224 | tf_op jit(solution)/shard_map/ppermute | solution.py:421
  38.0 4.8 %copy-start.2 = (bf16[256,2560]{1,0:T(8,128)(2,1)}, bf16[256,2560]{1,0:T(8,128)(2,1)S(1)}, u32[]{:S(2)}) copy-start(bf16[256,2560]{1,0:T(8,128)(2,1)S(1)} %hidden_rows.1.hidden_ref.h0_ref) | copy-start | bytes 3932164
  38.1 3.4 %collective-permute-start.14 = (bf16[256,2560]{1,0:T(8,128)(2,1)S(1)}, bf16[256,2560]{1,0:T(8,128)(2,1)S(1)}, u32[]{:S(2)}, u32[]{:S(2)}) collective-permute-start(bf16[256,2560]{1,0:T(8,128)(2,1)S(1)} %hidden_rows.1.hidden_ref.h0_ref), channel_id=1, source_target_pairs={{0,1},{1,0},{2,3},{3,2},{4,5},{5,4},{6,7},{7,6},{8,9},{9,8},{10,11... | collective-permute-start | bytes 3932168 | tf_op jit(solution)/shard_map/ppermute | solution.py:421
  38.7 2.7 %collective-permute-start.15 = (bf16[384,256]{1,0:T(8,128)(2,1)S(1)}, bf16[384,256]{1,0:T(8,128)(2,1)S(1)}, u32[]{:S(2)}, u32[]{:S(2)}) collective-permute-start(bf16[384,256]{1,0:T(8,128)(2,1)S(1)} %convolution_convert_fusion), channel_id=1, source_target_pairs={{0,1},{1,0},{2,3},{3,2},{4,5},{5,4},{6,7},{7,6},{8,9},{9,8},{10,11... | collective-permute-start | bytes 589832 | tf_op jit(solution)/shard_map/ppermute | solution.py:421
  42.8 1.3 %copy-start.1 = (bf16[64,120,128]{2,1,0:T(8,128)(2,1)}, bf16[64,120,128]{2,1,0:T(8,128)(2,1)S(1)}, u32[]{:S(2)}) copy-start(bf16[64,120,128]{2,1,0:T(8,128)(2,1)S(1)} %products.1) | copy-start | bytes 5898244
  44.1 38.0 %all-to-all-start = ((bf16[64,120,128]{2,1,0:T(8,128)(2,1)}), bf16[64,120,128]{2,1,0:T(8,128)(2,1)S(1)}, u32[]{:S(2)}, u32[]{:S(2)}) async-start(bf16[64,120,128]{2,1,0:T(8,128)(2,1)} %copy-done.1), calls=%async_computation | async-start | bytes 3932160 | tf_op jit(solution)/shard_map/all_to_all | solution.py:454
  53.5 1.3 %copy-start.3 = (bf16[256,2560]{1,0:T(8,128)(2,1)S(1)}, bf16[256,2560]{1,0:T(8,128)(2,1)}, u32[]{:S(2)}) copy-start(bf16[256,2560]{1,0:T(8,128)(2,1)} %copy-done.2) | copy-start | bytes 3932164
  54.8 2.1 %copy-start.4 = (bf16[768,2560]{1,0:T(8,128)(2,1)S(1)}, bf16[768,2560]{1,0:T(8,128)(2,1)}, u32[]{:S(2)}) copy-start(bf16[768,2560]{1,0:T(8,128)(2,1)} %weight_ref.1) | copy-start | bytes 11796484

commit v8 on v7

--- a/solution.py
+++ b/solution.py
@@ -323,22 +323,26 @@
     )(*values, earlier)
 
 
-def source_kernel(hidden_ref, weight_ref, out_ref):
+def source_kernel(hidden_ref, weight_ref, out_ref, done_ref):
     out_ref[...] = lax.dot_general(
         hidden_ref[...], weight_ref[...], (((1,), (1,)), ((), ())), preferred_element_type=F32
     ).astype(BF16)
+    done_ref[...] = jnp.zeros_like(done_ref)
 
 
 def source_rows(hidden, weight):
     vmem = pl.BlockSpec(memory_space=pltpu.VMEM)
     return pl.pallas_call(
         source_kernel,
-        out_shape=jax.ShapeDtypeStruct((OWN, D_IN), BF16),
+        out_shape=[
+            jax.ShapeDtypeStruct((OWN, D_IN), BF16),
+            jax.ShapeDtypeStruct((8, LANES), F32),
+        ],
         in_specs=[vmem] * 2,
-        out_specs=vmem,
+        out_specs=[vmem] * 2,
         compiler_params=pltpu.CompilerParams(vmem_limit_bytes=16 << 20),
         cost_estimate=pl.CostEstimate(
-            flops=1_000_000_000, bytes_accessed=6 << 20, transcendentals=0
+            flops=20_000_000_000, bytes_accessed=6 << 20, transcendentals=0
         ),
         name="source_rows",
     )(hidden, weight)
@@ -348,7 +352,7 @@
     return tile // 4 * 24 + tile // 2 % 2 * 12 + r * 2 + tile % 2
 
 
-def product_kernel(h0_ref, h1_ref, f0_ref, f1_ref, out_ref, chunks):
+def product_kernel(h0_ref, h1_ref, f0_ref, f1_ref, earlier_ref, out_ref, chunks):
     wide = 2 * LANES
     for pair in range(COLS // (2 * wide)):
         parts = []
@@ -367,12 +371,12 @@
     out_ref[...] = chunks[...].astype(BF16)
 
 
-def products(h0, h1, f0, f1):
+def products(h0, h1, f0, f1, earlier):
     vmem = pl.BlockSpec(memory_space=pltpu.VMEM)
     return pl.pallas_call(
         product_kernel,
         out_shape=jax.ShapeDtypeStruct((PEERS, CHUNK, LANES), BF16),
-        in_specs=[vmem] * 4,
+        in_specs=[vmem] * 4 + [pl.BlockSpec(memory_space=pl.ANY)],
         out_specs=vmem,
         scratch_shapes=[pltpu.VMEM((PEERS, CHUNK, LANES), F32)],
         compiler_params=pltpu.CompilerParams(vmem_limit_bytes=20 << 20),
@@ -380,7 +384,7 @@
             flops=1_000_000_000, bytes_accessed=5 << 20, transcendentals=0
         ),
         name="products",
-    )(h0, h1, f0, f1)
+    )(h0, h1, f0, f1, earlier)
 
 
 def sum_kernel(scale, got_ref, out_ref, sums):
@@ -448,8 +452,8 @@
 
     hidden = hidden_rows(place, [far[2], other_core(far[2])], pieces, planes)
     got = other_core(hidden)
-    source_grad = source_rows(hidden, weight)
-    chunks = products(hidden, got, feats, feats_other)
+    source_grad, done = source_rows(hidden, weight)
+    chunks = products(hidden, got, feats, feats_other, done)
     groups = [[2 * i + c for i in range(PEERS)] for c in range(2)]
     chunks = lax.all_to_all(
         chunks, ("dp", "rel"), 0, 0, tiled=True, axis_index_groups=groups

time: 83.4 us -> 82.8 us (level)
  blocking collectives: 0 us -> 39.2 us
  waiting for transfers between devices: 30.4 us -> 4.63 us
  starting transfers between devices: 21.1 us -> 12.3 us
  local copies, waits for them, and re-layouts: 6.02 us -> 0.97 us
    all_to_all x0 -> x1, blocking collectives: none -> 39.2 us  [on_device(): lax.all_to_all(chunks, ('dp', 'rel'), 0, 0, tiled=True, axis_index_groups...]
    all_to_all x1 -> x0, waiting for transfers between devices: 23.3 us -> none  [on_device(): lax.all_to_all(chunks, ('dp', 'rel'), 0, 0, tiled=True, axis_index_groups...]
    all_to_all x1 -> x0, starting transfers between devices: 9.37 us -> none  [on_device(): lax.all_to_all(chunks, ('dp', 'rel'), 0, 0, tiled=True, axis_index_groups...]
    unnamed x14 -> x8, local copies, waits for them, and re-layouts: 6.02 us -> 0.97 us
    ppermute x6, waiting for transfers between devices: 3.86 us -> 2.18 us  [along_z(): return lax.ppermute(v, 'rel', [(i, (i + 2 * k) % 8) for i in range(8)])]
  transfers between devices with their start and end apart: 17 -> 16, of which waited for: 8 -> 8; matrix products, arithmetic and copies ran while one was open for 1% -> 1% of each run, Pallas kernels for 14% -> 26%
where the time goes in v8:
time: 82.8 us; the launch traced here: 82.6 us
  blocking collectives  39.2 us (47%)
  Pallas kernels  23.9 us (29%)
  starting transfers between devices  12.3 us (15%)
  waiting for transfers between devices  4.63 us (6%)
  local copies, waits for them, and re-layouts  0.97 us (1%)
    all_to_all x1, blocking collectives, on_device(): lax.all_to_all(chunks, ('dp', 'rel'), 0, 0, tiled=True, axis_index_groups...  39.2 us
    ppermute x6, starting transfers between devices, along_z(): return lax.ppermute(v, 'rel', [(i, (i + 2 * k) % 8) for i in range(8)])  10.2 us
    pallas_call x1, Pallas kernels, hidden_rows(): pl.pallas_call(functools.partial(hidden_kernel, n), out_shape=jax.ShapeDt...  7.14 us
    pallas_call x2, Pallas kernels, count_edges(): pl.pallas_call(functools.partial(count_kernel, n), out_shape=jax.ShapeDty...  6.29 us
    pallas_call x1, Pallas kernels, count_first(): pl.pallas_call(functools.partial(first_kernel, n), out_shape=jax.ShapeDty...  3.38 us
    pallas_call x1, Pallas kernels, edge_codes(): pl.pallas_call(edge_kernel, out_shape=jax.ShapeDtypeStruct((BLKS * TILES...  2.79 us
    ppermute x10, waiting for transfers between devices, other_core(): return lax.ppermute(v, 'rel', [(i, i ^ 1) for i in range(8)])  2.45 us
    ppermute x6, waiting for transfers between devices, along_z(): return lax.ppermute(v, 'rel', [(i, (i + 2 * k) % 8) for i in range(8)])  2.18 us
  transfers between devices with their start and end apart: 16, of which 8 were waited for; matrix products, arithmetic and copies ran while one was open for 1% of the time, Pallas kernels for 26%

profile of v8, /device:TPU:0, one launch (start us, length us, event | category | flops | bytes accessed | tf_op | source)
XLA Modules:
  0.0 82.6 jit_solution(2880786800550103232)
XLA Ops:
  0.7 2.1 %collective-permute-start.4 = (bf16[64,1024]{1,0:T(8,128)(2,1)}, bf16[64,1024]{1,0:T(8,128)(2,1)S(1)}, u32[]{:S(2)}, u32[]{:S(2)}) collective-permute-start(bf16[64,1024]{1,0:T(8,128)(2,1)} %bitcast.8), channel_id=1, source_target_pairs={{0,2},{1,3},{2,4},{3,5},{4,6},{5,7},{6,0},{7,1},{8,10},{9,11},{10,... | collective-permute-start | bytes 393224 | tf_op jit(solution)/shard_map/ppermute | solution.py:422
  2.8 2.8 %edge_codes.1.refs_0_ = s32[65,8,128]{2,1,0:T(8,128)} custom-call(s32[1,8]{1,0:T(1,128)} %valid_ref.1, s32[8]{0:T(128)} %rel_ref.1, s32[8,512]{1,0:T(8,128)} %bitcast.12, s32[8,16,1024]{2,1,0:T(8,128)} %bitcast.11), custom_call_target="tpu_custom_call" | custom-call | bytes 1048576 | tf_op jit(solution)/shard_map/edge_codes/pallas_call | solution.py:72
  5.6 2.1 %collective-permute-start.7 = (s32[65,8,128]{2,1,0:T(8,128)}, s32[65,8,128]{2,1,0:T(8,128)S(1)}, u32[]{:S(2)}, u32[]{:S(2)}) collective-permute-start(s32[65,8,128]{2,1,0:T(8,128)} %edge_codes.1.refs_0_), channel_id=1, source_target_pairs={{0,6},{1,7},{2,0},{3,1},{4,2},{5,3},{6,4},{7,5},{8,14},{9,15},{10,... | collective-permute-start | bytes 798728 | tf_op jit(solution)/shard_map/ppermute | solution.py:422
  7.7 0.2 collective-permute-start.2
  7.9 0.4 convolution_convert_fusion.1.f0_ref
  8.4 1.1 %collective-permute-done.2.refs_1_ = s32[65,8,128]{2,1,0:T(8,128)S(1)} collective-permute-done((s32[65,8,128]{2,1,0:T(8,128)}, s32[65,8,128]{2,1,0:T(8,128)S(1)}, u32[]{:S(2)}, u32[]{:S(2)}) %collective-permute-start.2) | collective-permute-done | bytes 266272 | tf_op jit(solution)/shard_map/ppermute | solution.py:425
  9.5 2.1 %collective-permute-start.1 = (bf16[64,1024]{1,0:T(8,128)(2,1)S(1)}, bf16[64,1024]{1,0:T(8,128)(2,1)S(1)}, u32[]{:S(2)}, u32[]{:S(2)}) collective-permute-start(bf16[64,1024]{1,0:T(8,128)(2,1)S(1)} %bitcast.9), channel_id=1, source_target_pairs={{0,6},{1,7},{2,0},{3,1},{4,2},{5,3},{6,4},{7,5},{8,14},{9,15},{10,... | collective-permute-start | bytes 393224 | tf_op jit(solution)/shard_map/ppermute | solution.py:422
  11.6 0.9 %copy-done.1 = s32[65,8,128]{2,1,0:T(8,128)S(1)} copy-done((s32[65,8,128]{2,1,0:T(8,128)S(1)}, s32[65,8,128]{2,1,0:T(8,128)}, u32[]{:S(2)}) %copy-start.1) | copy-done | bytes 266264
  12.6 3.4 %count_first.1.refs_2_ = s32[5,10,8,8,128]{4,3,2,1,0:T(8,128)S(1)} custom-call(s32[2]{0:T(128)S(1)} %pad_add_fusion.place_ref, s32[65,8,128]{2,1,0:T(8,128)S(1)} %copy-done.1, s32[65,8,128]{2,1,0:T(8,128)S(1)} %collective-permute-done.2.refs_1_), custom_call_target="tpu_custom_call" | custom-call | flops 2000000000 | bytes 1048576 | tf_op jit(solution)/shard_map/count_first/pallas_call | solution.py:213
  16.0 1.3 %collective-permute-done.1.refs_1_ = bf16[64,1024]{1,0:T(8,128)(2,1)S(1)} collective-permute-done((bf16[64,1024]{1,0:T(8,128)(2,1)S(1)}, bf16[64,1024]{1,0:T(8,128)(2,1)S(1)}, u32[]{:S(2)}, u32[]{:S(2)}) %collective-permute-start.1) | collective-permute-done | bytes 131104 | tf_op jit(solution)/shard_map/ppermute | solution.py:422
  17.3 0.7 collective-permute-done.refs_0_
  18.0 1.1 %collective-permute-start.3 = (s32[65,8,128]{2,1,0:T(8,128)S(1)}, s32[65,8,128]{2,1,0:T(8,128)S(1)}, u32[]{:S(2)}, u32[]{:S(2)}) collective-permute-start(s32[65,8,128]{2,1,0:T(8,128)S(1)} %get-tuple-element.10.refs_0_), channel_id=1, source_target_pairs={{0,2},{1,3},{2,4},{3,5},{4,6},{5,7},{6,0},{7,1},{8,10},{9,11},{10,... | collective-permute-start | bytes 798728 | tf_op jit(solution)/shard_map/ppermute | solution.py:422
  19.1 0.2 collective-permute-start.8
  19.2 2.8 %count_edges.2.refs_2_ = s32[5,10,8,8,128]{4,3,2,1,0:T(8,128)S(1)} custom-call(s32[2]{0:T(128)S(1)} %pad_add_fusion.place_ref, s32[65,8,128]{2,1,0:T(8,128)S(1)} %get-tuple-element.10.refs_0_, s32[65,8,128]{2,1,0:T(8,128)S(1)} %collective-permute-done.7.refs_1_, s32[5,10,8,8,128]{4,3,2,1,0:T(8,128)S(1)} %count_first.1.refs_2_), custom_call_target="tpu_custom_call" | custom-call | flops 3000000000 | bytes 1048576 | tf_op jit(solution)/shard_map/count_edges/pallas_call | solution.py:231
  22.1 2.7 %collective-permute-start.5 = (bf16[64,1024]{1,0:T(8,128)(2,1)S(1)}, bf16[64,1024]{1,0:T(8,128)(2,1)S(1)}, u32[]{:S(2)}, u32[]{:S(2)}) collective-permute-start(bf16[64,1024]{1,0:T(8,128)(2,1)S(1)} %get-tuple-element.11.refs_3_), channel_id=1, source_target_pairs={{0,6},{1,7},{2,0},{3,1},{4,2},{5,3},{6,4},{7,5},{8,14},{9,15},{10,... | collective-permute-start | bytes 393224 | tf_op jit(solution)/shard_map/ppermute | solution.py:422
  24.8 3.5 %count_edges.3.refs_4_.refs_10_ = s32[5,10,8,8,128]{4,3,2,1,0:T(8,128)S(1)} custom-call(s32[2]{0:T(128)S(1)} %pad_add_fusion.place_ref, s32[65,8,128]{2,1,0:T(8,128)S(1)} %collective-permute-done.6.refs_0_, s32[65,8,128]{2,1,0:T(8,128)S(1)} %collective-permute-done.8.refs_1_, s32[5,10,8,8,128]{4,3,2,1,0:T(8,128)S(1)} %count_edges.2.refs_2_), custom_call_target="tpu_custom_call" | custom-call | flops 3000000000 | bytes 1048576 | tf_op jit(solution)/shard_map/count_edges/pallas_call | solution.py:231
  28.3 0.2 collective-permute-done.5.refs_2_
  28.5 0.5 collective-permute-start.11
  29.0 0.1 collective-permute-start.12
  29.1 0.4 collective-permute-start.13
  29.5 0.4 convolution_convert_fusion
  29.9 0.2 collective-permute-start.15
  30.1 0.1 collective-permute-done.11.refs_7_
  30.2 0.2 collective-permute-done.12.refs_8_
  30.4 0.2 collective-permute-done.13.refs_9_
  30.6 7.1 %hidden_rows.1.hidden_ref.h0_ref = bf16[256,2560]{1,0:T(8,128)(2,1)S(1)} custom-call(s32[2]{0:T(128)S(1)} %pad_add_fusion.place_ref, s32[65,8,128]{2,1,0:T(8,128)S(1)} %get-tuple-element.12.refs_0_, s32[65,8,128]{2,1,0:T(8,128)S(1)} %collective-permute-done.9.refs_1_, bf16[64,1024]{1,0:T(8,128)(2,1)S(1)} %bitcast.10, ...), custom_call_target="tpu_custom_call" | custom-call | flops 6000000000 | bytes 4194304 | tf_op jit(solution)/shard_map/hidden_rows/pallas_call | solution.py:285
  37.8 0.5 collective-permute-start.14
  38.3 2.0 %source_rows.1 = (bf16[256,768]{1,0:T(8,128)(2,1)}, f32[8,128]{1,0:T(8,128)S(1)}) custom-call(bf16[256,2560]{1,0:T(8,128)(2,1)S(1)} %hidden_rows.1.hidden_ref.h0_ref, bf16[768,2560]{1,0:T(8,128)(2,1)S(1)} %copy-done.2), custom_call_target="tpu_custom_call" | custom-call | flops 20000000000 | bytes 6291456 | tf_op jit(solution)/shard_map/source_rows/pallas_call | solution.py:335
  40.3 0.8 collective-permute-done.14.h1_ref
  41.1 1.4 %products.1 = bf16[64,120,128]{2,1,0:T(8,128)(2,1)S(1)} custom-call(bf16[256,2560]{1,0:T(8,128)(2,1)S(1)} %hidden_rows.1.hidden_ref.h0_ref, bf16[256,2560]{1,0:T(8,128)(2,1)S(1)} %collective-permute-done.14.h1_ref, bf16[384,256]{1,0:T(8,128)(2,1)S(1)} %convolution_convert_fusion.1.f0_ref, bf16[384,256]{1,0:T(8,128)(2,1)S(1)} %collective-permute-done.15.f1_ref, ...), custom_call_target="tpu_custom_call" | custom-call | flops 1000000000 | bytes 5242880 | tf_op jit(solution)/shard_map/products/pallas_call | solution.py:376
  42.5 39.2 %all_to_all.5.got_ref = bf16[64,120,128]{2,1,0:T(8,128)(2,1)S(1)} all-to-all(bf16[64,120,128]{2,1,0:T(8,128)(2,1)S(1)} %products.1), channel_id=1, replica_groups={{0,2,4,6,8,10,12,14,16,18,20,22,24,26,28,30,32,34,36,38,40,42,44,46,48,..., dimensions={0} | all-to-all | bytes 3932160 | tf_op jit(solution)/shard_map/all_to_all | solution.py:458
  81.6 0.9 %sum_chunks.1 = f32[6,2560]{1,0:T(8,128)} custom-call(bf16[64,120,128]{2,1,0:T(8,128)(2,1)S(1)} %all_to_all.5.got_ref), custom_call_target="tpu_custom_call" | custom-call | flops 1048576 | bytes 2097152 | tf_op jit(solution)/shard_map/sum_chunks/pallas_call | solution.py:404
  (24 shorter events, 0.2 us)
Async XLA Ops:
  0.6 7.3 %copy-start = (bf16[256,768]{1,0:T(8,128)(2,1)S(1)}, bf16[256,768]{1,0:T(8,128)(2,1)}, u32[]{:S(2)}) copy-start(bf16[256,768]{1,0:T(8,128)(2,1)} %param.8) | copy-start | bytes 1179652
  0.6 8.9 %copy-start.3 = (bf16[1024,64]{0,1:T(8,128)(2,1)S(1)}, bf16[1024,64]{0,1:T(8,128)(2,1)}, u32[]{:S(2)}) copy-start(bf16[1024,64]{0,1:T(8,128)(2,1)} %param.7) | copy-start | bytes 393220
  0.7 29.3 %collective-permute-start.10 = (bf16[64,1024]{1,0:T(8,128)(2,1)}, bf16[64,1024]{1,0:T(8,128)(2,1)S(1)}, u32[]{:S(2)}, u32[]{:S(2)}) collective-permute-start(bf16[64,1024]{1,0:T(8,128)(2,1)} %bitcast.7), channel_id=1, source_target_pairs={{0,1},{1,0},{2,3},{3,2},{4,5},{5,4},{6,7},{7,6},{8,9},{9,8},{10,11... | collective-permute-start | bytes 393224 | tf_op jit(solution)/shard_map/ppermute | solution.py:425
  0.7 27.6 %collective-permute-start.4 = (bf16[64,1024]{1,0:T(8,128)(2,1)}, bf16[64,1024]{1,0:T(8,128)(2,1)S(1)}, u32[]{:S(2)}, u32[]{:S(2)}) collective-permute-start(bf16[64,1024]{1,0:T(8,128)(2,1)} %bitcast.8), channel_id=1, source_target_pairs={{0,2},{1,3},{2,4},{3,5},{4,6},{5,7},{6,0},{7,1},{8,10},{9,11},{10,... | collective-permute-start | bytes 393224 | tf_op jit(solution)/shard_map/ppermute | solution.py:422
  5.6 13.5 %collective-permute-start.7 = (s32[65,8,128]{2,1,0:T(8,128)}, s32[65,8,128]{2,1,0:T(8,128)S(1)}, u32[]{:S(2)}, u32[]{:S(2)}) collective-permute-start(s32[65,8,128]{2,1,0:T(8,128)} %edge_codes.1.refs_0_), channel_id=1, source_target_pairs={{0,6},{1,7},{2,0},{3,1},{4,2},{5,3},{6,4},{7,5},{8,14},{9,15},{10,... | collective-permute-start | bytes 798728 | tf_op jit(solution)/shard_map/ppermute | solution.py:422
  7.7 1.8 %collective-permute-start.2 = (s32[65,8,128]{2,1,0:T(8,128)}, s32[65,8,128]{2,1,0:T(8,128)S(1)}, u32[]{:S(2)}, u32[]{:S(2)}) collective-permute-start(s32[65,8,128]{2,1,0:T(8,128)} %edge_codes.1.refs_0_), channel_id=1, source_target_pairs={{0,1},{1,0},{2,3},{3,2},{4,5},{5,4},{6,7},{7,6},{8,9},{9,8},{10,11... | collective-permute-start | bytes 798728 | tf_op jit(solution)/shard_map/ppermute | solution.py:425
  7.9 10.1 %collective-permute-start = (s32[65,8,128]{2,1,0:T(8,128)}, s32[65,8,128]{2,1,0:T(8,128)S(1)}, u32[]{:S(2)}, u32[]{:S(2)}) collective-permute-start(s32[65,8,128]{2,1,0:T(8,128)} %edge_codes.1.refs_0_), channel_id=1, source_target_pairs={{0,2},{1,3},{2,4},{3,5},{4,6},{5,7},{6,0},{7,1},{8,10},{9,11},{10,... | collective-permute-start | bytes 798728 | tf_op jit(solution)/shard_map/ppermute | solution.py:422
  9.5 7.8 %collective-permute-start.1 = (bf16[64,1024]{1,0:T(8,128)(2,1)S(1)}, bf16[64,1024]{1,0:T(8,128)(2,1)S(1)}, u32[]{:S(2)}, u32[]{:S(2)}) collective-permute-start(bf16[64,1024]{1,0:T(8,128)(2,1)S(1)} %bitcast.9), channel_id=1, source_target_pairs={{0,6},{1,7},{2,0},{3,1},{4,2},{5,3},{6,4},{7,5},{8,14},{9,15},{10,... | collective-permute-start | bytes 393224 | tf_op jit(solution)/shard_map/ppermute | solution.py:422
  11.6 1.0 %copy-start.1 = (s32[65,8,128]{2,1,0:T(8,128)S(1)}, s32[65,8,128]{2,1,0:T(8,128)}, u32[]{:S(2)}) copy-start(s32[65,8,128]{2,1,0:T(8,128)} %edge_codes.1.refs_0_) | copy-start | bytes 798724
  18.0 6.9 %collective-permute-start.6 = (s32[65,8,128]{2,1,0:T(8,128)S(1)}, s32[65,8,128]{2,1,0:T(8,128)S(1)}, u32[]{:S(2)}, u32[]{:S(2)}) collective-permute-start(s32[65,8,128]{2,1,0:T(8,128)S(1)} %get-tuple-element.10.refs_0_), channel_id=1, source_target_pairs={{0,1},{1,0},{2,3},{3,2},{4,5},{5,4},{6,7},{7,6},{8,9},{9,8},{10,11... | collective-permute-start | bytes 798728 | tf_op jit(solution)/shard_map/ppermute | solution.py:425
  18.0 10.5 %collective-permute-start.3 = (s32[65,8,128]{2,1,0:T(8,128)S(1)}, s32[65,8,128]{2,1,0:T(8,128)S(1)}, u32[]{:S(2)}, u32[]{:S(2)}) collective-permute-start(s32[65,8,128]{2,1,0:T(8,128)S(1)} %get-tuple-element.10.refs_0_), channel_id=1, source_target_pairs={{0,2},{1,3},{2,4},{3,5},{4,6},{5,7},{6,0},{7,1},{8,10},{9,11},{10,... | collective-permute-start | bytes 798728 | tf_op jit(solution)/shard_map/ppermute | solution.py:422
  19.1 3.0 %collective-permute-start.8 = (s32[65,8,128]{2,1,0:T(8,128)S(1)}, s32[65,8,128]{2,1,0:T(8,128)S(1)}, u32[]{:S(2)}, u32[]{:S(2)}) collective-permute-start(s32[65,8,128]{2,1,0:T(8,128)S(1)} %collective-permute-done.7.refs_1_), channel_id=1, source_target_pairs={{0,1},{1,0},{2,3},{3,2},{4,5},{5,4},{6,7},{7,6},{8,9},{9,8},{10,11... | collective-permute-start | bytes 798728 | tf_op jit(solution)/shard_map/ppermute | solution.py:425
  22.1 6.4 %collective-permute-start.5 = (bf16[64,1024]{1,0:T(8,128)(2,1)S(1)}, bf16[64,1024]{1,0:T(8,128)(2,1)S(1)}, u32[]{:S(2)}, u32[]{:S(2)}) collective-permute-start(bf16[64,1024]{1,0:T(8,128)(2,1)S(1)} %get-tuple-element.11.refs_3_), channel_id=1, source_target_pairs={{0,6},{1,7},{2,0},{3,1},{4,2},{5,3},{6,4},{7,5},{8,14},{9,15},{10,... | collective-permute-start | bytes 393224 | tf_op jit(solution)/shard_map/ppermute | solution.py:422
  28.5 2.1 %collective-permute-start.9 = (s32[65,8,128]{2,1,0:T(8,128)S(1)}, s32[65,8,128]{2,1,0:T(8,128)S(1)}, u32[]{:S(2)}, u32[]{:S(2)}) collective-permute-start(s32[65,8,128]{2,1,0:T(8,128)S(1)} %get-tuple-element.12.refs_0_), channel_id=1, source_target_pairs={{0,1},{1,0},{2,3},{3,2},{4,5},{5,4},{6,7},{7,6},{8,9},{9,8},{10,11... | collective-permute-start | bytes 798728 | tf_op jit(solution)/shard_map/ppermute | solution.py:425
  28.5 1.7 %collective-permute-start.11 = (bf16[64,1024]{1,0:T(8,128)(2,1)S(1)}, bf16[64,1024]{1,0:T(8,128)(2,1)S(1)}, u32[]{:S(2)}, u32[]{:S(2)}) collective-permute-start(bf16[64,1024]{1,0:T(8,128)(2,1)S(1)} %get-tuple-element.13.refs_3_), channel_id=1, source_target_pairs={{0,1},{1,0},{2,3},{3,2},{4,5},{5,4},{6,7},{7,6},{8,9},{9,8},{10,11... | collective-permute-start | bytes 393224 | tf_op jit(solution)/shard_map/ppermute | solution.py:425
  29.0 1.4 %collective-permute-start.12 = (bf16[64,1024]{1,0:T(8,128)(2,1)S(1)}, bf16[64,1024]{1,0:T(8,128)(2,1)S(1)}, u32[]{:S(2)}, u32[]{:S(2)}) collective-permute-start(bf16[64,1024]{1,0:T(8,128)(2,1)S(1)} %get-tuple-element.14.refs_4_), channel_id=1, source_target_pairs={{0,1},{1,0},{2,3},{3,2},{4,5},{5,4},{6,7},{7,6},{8,9},{9,8},{10,11... | collective-permute-start | bytes 393224 | tf_op jit(solution)/shard_map/ppermute | solution.py:425
  29.1 1.5 %collective-permute-start.13 = (bf16[64,1024]{1,0:T(8,128)(2,1)S(1)}, bf16[64,1024]{1,0:T(8,128)(2,1)S(1)}, u32[]{:S(2)}, u32[]{:S(2)}) collective-permute-start(bf16[64,1024]{1,0:T(8,128)(2,1)S(1)} %get-tuple-element.15.refs_5_), channel_id=1, source_target_pairs={{0,1},{1,0},{2,3},{3,2},{4,5},{5,4},{6,7},{7,6},{8,9},{9,8},{10,11... | collective-permute-start | bytes 393224 | tf_op jit(solution)/shard_map/ppermute | solution.py:425
  29.9 8.4 %copy-start.2 = (bf16[768,2560]{1,0:T(8,128)(2,1)S(1)}, bf16[768,2560]{1,0:T(8,128)(2,1)}, u32[]{:S(2)}) copy-start(bf16[768,2560]{1,0:T(8,128)(2,1)} %weight_ref.1) | copy-start | bytes 11796484
  29.9 10.3 %collective-permute-start.15 = (bf16[384,256]{1,0:T(8,128)(2,1)S(1)}, bf16[384,256]{1,0:T(8,128)(2,1)S(1)}, u32[]{:S(2)}, u32[]{:S(2)}) collective-permute-start(bf16[384,256]{1,0:T(8,128)(2,1)S(1)} %convolution_convert_fusion), channel_id=1, source_target_pairs={{0,1},{1,0},{2,3},{3,2},{4,5},{5,4},{6,7},{7,6},{8,9},{9,8},{10,11... | collective-permute-start | bytes 589832 | tf_op jit(solution)/shard_map/ppermute | solution.py:425
  37.8 3.3 %collective-permute-start.14 = (bf16[256,2560]{1,0:T(8,128)(2,1)S(1)}, bf16[256,2560]{1,0:T(8,128)(2,1)S(1)}, u32[]{:S(2)}, u32[]{:S(2)}) collective-permute-start(bf16[256,2560]{1,0:T(8,128)(2,1)S(1)} %hidden_rows.1.hidden_ref.h0_ref), channel_id=1, source_target_pairs={{0,1},{1,0},{2,3},{3,2},{4,5},{5,4},{6,7},{7,6},{8,9},{9,8},{10,11... | collective-permute-start | bytes 3932168 | tf_op jit(solution)/shard_map/ppermute | solution.py:425
